TPU v7x, 512 devices: a whole 4x8x8 slice. The times are simulated.
512 devices in a mesh: row: 32 (over y_hi, z), col: 16 (over y_lo, x, core).
Axes of the slice: x: 4, y: 8 (y_hi: 4, y_lo: 2; y = y_hi * 2 + y_lo), z: 8, core: 2. Of those that a mesh axis runs over, the one named last changes fastest.
Arguments:
- tiles: bfloat16 [32, 16, 96, 128, 128], P('row', 'col'), may hold values from -0.0546875 to 0.0546875
- tile_row: int32 [32, 16, 96], P('row', 'col'), may hold values from 0 to 31, as said below
- tile_col: int32 [32, 16, 96], P('row', 'col'), may hold values from 0 to 63
- tile_counts: int32 [32, 16], P('row', 'col'), may hold values from 12 to 96, as said below
- start: float32 [16, 131072], P(None, 'row'), may hold values from -16 to 16
- rotation: float32 [3, 3, 16, 16], replicated, may hold values from -3 to 3
Outputs:
- eigen_block: float32 [16, 131072], P(None, 'row')
- ritz: float32 [16, 16], replicated
Inputs may be any that keep to these rules, and one draw needn't show every extreme that they name: Within a block the pairs (tile_row, tile_col) of all 96 slots are distinct. `tile_counts`: some block is full.
All inputs are finite; a program needn't handle non-finite values.
Results may differ from a plain program's by a relative error of at most 0.0003.
Values sent between devices are 32-bit elements; how exact they have to be, the bound alone decides.
No kernel may reach another device: no remote copies, remote signals or barrier semaphores. Data moves between devices by JAX's collectives and lax.ppermute only.
A program may use at most 64 MiB of HBM per device.

v0:
```python
import jax
import jax.numpy as jnp
from jax import lax
from jax.sharding import PartitionSpec as P

ITERS = 3


def broadcast(shard, axis, root):
    mine = lax.axis_index(axis) == root
    return lax.psum(jnp.where(mine, shard, jnp.zeros_like(shard)), axis)


def rotate(coeffs, vectors):
    return jnp.einsum("uv,un->vn", coeffs, vectors, precision=lax.Precision.HIGHEST)


def body(tiles, tile_row, tile_col, tile_counts, start, rotation):
    hi = lax.Precision.HIGHEST
    tile_vals = tiles.reshape(tiles.shape[2:]).astype(jnp.float32)
    rows_here = tile_row.reshape(-1)
    cols_here = tile_col.reshape(-1)
    slot_limit = tile_counts.reshape(())
    vec_count, seg_rows = start.shape
    row_count = lax.axis_size("row")
    col_count = lax.axis_size("col")
    per_column = row_count // col_count
    block_rows = seg_rows * per_column
    all_rows = seg_rows * row_count
    here_row = lax.axis_index("row")
    here_col = lax.axis_index("col")
    owner_col = here_row // per_column
    part_index = here_row % per_column
    slot_count = rows_here.shape[0]
    live_slots = (jnp.arange(slot_count, dtype=jnp.int32) < slot_limit).astype(jnp.float32)
    hot_rows = (rows_here[:, None] == jnp.arange(seg_rows // 128, dtype=jnp.int32)[None, :]).astype(
        jnp.float32
    ) * live_slots[:, None]
    hot_cols = (
        cols_here[:, None] == jnp.arange(block_rows // 128, dtype=jnp.int32)[None, :]
    ).astype(jnp.float32) * live_slots[:, None]

    def apply_op(vectors):
        segments_in = [
            broadcast(vectors, "row", here_col * per_column + member)
            for member in range(per_column)
        ]
        block = jnp.concatenate(segments_in, axis=1)
        picked = block.reshape(vec_count, block_rows // 128, 128)[:, cols_here, :]
        products = jnp.einsum("kab,vkb->vka", tile_vals, picked, precision=hi)
        direct = jnp.einsum("vka,kt->vta", products, hot_rows, precision=hi).reshape(
            vec_count, seg_rows
        )
        taken = vectors.reshape(vec_count, seg_rows // 128, 128)[:, rows_here, :]
        mirrored = jnp.einsum("kab,vka->vkb", tile_vals, taken, precision=hi)
        spread_out = jnp.einsum("vkb,kt->vtb", mirrored, hot_cols, precision=hi).reshape(
            vec_count, block_rows
        )
        mirror_total = lax.psum(spread_out, "row")
        own_piece = lax.dynamic_slice_in_dim(mirror_total, part_index * seg_rows, seg_rows, 1)
        return lax.psum(direct, "col") + broadcast(own_piece, "col", owner_col)

    current = start
    image = apply_op(current)
    search = jnp.zeros_like(start)
    search_image = jnp.zeros_like(start)
    theta = jnp.zeros((vec_count, vec_count), jnp.float32)
    for iteration in range(ITERS):
        gram_local = jnp.einsum("un,vn->uv", current, image, precision=hi)
        theta = lax.psum(gram_local, "row") / all_rows
        residual = image - rotate(theta, current)
        spread = lax.psum(jnp.sum(residual * residual, axis=1), "row") / all_rows
        residual = residual / jnp.sqrt(spread + 1e-06)[:, None]
        residual_image = apply_op(residual)
        coeffs = rotation[iteration]
        new_search = rotate(coeffs[1], residual) + rotate(coeffs[2], search)
        new_search_image = rotate(coeffs[1], residual_image) + rotate(coeffs[2], search_image)
        current = rotate(coeffs[0], current) + new_search
        image = rotate(coeffs[0], image) + new_search_image
        search, search_image = (new_search, new_search_image)
    return (current, theta)


def solution(mesh):
    return jax.shard_map(
        body,
        mesh=mesh,
        in_specs=(
            P("row", "col", None, None, None),
            P("row", "col", None),
            P("row", "col", None),
            P("row", "col"),
            P(None, "row"),
            P(),
        ),
        out_specs=(P(None, "row"), P()),
        check_vma=False,
    )
```

profile of v0, /device:TPU:1, one launch (start us, length us, event | category | flops | bytes accessed | tf_op | source)
XLA Modules:
  0.0 1875.9 jit_solution(4076663815108613244)
XLA Ops:
  8.0 0.7 fusion.119
  8.8 1.0 copy_bitcast_fusion.8
  9.8 1.6 gather_fusion.1
  11.4 3.7 fusion.18
  15.1 0.8 fusion.47
  15.9 1.1 copy.68
  17.0 0.8 broadcast_select_fusion.5
  18.0 303.6 %all-reduce.20.cloned.1.call-done = (f32[16,4096]{1,0:T(8,128)}, f32[16,4096]{1,0:T(8,128)}, f32[16,8192]{1,0:T(8,128)}) async-done(((f32[16,4096]{1,0:T(8,128)}, f32[16,4096]{1,0:T(8,128)}, f32[16,8192]{1,0:T(8,128)}), (f32[16,4096]{1,0:T(8,128)}, f32[16,4096]{1,0:T(8,128)}, f32[16,8192]{1,0:T(8,128)})) %all-reduce.20.cloned.1.call-update) | async-done | bytes 1048592 | tf_op jit(solution)/shard_map/psum | solution.py:11
  321.6 1.9 copy_bitcast_fusion.5
  323.5 2.5 gather_fusion
  326.1 6.1 fusion.15
  332.2 0.7 fusion.49
  333.0 0.9 bitcast_add_fusion.2
  333.9 143.9 %all-reduce.10.cloned.1.call-done = f32[16,4096]{1,0:T(8,128)} async-done(((f32[16,4096]{1,0:T(8,128)}), f32[16,4096]{1,0:T(8,128)}) %all-reduce.10.cloned.1.call-update) | async-done | bytes 262160 | tf_op jit(solution)/shard_map/psum | solution.py:61
  477.8 1.4 convolution_bitcast_fusion
  479.2 70.2 %psum.152 = f32[16,16]{0,1:T(8,128)S(1)} all-reduce(f32[16,16]{0,1:T(8,128)S(1)} %convolution_bitcast_fusion), channel_id=1, replica_groups=mesh['row'=32,'col'=16] {'row'}, use_global_device_ids=true, to_apply=%region_5.6 | all-reduce | flops 256 | bytes 2048 | tf_op jit(solution)/shard_map/psum | solution.py:70
  549.4 2.1 multiply_reduce_fusion.2
  551.6 63.1 %psum.153 = f32[16]{0:T(128)S(1)} all-reduce(f32[16]{0:T(128)S(1)} %get-tuple-element.21), channel_id=1, replica_groups=mesh['row'=32,'col'=16] {'row'}, use_global_device_ids=true, to_apply=%region_7.8 | all-reduce | flops 16 | bytes 128 | tf_op jit(solution)/shard_map/psum | solution.py:72
  614.7 1.9 fusion.128
  616.6 0.7 copy.70
  617.3 2.4 gather_fusion.3
  619.7 3.7 fusion.24
  623.5 0.8 fusion.43
  624.3 1.1 copy.67
  625.5 318.4 %all-reduce.18.cloned.1.call-done = (f32[16,4096]{1,0:T(8,128)}, f32[16,4096]{1,0:T(8,128)}, f32[16,8192]{1,0:T(8,128)}) async-done(((f32[16,4096]{1,0:T(8,128)}, f32[16,4096]{1,0:T(8,128)}, f32[16,8192]{1,0:T(8,128)}), (f32[16,4096]{1,0:T(8,128)}, f32[16,4096]{1,0:T(8,128)}, f32[16,8192]{1,0:T(8,128)})) %all-reduce.18.cloned.1.call-update) | async-done | bytes 1048592 | tf_op jit(solution)/shard_map/psum | solution.py:11
  943.9 1.9 copy_bitcast_fusion.4
  945.8 2.5 gather_fusion.2
  948.3 6.1 fusion.21
  954.5 0.7 fusion.45
  955.2 0.9 bitcast_add_fusion.1
  956.2 1.4 convolution_add_fusion.6
  958.3 1.1 convolution_add_fusion.7
  959.4 140.7 %all-reduce.12.cloned.1.call-done = f32[16,4096]{1,0:T(8,128)} async-done(((f32[16,4096]{1,0:T(8,128)}), f32[16,4096]{1,0:T(8,128)}) %all-reduce.12.cloned.1.call-update) | async-done | bytes 262160 | tf_op jit(solution)/shard_map/psum | solution.py:61
  1100.1 1.4 convolution_add_fusion.3
  1102.2 1.4 convolution_add_fusion.4
  1103.6 1.5 fusion.130
  1105.1 70.2 %psum.159 = f32[16,16]{0,1:T(8,128)S(1)} all-reduce(f32[16,16]{0,1:T(8,128)S(1)} %fusion.130), channel_id=1, replica_groups=mesh['row'=32,'col'=16] {'row'}, use_global_device_ids=true, to_apply=%region_14.15 | all-reduce | flops 256 | bytes 2048 | tf_op jit(solution)/shard_map/psum | solution.py:70
  1175.3 2.1 multiply_reduce_fusion.1
  1177.4 63.1 %psum.160 = f32[16]{0:T(128)S(1)} all-reduce(f32[16]{0:T(128)S(1)} %get-tuple-element.23), channel_id=1, replica_groups=mesh['row'=32,'col'=16] {'row'}, use_global_device_ids=true, to_apply=%region_16.17 | all-reduce | flops 16 | bytes 128 | tf_op jit(solution)/shard_map/psum | solution.py:72
  1240.5 1.9 fusion.129
  1242.5 1.6 gather_fusion.5
  1244.0 3.7 fusion.30
  1247.7 0.8 fusion.39
  1248.6 1.1 copy.66
  1249.7 1.4 fusion.83
  1251.1 1.4 convolution_add_fusion.2
  1253.2 1.1 convolution_add_fusion.5
  1254.3 313.7 %all-reduce.16.cloned.1.call-done = (f32[16,4096]{1,0:T(8,128)}, f32[16,4096]{1,0:T(8,128)}, f32[16,8192]{1,0:T(8,128)}) async-done(((f32[16,4096]{1,0:T(8,128)}, f32[16,4096]{1,0:T(8,128)}, f32[16,8192]{1,0:T(8,128)}), (f32[16,4096]{1,0:T(8,128)}, f32[16,4096]{1,0:T(8,128)}, f32[16,8192]{1,0:T(8,128)})) %all-reduce.16.cloned.1.call-update) | async-done | bytes 1048592 | tf_op jit(solution)/shard_map/psum | solution.py:11
  1568.0 1.9 copy_bitcast_fusion.3
  1569.9 2.5 gather_fusion.4
  1572.4 6.2 fusion.27
  1578.6 0.7 fusion.41
  1579.3 0.9 bitcast_add_fusion
  1580.2 1.1 fusion.85
  1581.4 2.1 fusion.77
  1583.5 140.7 %all-reduce.14.cloned.1.call-done = f32[16,4096]{1,0:T(8,128)} async-done(((f32[16,4096]{1,0:T(8,128)}), f32[16,4096]{1,0:T(8,128)}) %all-reduce.14.cloned.1.call-update) | async-done | bytes 262160 | tf_op jit(solution)/shard_map/psum | solution.py:61
  1724.2 1.4 fusion.81
  1725.5 1.4 fusion.2
  1727.7 1.4 fusion.131
  1729.1 70.3 %psum.166 = f32[16,16]{0,1:T(8,128)S(1)} all-reduce(f32[16,16]{0,1:T(8,128)S(1)} %fusion.131), channel_id=1, replica_groups=mesh['row'=32,'col'=16] {'row'}, use_global_device_ids=true, to_apply=%region_22.23 | all-reduce | flops 256 | bytes 2048 | tf_op jit(solution)/shard_map/psum | solution.py:70
  1799.4 2.2 multiply_reduce_fusion
  1802.3 63.3 %psum.167 = f32[16]{0:T(128)S(1)} all-reduce(f32[16]{0:T(128)S(1)} %get-tuple-element.25), channel_id=1, replica_groups=mesh['row'=32,'col'=16] {'row'}, use_global_device_ids=true, to_apply=%region_24.25 | all-reduce | flops 16 | bytes 128 | tf_op jit(solution)/shard_map/psum | solution.py:72
  1865.6 1.4 fusion.51
  1867.0 2.1 fusion.1
  (55 shorter events, 4.0 us)
Async XLA Ops:
  7.2 4.2 copy-start
  7.2 314.4 %all-reduce.20.cloned.1.call-start = ((), (), s32[]{:S(2)}) async-start(), calls=%async_computation.5 | async-start | bytes 2097152 | tf_op jit(solution)/shard_map/psum | solution.py:11
  9.8 5.3 copy-start.15
  11.4 5.7 copy-start.1
  17.9 459.9 %all-reduce.10.cloned.1.call-start = ((), (), s32[]{:S(2)}) async-start(), calls=%async_computation | async-start | bytes 524288 | tf_op jit(solution)/shard_map/psum | solution.py:61
  323.5 8.7 copy-start.14
  326.1 6.9 copy-start.10
  333.9 610.0 %all-reduce.18.cloned.1.call-start = ((), (), s32[]{:S(2)}) async-start(), calls=%async_computation.4 | async-start | bytes 2097152 | tf_op jit(solution)/shard_map/psum | solution.py:11
  619.7 5.7 copy-start.13
  625.4 474.7 %all-reduce.12.cloned.1.call-start = ((), (), s32[]{:S(2)}) async-start(), calls=%async_computation.1 | async-start | bytes 524288 | tf_op jit(solution)/shard_map/psum | solution.py:61
  948.3 6.9 copy-start.12
  956.2 611.8 %all-reduce.16.cloned.1.call-start = ((), (), s32[]{:S(2)}) async-start(), calls=%async_computation.3 | async-start | bytes 2097152 | tf_op jit(solution)/shard_map/psum | solution.py:11
  957.6 0.7 copy-start.9
  1101.5 0.7 copy-start.5
  1103.6 138.9 %copy-start.3 = (f32[4096,16]{0,1:T(8,128)}, f32[4096,16]{0,1:T(8,128)S(1)}, u32[]{:S(2)}) copy-start(f32[4096,16]{0,1:T(8,128)S(1)} %convolution_add_fusion.4) | copy-start | bytes 786436
  1247.7 5.5 copy-start.2
  1249.7 474.5 %all-reduce.14.cloned.1.call-start = ((), (), s32[]{:S(2)}) async-start(), calls=%async_computation.2 | async-start | bytes 524288 | tf_op jit(solution)/shard_map/psum | solution.py:61
  1252.5 0.7 copy-start.6
  1572.4 6.9 copy-start.11
  1572.4 7.8 copy-start.4
  1581.4 285.6 %copy-start.7 = (f32[4096,16]{0,1:T(8,128)S(1)}, f32[4096,16]{0,1:T(8,128)}, u32[]{:S(2)}) copy-start(f32[4096,16]{0,1:T(8,128)} %copy-done.6) | copy-start | bytes 786436
  1727.0 0.7 copy-start.8
Sparse Core Ops, SparseCore 0:
  18.0 303.5 all-reduce.19
  334.0 143.7 all-reduce.9
  625.5 318.3 all-reduce.17
  956.3 143.7 all-reduce.11
  1249.8 318.1 all-reduce.15
  1580.4 143.7 all-reduce.13
where the time goes:
time: 1900 us; the launch traced here: 1880 us
  waiting for transfers between devices  1360 us (72%)
  blocking collectives  400 us (21%)
  matrix products  63.6 us (3%)
  local copies, waits for them, and re-layouts  21.7 us (1%)
    psum x3, waiting for transfers between devices, broadcast(): return lax.psum(jnp.where(mine, shard, jnp.zeros_like(shard)), axis)  936 us
    psum x3, waiting for transfers between devices, apply_op(): return lax.psum(direct, 'col') + broadcast(own_piece, 'col', owner_col)  425 us
    psum x3, blocking collectives, body(): theta = lax.psum(gram_local, 'row') / all_rows  211 us
    psum x3, blocking collectives, body(): spread = lax.psum(jnp.sum(residual * residual, axis=1), 'row') / all_rows  190 us
  transfers between devices with their start and end apart: 6, of which 6 were waited for; matrix products, arithmetic and copies ran while one was open for 1% of the time, Pallas kernels for 0%

commit v1 on v0

v1 whole, which is shorter than its diff:
```python
import functools

import jax
import jax.numpy as jnp
from jax import lax
from jax.experimental import pallas as pl
from jax.experimental.pallas import tpu as pltpu
from jax.sharding import PartitionSpec as P

ITERS = 3
LANE = 128
GROUP = 8
BOTH = ("row", "col")
HIGH = lax.Precision.HIGHEST
NT = (((1,), (1,)), ((), ()))
NN = (((1,), (0,)), ((), ()))
SMEM = pl.BlockSpec(memory_space=pltpu.SMEM)
VMEM = pl.BlockSpec(memory_space=pltpu.VMEM)


def kernel_call(kernel, name, out, ins, scratch=()):
    return pl.pallas_call(
        kernel,
        name=name,
        out_shape=out,
        in_specs=ins,
        out_specs=jax.tree.map(lambda _: VMEM, out),
        scratch_shapes=scratch,
        compiler_params=pltpu.CompilerParams(vmem_limit_bytes=48 << 20),
    )


def f32(*shape):
    return jax.ShapeDtypeStruct(shape, jnp.float32)


def multiply(get_seg, get_block, count_ref, row_ref, col_ref, tiles_ref, refs, out_ref, split, total):
    seg_tiles = out_ref.shape[0]
    vecs = out_ref.shape[1]

    def keep(slot, values):
        high = values.astype(jnp.bfloat16)
        split[slot, 0:vecs, :] = high
        split[slot, vecs : 2 * vecs, :] = (values - high.astype(jnp.float32)).astype(jnp.bfloat16)

    for t in range(seg_tiles):
        keep(t, get_seg(refs, t))
        for half in range(2):
            keep(seg_tiles * (1 + half) + t, get_block(refs, t, half))
    total[...] = jnp.zeros_like(total)
    count = count_ref[0]

    def group(g, carry):
        parts = []
        for j in range(GROUP):
            slot = g * GROUP + j
            row = row_ref[slot]
            col = col_ref[slot] + seg_tiles
            tile = tiles_ref[slot]
            direct = lax.dot_general(split[col], tile, NT, preferred_element_type=jnp.float32)
            mirror = lax.dot_general(split[row], tile, NN, preferred_element_type=jnp.float32)
            live = slot < count
            parts.append((row, jnp.where(live, direct[:vecs] + direct[vecs:], 0.0)))
            parts.append((col, jnp.where(live, mirror[:vecs] + mirror[vecs:], 0.0)))
        for place, part in parts:
            total[place] += part
        return carry

    lax.fori_loop(0, (count + (GROUP - 1)) // GROUP, group, 0)
    for t in range(seg_tiles):
        out_ref[t, :, 0:LANE] = total[t]
        out_ref[t, :, LANE : 2 * LANE] = total[seg_tiles + t]
        out_ref[t, :, 2 * LANE : 3 * LANE] = total[2 * seg_tiles + t]


def multiply_first(count_ref, row_ref, col_ref, tiles_ref, seg_ref, block_ref, out_ref, split, total):
    multiply(
        lambda refs, t: refs[0][t],
        lambda refs, t, half: refs[1][t, half],
        count_ref, row_ref, col_ref, tiles_ref, (seg_ref, block_ref), out_ref, split, total,
    )


def multiply_next(count_ref, row_ref, col_ref, tiles_ref, all_ref, out_ref, split, total):
    multiply(
        lambda refs, t: refs[0][t, :, 0:LANE],
        lambda refs, t, half: refs[0][t, :, (1 + half) * LANE : (2 + half) * LANE],
        count_ref, row_ref, col_ref, tiles_ref, (all_ref,), out_ref, split, total,
    )


def add_up(got_ref, sums):
    rows, cols = got_ref.shape[0], got_ref.shape[1]
    for r in range(rows):
        half = r % 2
        sums[r // 2 : r // 2 + 1, half * LANE : (half + 1) * LANE] = jnp.sum(
            got_ref[r, :, 0:LANE], axis=0, keepdims=True
        )
    mirror = got_ref[0, :, LANE : 3 * LANE]
    for r in range(1, rows):
        mirror = mirror + got_ref[r, :, LANE : 3 * LANE]
    sums[...] = sums[...] + mirror


def sum_and_deal(got_ref, out_ref, sums):
    rows, cols = got_ref.shape[0], got_ref.shape[1]
    add_up(got_ref, sums)
    block = sums[...]
    for r in range(rows):
        half = r % 2
        out_ref[r, :, 0:LANE] = jnp.broadcast_to(
            sums[r // 2 : r // 2 + 1, half * LANE : (half + 1) * LANE], (cols, LANE)
        )
        out_ref[r, :, LANE : 3 * LANE] = block


def sum_and_deal_rows(got_ref, out_ref, sums):
    rows, cols = got_ref.shape[0], got_ref.shape[1]
    add_up(got_ref, sums)
    for r in range(rows):
        half = r % 2
        out_ref[r] = jnp.broadcast_to(
            sums[r // 2 : r // 2 + 1, half * LANE : (half + 1) * LANE], (cols, LANE)
        )


def gram(start_ref, one_ref, two_ref, three_ref, basis_ref, gram_ref):
    tiles, vecs = three_ref.shape[0], three_ref.shape[1]
    basis_ref[0:vecs, :] = start_ref[...]
    for t in range(tiles):
        lanes = slice(t * LANE, (t + 1) * LANE)
        basis_ref[vecs : 2 * vecs, lanes] = one_ref[t, :, 0:LANE]
        basis_ref[2 * vecs : 3 * vecs, lanes] = two_ref[t, :, 0:LANE]
        basis_ref[3 * vecs : 4 * vecs, lanes] = three_ref[t]
    parts = []
    for j in range(ITERS + 1):
        top = min(j + 2, ITERS + 1)
        parts.append(
            lax.dot_general(
                basis_ref[j * vecs : (j + 1) * vecs, :],
                basis_ref[j * vecs : top * vecs, :],
                NT, precision=HIGH, preferred_element_type=jnp.float32,
            )
        )
    parts.append(jnp.zeros((vecs, LANE - (2 * ITERS + 1) * vecs), jnp.float32))
    gram_ref[...] = jnp.concatenate(parts, axis=1)


def finish(states, grams_ref, turn_ref, basis_ref, eigen_ref, ritz_ref):
    vecs = eigen_ref.shape[0]

    def mul(a, b, dims=NN):
        full = jnp.concatenate([b, jnp.zeros((LANE - b.shape[0], b.shape[1]), jnp.float32)], axis=0)
        return lax.dot_general(a, full, dims, precision=HIGH, preferred_element_type=jnp.float32)

    moments = grams_ref[0]
    for r in range(1, grams_ref.shape[0]):
        moments = moments + grams_ref[r]
    moments = moments * (1.0 / states)
    hankel = jnp.concatenate(
        [moments] + [pltpu.roll(moments, LANE - j * vecs, 1) for j in range(1, ITERS)], axis=0
    )
    eye = lax.broadcasted_iota(jnp.int32, (vecs, LANE), 0) == lax.broadcasted_iota(jnp.int32, (vecs, LANE), 1)
    iterate = eye.astype(jnp.float32)
    search = None
    for i in range(ITERS):
        keep, step, past = (turn_ref[i, j] for j in range(3))
        weighted = mul(iterate, hankel) if i else moments
        own = mul(weighted, iterate, NT)
        theta = mul(pltpu.roll(weighted, LANE - vecs, 1), iterate, NT)
        images = mul(pltpu.roll(weighted, LANE - 2 * vecs, 1), iterate, NT)
        terms = jnp.where(eye, images, 0.0) - 2.0 * theta * theta + theta * mul(own, theta)
        spread = jnp.maximum(jnp.sum(terms, axis=0, keepdims=True), 0.0)
        scaled = step / jnp.sqrt(spread + 1e-06)
        residual = pltpu.roll(iterate, vecs, 1) - mul(theta, iterate)
        moved = mul(scaled, residual)
        if search is not None:
            moved = moved - mul(-past, search)
        iterate = moved - mul(-keep, iterate)
        search = moved
    ritz_ref[...] = theta[:, :vecs]
    width = 4 * LANE
    for j in range(eigen_ref.shape[1] // width):
        lanes = slice(j * width, (j + 1) * width)
        eigen_ref[:, lanes] = mul(iterate, basis_ref[:, lanes])


def body(tiles, tile_row, tile_col, tile_counts, start, rotation):
    tiles = tiles.reshape(tiles.shape[2:])
    slots = tiles.shape[0]
    vecs, seg_rows = start.shape
    rows = lax.axis_size("row")
    cols = lax.axis_size("col")
    seg_tiles = seg_rows // LANE
    index = (tile_counts.reshape(1), tile_row.reshape(slots), tile_col.reshape(slots))
    own_col = lax.axis_index("col")
    dealt = f32(seg_tiles, vecs, 3 * LANE)
    work = [
        pltpu.VMEM((3 * seg_tiles, 2 * vecs, LANE), jnp.bfloat16),
        pltpu.VMEM((3 * seg_tiles, vecs, LANE), jnp.float32),
    ]
    sums = [pltpu.VMEM((cols, 2 * LANE), jnp.float32)]
    got = f32(rows, cols, 3 * LANE)

    def swap(x):
        width = x.shape[-1]
        moved = lax.all_to_all(x.reshape(rows * cols, width), BOTH, 0, 0)
        return moved.reshape(rows, cols, width)

    start_tiles = start.reshape(vecs, seg_tiles, LANE).transpose(1, 0, 2)
    pieces = lax.all_to_all(start_tiles, "row", 0, 0)
    piece = lax.dynamic_slice_in_dim(pieces, 2 * own_col, 2, 0)
    block = lax.all_to_all(jnp.broadcast_to(piece, (rows, 2, vecs, LANE)), "row", 0, 0)

    sent = kernel_call(multiply_first, "multiply_first", dealt, [SMEM] * 3 + [VMEM] * 3, work)(
        *index, tiles, start_tiles, block
    )
    images = []
    for _ in range(ITERS - 1):
        given = kernel_call(sum_and_deal, "sum_and_deal", got, [VMEM], sums)(swap(sent))
        images.append(swap(given))
        sent = kernel_call(multiply_next, "multiply_next", dealt, [SMEM] * 3 + [VMEM] * 2, work)(
            *index, tiles, images[-1]
        )
    given = kernel_call(sum_and_deal_rows, "sum_rows", f32(rows, cols, LANE), [VMEM], sums)(swap(sent))
    images.append(swap(given))

    basis, grams = kernel_call(
        gram, "gram", (f32((ITERS + 1) * vecs, seg_rows), f32(vecs, LANE)), [VMEM] * 4
    )(start, *images)
    turned = jnp.pad(jnp.swapaxes(rotation, 2, 3), ((0, 0),) * 3 + ((0, LANE - vecs),))
    grams = lax.all_to_all(jnp.broadcast_to(grams, (rows, vecs, LANE)), "row", 0, 0)
    return kernel_call(
        functools.partial(finish, seg_rows * rows),
        "finish",
        (f32(vecs, seg_rows), f32(vecs, vecs)),
        [VMEM] * 3,
    )(grams, turned, basis)


def solution(mesh):
    return jax.shard_map(
        body,
        mesh=mesh,
        in_specs=(
            P("row", "col", None, None, None),
            P("row", "col", None),
            P("row", "col", None),
            P("row", "col"),
            P(None, "row"),
            P(),
        ),
        out_specs=(P(None, "row"), P()),
        check_vma=False,
    )
```

time: 1900 us -> 314 us (0.17); the launches traced: 1880 us -> 312 us
  waiting for transfers between devices: 1360 us -> 42.2 us
  blocking collectives: 400 us -> 211 us
  matrix products: 63.6 us -> 0 us
  starting transfers between devices: 0.25 us -> 26.9 us
  Pallas kernels: 0 us -> 20.1 us
    psum x6 -> x0, waiting for transfers between devices: 1360 us -> none  [the longest x3 936 us: broadcast(): return lax.psum(jnp.where(mine, shard, jnp.zeros_like(shard)), axis)]
    psum x6 -> x0, blocking collectives: 400 us -> none  [the longest x3 211 us: body(): theta = lax.psum(gram_local, 'row') / all_rows]
    all_to_all x0 -> x6, blocking collectives: none -> 211 us  [swap(): moved = lax.all_to_all(x.reshape(rows * cols, width), BOTH, 0, 0)]
    dot_general x31 -> x0, matrix products: 63.6 us -> none  [the longest x16 25 us: rotate(): jnp.einsum('uv,un->vn', coeffs, vectors, precision=lax.Precision.HIGHEST)]
    all_to_all x0 -> x3, waiting for transfers between devices: none -> 42.2 us  [the longest x1 17.4 us: body(): lax.all_to_all(jnp.broadcast_to(piece, (rows, 2, vecs, LANE)), 'row', 0, 0)]
    all_to_all x0 -> x3, starting transfers between devices: none -> 26.9 us  [the longest x1 16.5 us: body(): pieces = lax.all_to_all(start_tiles, 'row', 0, 0)]
    pallas_call x0 -> x8, Pallas kernels: none -> 20.1 us  [the longest x2 9.54 us: body(): kernel_call(multiply_next, 'multiply_next', dealt, [SMEM] * 3 + [VMEM] *...]
  transfers between devices with their start and end apart: 6 -> 3, of which waited for: 6 -> 3; matrix products, arithmetic and copies ran while one was open for 1% -> 0% of each run, Pallas kernels for 0% -> 0%
where the time goes in v1:
time: 314 us; the launch traced here: 312 us
  blocking collectives  211 us (67%)
  waiting for transfers between devices  42.2 us (13%)
  starting transfers between devices  26.9 us (9%)
  Pallas kernels  20.1 us (6%)
  local copies, waits for them, and re-layouts  10.9 us (3%)
    all_to_all x6, blocking collectives, swap(): moved = lax.all_to_all(x.reshape(rows * cols, width), BOTH, 0, 0)  211 us
    all_to_all x1, waiting for transfers between devices, body(): lax.all_to_all(jnp.broadcast_to(piece, (rows, 2, vecs, LANE)), 'row', 0, 0)  17.4 us
    all_to_all x1, starting transfers between devices, body(): pieces = lax.all_to_all(start_tiles, 'row', 0, 0)  16.5 us
    all_to_all x1, waiting for transfers between devices, body(): pieces = lax.all_to_all(start_tiles, 'row', 0, 0)  12.5 us
    all_to_all x1, waiting for transfers between devices, body(): lax.all_to_all(jnp.broadcast_to(grams, (rows, vecs, LANE)), 'row', 0, 0)  12.4 us
    pallas_call x2, Pallas kernels, body(): kernel_call(multiply_next, 'multiply_next', dealt, [SMEM] * 3 + [VMEM] *...  9.54 us
    all_to_all x1, starting transfers between devices, body(): lax.all_to_all(jnp.broadcast_to(piece, (rows, 2, vecs, LANE)), 'row', 0, 0)  6.34 us
  transfers between devices with their start and end apart: 3, of which 3 were waited for; matrix products, arithmetic and copies ran while one was open for 0% of the time, Pallas kernels for 0%

profile of v1, /device:TPU:1, one launch (start us, length us, event | category | flops | bytes accessed | tf_op | source)
XLA Modules:
  0.0 312.5 jit_solution(4317054191144766261)
XLA Ops:
  0.6 1.7 bitcast_bitcast_fusion.seg_ref
  2.3 16.5 %all-to-all-start = ((f32[32,16,128]{2,1,0:T(8,128)}), f32[32,16,128]{2,1,0:T(8,128)S(1)}, u32[]{:S(2)}, u32[]{:S(2)}) async-start(f32[32,16,128]{2,1,0:T(8,128)} %bitcast_bitcast_fusion.seg_ref), calls=%async_computation | async-start | bytes 524288 | tf_op jit(solution)/shard_map/all_to_all | solution.py:211
  18.8 12.5 %all-to-all-done = f32[32,16,128]{2,1,0:T(8,128)S(1)} async-done(((f32[32,16,128]{2,1,0:T(8,128)}), f32[32,16,128]{2,1,0:T(8,128)S(1)}, u32[]{:S(2)}, u32[]{:S(2)}) %all-to-all-start) | async-done | bytes 262176 | tf_op jit(solution)/shard_map/all_to_all | solution.py:211
  31.3 0.9 broadcast_in_dim.6
  32.2 6.3 %all-to-all-start.1 = ((f32[32,2,16,128]{3,2,1,0:T(8,128)}), f32[32,2,16,128]{3,2,1,0:T(8,128)S(1)}, u32[]{:S(2)}, u32[]{:S(2)}) async-start(f32[32,2,16,128]{3,2,1,0:T(8,128)} %broadcast_in_dim.6), calls=%async_computation.1 | async-start | bytes 1048576 | tf_op jit(solution)/shard_map/all_to_all | solution.py:213
  39.2 17.4 %all-to-all-done.1.block_ref = f32[32,2,16,128]{3,2,1,0:T(8,128)S(1)} async-done(((f32[32,2,16,128]{3,2,1,0:T(8,128)}), f32[32,2,16,128]{3,2,1,0:T(8,128)S(1)}, u32[]{:S(2)}, u32[]{:S(2)}) %all-to-all-start.1) | async-done | bytes 524320 | tf_op jit(solution)/shard_map/all_to_all | solution.py:213
  56.5 0.0 copy-start
  56.5 1.9 copy-done
  58.4 0.0 copy-start.3
  58.4 0.7 copy-done.3
  59.1 0.0 copy-start.5
  59.1 0.7 copy-done.5
  59.7 5.2 %multiply_first.1 = f32[32,16,384]{2,1,0:T(8,128)S(1)} custom-call(s32[1]{0:T(128)} %bitcast.26.count_ref, s32[96]{0:T(128)S(1)} %bitcast.46, s32[96]{0:T(128)S(1)} %bitcast.49, bf16[96,128,128]{2,1,0:T(8,128)(2,1)S(1)} %bitcast.29, f32[32,16,128]{2,1,0:T(8,128)} %bitcast_bitcast_fusion.seg_ref, f32[32,2,16,128]{3,2,1,0:T(8,128)S(1)} %all-to-all-done.1.block_ref), custom_call_target="tpu_custom_call" | custom-call | tf_op jit(solution)/shard_map/multiply_first/pallas_call | solution.py:215
  64.9 0.8 copy.12
  65.7 40.5 %all_to_all.69 = f32[512,1,384]{2,1,0:T(1,128)S(1)} all-to-all(f32[512,1,384]{2,1,0:T(1,128)S(1)} %copy.12), channel_id=1, replica_groups=mesh['row'=32,'col'=16] {'row','col'}, dimensions={0} | all-to-all | bytes 1572864 | tf_op jit(solution)/shard_map/all_to_all | solution.py:207
  106.2 0.1 copy.19
  106.3 0.0 copy-start.1
  106.3 0.0 copy-start.4
  106.3 0.0 copy-start.6
  106.3 0.1 sum_and_deal.2
  106.5 0.8 copy.13
  107.3 36.3 %all_to_all.70 = f32[512,1,384]{2,1,0:T(1,128)S(1)} all-to-all(f32[512,1,384]{2,1,0:T(1,128)S(1)} %copy.13), channel_id=1, replica_groups=mesh['row'=32,'col'=16] {'row','col'}, dimensions={0} | all-to-all | bytes 1572864 | tf_op jit(solution)/shard_map/all_to_all | solution.py:207
  143.6 0.1 copy.20
  143.7 0.0 copy-done.1
  143.7 0.0 copy-done.4
  143.7 0.0 copy-done.6
  143.7 4.8 %multiply_next.2 = f32[32,16,384]{2,1,0:T(8,128)S(1)} custom-call(s32[1]{0:T(128)} %bitcast.27.count_ref, s32[96]{0:T(128)S(1)} %bitcast.47, s32[96]{0:T(128)S(1)} %bitcast.50, bf16[96,128,128]{2,1,0:T(8,128)(2,1)S(1)} %bitcast.30, f32[32,16,384]{2,1,0:T(8,128)S(1)} %bitcast.32), custom_call_target="tpu_custom_call" | custom-call | tf_op jit(solution)/shard_map/multiply_next/pallas_call | solution.py:222
  148.5 0.8 copy.14
  149.3 35.6 %all_to_all.71 = f32[512,1,384]{2,1,0:T(1,128)S(1)} all-to-all(f32[512,1,384]{2,1,0:T(1,128)S(1)} %copy.14), channel_id=1, replica_groups=mesh['row'=32,'col'=16] {'row','col'}, dimensions={0} | all-to-all | bytes 1572864 | tf_op jit(solution)/shard_map/all_to_all | solution.py:207
  184.9 0.1 copy.21
  185.0 0.1 sum_and_deal.3
  185.1 0.8 copy.15
  185.9 36.3 %all_to_all.72 = f32[512,1,384]{2,1,0:T(1,128)S(1)} all-to-all(f32[512,1,384]{2,1,0:T(1,128)S(1)} %copy.15), channel_id=1, replica_groups=mesh['row'=32,'col'=16] {'row','col'}, dimensions={0} | all-to-all | bytes 1572864 | tf_op jit(solution)/shard_map/all_to_all | solution.py:207
  222.3 0.1 copy.22
  222.3 4.8 %multiply_next.3 = f32[32,16,384]{2,1,0:T(8,128)S(1)} custom-call(s32[1]{0:T(128)} %bitcast.28.count_ref, s32[96]{0:T(128)S(1)} %bitcast.48, s32[96]{0:T(128)S(1)} %bitcast.51, bf16[96,128,128]{2,1,0:T(8,128)(2,1)S(1)} %bitcast.31, f32[32,16,384]{2,1,0:T(8,128)S(1)} %bitcast.34), custom_call_target="tpu_custom_call" | custom-call | tf_op jit(solution)/shard_map/multiply_next/pallas_call | solution.py:222
  227.1 0.0 copy-start.2
  227.1 0.8 copy.16
  227.9 35.6 %all_to_all.73 = f32[512,1,384]{2,1,0:T(1,128)S(1)} all-to-all(f32[512,1,384]{2,1,0:T(1,128)S(1)} %copy.16), channel_id=1, replica_groups=mesh['row'=32,'col'=16] {'row','col'}, dimensions={0} | all-to-all | bytes 1572864 | tf_op jit(solution)/shard_map/all_to_all | solution.py:207
  263.6 0.0 copy-start.7
  263.6 0.1 copy.23
  263.6 0.1 sum_rows.1
  263.7 26.3 %all_to_all.74 = f32[512,1,128]{2,1,0:T(1,128)S(1)} all-to-all(f32[512,1,128]{2,1,0:T(1,128)S(1)} %bitcast.44), channel_id=1, replica_groups=mesh['row'=32,'col'=16] {'row','col'}, dimensions={0} | all-to-all | bytes 524288 | tf_op jit(solution)/shard_map/all_to_all | solution.py:207
  290.1 0.0 copy-done.2
  290.1 1.9 gram.1
  291.9 0.8 broadcast_in_dim.7
  292.7 4.1 %all-to-all-start.8 = ((f32[32,16,128]{2,1,0:T(8,128)}), f32[32,16,128]{2,1,0:T(8,128)S(1)}, u32[]{:S(2)}, u32[]{:S(2)}) async-start(f32[32,16,128]{2,1,0:T(8,128)} %broadcast_in_dim.7), calls=%async_computation.8 | async-start | bytes 524288 | tf_op jit(solution)/shard_map/all_to_all | solution.py:232
  296.8 0.0 copy-done.7
  296.8 0.1 copy.18
  296.9 12.4 %all-to-all-done.8.grams_ref = f32[32,16,128]{2,1,0:T(8,128)S(1)} async-done(((f32[32,16,128]{2,1,0:T(8,128)}), f32[32,16,128]{2,1,0:T(8,128)S(1)}, u32[]{:S(2)}, u32[]{:S(2)}) %all-to-all-start.8) | async-done | bytes 262176 | tf_op jit(solution)/shard_map/all_to_all | solution.py:232
  309.3 3.2 %finish.1 = (f32[16,4096]{1,0:T(8,128)}, f32[16,16]{1,0:T(8,128)}) custom-call(f32[32,16,128]{2,1,0:T(8,128)S(1)} %all-to-all-done.8.grams_ref, f32[3,3,16,128]{3,2,1,0:T(8,128)S(1)} %pad.4.turn_ref, f32[64,4096]{1,0:T(8,128)S(1)} %get-tuple-element.5.basis_ref), custom_call_target="tpu_custom_call" | custom-call | tf_op jit(solution)/shard_map/finish/pallas_call | solution.py:233
  (2 shorter events, 0.0 us)
Async XLA Ops:
  2.3 29.0 %all-to-all-start = ((f32[32,16,128]{2,1,0:T(8,128)}), f32[32,16,128]{2,1,0:T(8,128)S(1)}, u32[]{:S(2)}, u32[]{:S(2)}) async-start(f32[32,16,128]{2,1,0:T(8,128)} %bitcast_bitcast_fusion.seg_ref), calls=%async_computation | async-start | bytes 524288 | tf_op jit(solution)/shard_map/all_to_all | solution.py:211
  32.2 24.4 %all-to-all-start.1 = ((f32[32,2,16,128]{3,2,1,0:T(8,128)}), f32[32,2,16,128]{3,2,1,0:T(8,128)S(1)}, u32[]{:S(2)}, u32[]{:S(2)}) async-start(f32[32,2,16,128]{3,2,1,0:T(8,128)} %broadcast_in_dim.6), calls=%async_computation.1 | async-start | bytes 1048576 | tf_op jit(solution)/shard_map/all_to_all | solution.py:213
  56.5 1.9 copy-start
  58.4 0.7 copy-start.3
  59.1 0.7 copy-start.5
  106.3 37.4 %copy-start.1 = (bf16[1,1,96,128,128]{4,3,2,1,0:T(8,128)(2,1)S(1)}, bf16[1,1,96,128,128]{4,3,2,1,0:T(8,128)(2,1)}, u32[]{:S(2)}) copy-start(bf16[1,1,96,128,128]{4,3,2,1,0:T(8,128)(2,1)} %param.6) | copy-start | bytes 9437188
  106.3 37.4 %copy-start.4 = (s32[1,1,96]{2,1,0:T(1,128)S(1)}, s32[1,1,96]{2,1,0:T(1,128)}, u32[]{:S(2)}) copy-start(s32[1,1,96]{2,1,0:T(1,128)} %param.7) | copy-start | bytes 1156
  106.3 37.4 %copy-start.6 = (s32[1,1,96]{2,1,0:T(1,128)S(1)}, s32[1,1,96]{2,1,0:T(1,128)}, u32[]{:S(2)}) copy-start(s32[1,1,96]{2,1,0:T(1,128)} %param.8) | copy-start | bytes 1156
  227.1 62.9 %copy-start.2 = (f32[16,4096]{1,0:T(8,128)S(1)}, f32[16,4096]{1,0:T(8,128)}, u32[]{:S(2)}) copy-start(f32[16,4096]{1,0:T(8,128)} %start_ref.1) | copy-start | bytes 786436
  263.6 33.2 %copy-start.7 = (f32[3,3,16,16]{3,2,1,0:T(8,128)S(1)}, f32[3,3,16,16]{3,2,1,0:T(8,128)}, u32[]{:S(2)}) copy-start(f32[3,3,16,16]{3,2,1,0:T(8,128)} %param.11) | copy-start | bytes 27652
  292.7 16.6 %all-to-all-start.8 = ((f32[32,16,128]{2,1,0:T(8,128)}), f32[32,16,128]{2,1,0:T(8,128)S(1)}, u32[]{:S(2)}, u32[]{:S(2)}) async-start(f32[32,16,128]{2,1,0:T(8,128)} %broadcast_in_dim.7), calls=%async_computation.8 | async-start | bytes 524288 | tf_op jit(solution)/shard_map/all_to_all | solution.py:232

commit v2 on v1

--- a/solution.py
+++ b/solution.py
@@ -16,6 +16,7 @@
 NN = (((1,), (0,)), ((), ()))
 SMEM = pl.BlockSpec(memory_space=pltpu.SMEM)
 VMEM = pl.BlockSpec(memory_space=pltpu.VMEM)
+ANY = pl.BlockSpec(memory_space=pl.ANY)
 
 
 def kernel_call(kernel, name, out, ins, scratch=()):
@@ -34,9 +35,10 @@
     return jax.ShapeDtypeStruct(shape, jnp.float32)
 
 
-def multiply(get_seg, get_block, count_ref, row_ref, col_ref, tiles_ref, refs, out_ref, split, total):
-    seg_tiles = out_ref.shape[0]
-    vecs = out_ref.shape[1]
+def multiply(get_seg, get_block, index, tiles_ref, refs, split, total, ready=None):
+    count_ref, row_ref, col_ref = index
+    seg_tiles = total.shape[0] // 3
+    vecs = total.shape[1]
 
     def keep(slot, values):
         high = values.astype(jnp.bfloat16)
@@ -48,9 +50,13 @@
         for half in range(2):
             keep(seg_tiles * (1 + half) + t, get_block(refs, t, half))
     total[...] = jnp.zeros_like(total)
+    if ready is not None:
+        ready()
     count = count_ref[0]
 
     def group(g, carry):
+        if ready is not None:
+            ready(g)
         parts = []
         for j in range(GROUP):
             slot = g * GROUP + j
@@ -66,27 +72,70 @@
             total[place] += part
         return carry
 
-    lax.fori_loop(0, (count + (GROUP - 1)) // GROUP, group, 0)
+    groups = tiles_ref.shape[0] // GROUP if ready is not None else (count + (GROUP - 1)) // GROUP
+    lax.fori_loop(0, groups, group, 0)
+
+
+def lay_out(total, out_ref):
+    seg_tiles = out_ref.shape[0]
     for t in range(seg_tiles):
-        out_ref[t, :, 0:LANE] = total[t]
-        out_ref[t, :, LANE : 2 * LANE] = total[seg_tiles + t]
-        out_ref[t, :, 2 * LANE : 3 * LANE] = total[2 * seg_tiles + t]
-
-
-def multiply_first(count_ref, row_ref, col_ref, tiles_ref, seg_ref, block_ref, out_ref, split, total):
+        for part in range(3):
+            out_ref[t, :, part * LANE : (part + 1) * LANE] = total[part * seg_tiles + t]
+
+
+def multiply_first(count_hbm, row_hbm, col_hbm, tiles_hbm, seg_ref, block_ref, out_ref, split, total, tiles_ref, *more):
+    index, index_sem, tiles_sem = more[0:3], more[3], more[4]
+    seg_tiles = seg_ref.shape[0]
+    vecs = seg_ref.shape[1]
+    index_copies = [
+        pltpu.make_async_copy(source, place, index_sem.at[i])
+        for i, (source, place) in enumerate(zip((count_hbm, row_hbm, col_hbm), index))
+    ]
+
+    def tile_copy(g):
+        some = pl.ds(g * GROUP, GROUP)
+        return pltpu.make_async_copy(tiles_hbm.at[some], tiles_ref.at[some], tiles_sem.at[g])
+
+    for copy in index_copies:
+        copy.start()
+    for g in range(tiles_ref.shape[0] // GROUP):
+        tile_copy(g).start()
+
+    def ready(g=None):
+        if g is None:
+            for copy in index_copies:
+                copy.wait()
+        else:
+            tile_copy(g).wait()
+
     multiply(
         lambda refs, t: refs[0][t],
-        lambda refs, t, half: refs[1][t, half],
-        count_ref, row_ref, col_ref, tiles_ref, (seg_ref, block_ref), out_ref, split, total,
-    )
+        lambda refs, t, half: refs[1][(half * seg_tiles + t) // 2, t % 2],
+        index, tiles_ref, (seg_ref, block_ref), split, total, ready,
+    )
+    lay_out(total, out_ref)
+
+
+def take_seg(refs, t):
+    return refs[0][t, :, 0:LANE]
+
+
+def take_block(refs, t, half):
+    return refs[0][t, :, (1 + half) * LANE : (2 + half) * LANE]
 
 
 def multiply_next(count_ref, row_ref, col_ref, tiles_ref, all_ref, out_ref, split, total):
-    multiply(
-        lambda refs, t: refs[0][t, :, 0:LANE],
-        lambda refs, t, half: refs[0][t, :, (1 + half) * LANE : (2 + half) * LANE],
-        count_ref, row_ref, col_ref, tiles_ref, (all_ref,), out_ref, split, total,
-    )
+    multiply(take_seg, take_block, (count_ref, row_ref, col_ref), tiles_ref, (all_ref,), split, total)
+    lay_out(total, out_ref)
+
+
+def multiply_last(count_ref, row_ref, col_ref, tiles_ref, all_ref, direct_ref, mirror_ref, split, total):
+    multiply(take_seg, take_block, (count_ref, row_ref, col_ref), tiles_ref, (all_ref,), split, total)
+    seg_tiles = direct_ref.shape[0]
+    for t in range(seg_tiles):
+        direct_ref[t] = total[t]
+        for half in range(2):
+            mirror_ref[half * seg_tiles + t] = total[(1 + half) * seg_tiles + t]
 
 
 def add_up(got_ref, sums):
@@ -114,39 +163,22 @@
         out_ref[r, :, LANE : 3 * LANE] = block
 
 
-def sum_and_deal_rows(got_ref, out_ref, sums):
-    rows, cols = got_ref.shape[0], got_ref.shape[1]
-    add_up(got_ref, sums)
-    for r in range(rows):
-        half = r % 2
-        out_ref[r] = jnp.broadcast_to(
-            sums[r // 2 : r // 2 + 1, half * LANE : (half + 1) * LANE], (cols, LANE)
-        )
-
-
-def gram(start_ref, one_ref, two_ref, three_ref, basis_ref, gram_ref):
-    tiles, vecs = three_ref.shape[0], three_ref.shape[1]
-    basis_ref[0:vecs, :] = start_ref[...]
-    for t in range(tiles):
-        lanes = slice(t * LANE, (t + 1) * LANE)
-        basis_ref[vecs : 2 * vecs, lanes] = one_ref[t, :, 0:LANE]
-        basis_ref[2 * vecs : 3 * vecs, lanes] = two_ref[t, :, 0:LANE]
-        basis_ref[3 * vecs : 4 * vecs, lanes] = three_ref[t]
+def gram(own_ref, three_ref, gram_ref):
+    vecs = three_ref.shape[1]
+    basis = [jnp.concatenate([own_ref[j, i] for i in range(2)], axis=1) for j in range(ITERS)]
+    basis.append(jnp.concatenate([three_ref[i] for i in range(2)], axis=1))
     parts = []
-    for j in range(ITERS + 1):
-        top = min(j + 2, ITERS + 1)
+    for j in range(2 * ITERS + 1):
         parts.append(
             lax.dot_general(
-                basis_ref[j * vecs : (j + 1) * vecs, :],
-                basis_ref[j * vecs : top * vecs, :],
-                NT, precision=HIGH, preferred_element_type=jnp.float32,
+                basis[j // 2], basis[(j + 1) // 2], NT, precision=HIGH, preferred_element_type=jnp.float32
             )
         )
     parts.append(jnp.zeros((vecs, LANE - (2 * ITERS + 1) * vecs), jnp.float32))
     gram_ref[...] = jnp.concatenate(parts, axis=1)
 
 
-def finish(states, grams_ref, turn_ref, basis_ref, eigen_ref, ritz_ref):
+def finish(states, grams_ref, turn_ref, start_ref, one_ref, two_ref, three_ref, eigen_ref, ritz_ref):
     vecs = eigen_ref.shape[0]
 
     def mul(a, b, dims=NN):
@@ -179,10 +211,10 @@
         iterate = moved - mul(-keep, iterate)
         search = moved
     ritz_ref[...] = theta[:, :vecs]
-    width = 4 * LANE
-    for j in range(eigen_ref.shape[1] // width):
-        lanes = slice(j * width, (j + 1) * width)
-        eigen_ref[:, lanes] = mul(iterate, basis_ref[:, lanes])
+    for t in range(three_ref.shape[0]):
+        lanes = slice(t * LANE, (t + 1) * LANE)
+        basis = [start_ref[:, lanes], one_ref[t, :, 0:LANE], two_ref[t, :, 0:LANE], three_ref[t]]
+        eigen_ref[:, lanes] = mul(iterate, jnp.concatenate(basis, axis=0))
 
 
 def body(tiles, tile_row, tile_col, tile_counts, start, rotation):
@@ -199,43 +231,72 @@
         pltpu.VMEM((3 * seg_tiles, 2 * vecs, LANE), jnp.bfloat16),
         pltpu.VMEM((3 * seg_tiles, vecs, LANE), jnp.float32),
     ]
+    fetched = [
+        pltpu.VMEM(tiles.shape, tiles.dtype),
+        pltpu.SMEM((1,), jnp.int32),
+        pltpu.SMEM((slots,), jnp.int32),
+        pltpu.SMEM((slots,), jnp.int32),
+        pltpu.SemaphoreType.DMA((3,)),
+        pltpu.SemaphoreType.DMA((slots // GROUP,)),
+    ]
     sums = [pltpu.VMEM((cols, 2 * LANE), jnp.float32)]
     got = f32(rows, cols, 3 * LANE)
+    corner = []
+    for r in range(rows):
+        for c in range(cols):
+            corner.append((r * cols + c, ((r % 2) * cols + c) * cols + r // 2))
 
     def swap(x):
         width = x.shape[-1]
         moved = lax.all_to_all(x.reshape(rows * cols, width), BOTH, 0, 0)
         return moved.reshape(rows, cols, width)
 
+    def own_tiles(x):
+        return lax.dynamic_slice_in_dim(x, 2 * own_col, 2, 0)[:, :, :LANE]
+
     start_tiles = start.reshape(vecs, seg_tiles, LANE).transpose(1, 0, 2)
-    pieces = lax.all_to_all(start_tiles, "row", 0, 0)
-    piece = lax.dynamic_slice_in_dim(pieces, 2 * own_col, 2, 0)
+    own_start = own_tiles(start_tiles)
+    piece = lax.ppermute(own_start, BOTH, corner)
     block = lax.all_to_all(jnp.broadcast_to(piece, (rows, 2, vecs, LANE)), "row", 0, 0)
 
-    sent = kernel_call(multiply_first, "multiply_first", dealt, [SMEM] * 3 + [VMEM] * 3, work)(
+    sent = kernel_call(multiply_first, "multiply_first", dealt, [ANY] * 4 + [VMEM] * 2, work + fetched)(
         *index, tiles, start_tiles, block
     )
     images = []
-    for _ in range(ITERS - 1):
+    for i in range(ITERS - 1):
         given = kernel_call(sum_and_deal, "sum_and_deal", got, [VMEM], sums)(swap(sent))
         images.append(swap(given))
-        sent = kernel_call(multiply_next, "multiply_next", dealt, [SMEM] * 3 + [VMEM] * 2, work)(
-            *index, tiles, images[-1]
-        )
-    given = kernel_call(sum_and_deal_rows, "sum_rows", f32(rows, cols, LANE), [VMEM], sums)(swap(sent))
-    images.append(swap(given))
-
-    basis, grams = kernel_call(
-        gram, "gram", (f32((ITERS + 1) * vecs, seg_rows), f32(vecs, LANE)), [VMEM] * 4
-    )(start, *images)
+        if i < ITERS - 2:
+            sent = kernel_call(multiply_next, "multiply_next", dealt, [SMEM] * 3 + [VMEM] * 2, work)(
+                *index, tiles, images[-1]
+            )
+    direct, mirror = kernel_call(
+        multiply_last,
+        "multiply_last",
+        (f32(seg_tiles, vecs, LANE), f32(2 * seg_tiles, vecs, LANE)),
+        [SMEM] * 3 + [VMEM] * 2,
+        work,
+    )(*index, tiles, images[-1])
+
+    mirror = jnp.sum(lax.all_to_all(mirror.reshape(rows, 2, vecs, LANE), "row", 0, 0), axis=0)
+    direct, mirror = lax.optimization_barrier((direct, mirror))
+    turned_back = lax.ppermute(mirror, BOTH, [(to, at) for at, to in corner])
+    direct = jnp.sum(lax.all_to_all(direct.reshape(cols, 2, vecs, LANE), "col", 0, 0), axis=0)
+    last_piece = direct + turned_back
+    own = jnp.stack([own_start] + [own_tiles(image) for image in images])
+    grams = kernel_call(gram, "gram", f32(vecs, LANE), [VMEM] * 2)(own, last_piece)
+    shared = jnp.concatenate([last_piece, grams[None]], axis=0)
+    shared = lax.all_to_all(jnp.broadcast_to(shared, (cols, 3, vecs, LANE)), "col", 0, 0)
+    last = shared[:, 0:2].reshape(seg_tiles, vecs, LANE)
+    grams = jnp.sum(shared[:, 2], axis=0)
+    grams = lax.all_to_all(jnp.broadcast_to(grams, (rows, vecs, LANE)), "row", 0, 0)
     turned = jnp.pad(jnp.swapaxes(rotation, 2, 3), ((0, 0),) * 3 + ((0, LANE - vecs),))
-    grams = lax.all_to_all(jnp.broadcast_to(grams, (rows, vecs, LANE)), "row", 0, 0)
     return kernel_call(
         functools.partial(finish, seg_rows * rows),
         "finish",
         (f32(vecs, seg_rows), f32(vecs, vecs)),
-        [VMEM] * 3,
-    )(grams, turned, basis)
+        [VMEM] * 6,
+    )(grams, turned, start, *images, last)
 
 
 def solution(mesh):

time: 314 us -> 301 us (0.959)
  starting transfers between devices: 26.9 us -> 44.7 us
  blocking collectives: 211 us -> 195 us
  Pallas kernels: 20.1 us -> 13.1 us
  waiting for transfers between devices: 42.2 us -> 35.6 us
    all_to_all x6 -> x4, blocking collectives: 211 us -> 151 us  [swap(): moved = lax.all_to_all(x.reshape(rows * cols, width), BOTH, 0, 0)]
    all_to_all x0 -> x2, blocking collectives: none -> 44.3 us  [the longest x1 24.7 us: body(): lax.all_to_all(mirror.reshape(rows, 2, vecs, LANE), 'row', 0, 0)]
    all_to_all x1, starting transfers between devices: 6.34 us -> 23.2 us  [body(): lax.all_to_all(jnp.broadcast_to(piece, (rows, 2, vecs, LANE)), 'row', 0, 0)]
    all_to_all x1, starting transfers between devices: 16.5 us -> 5.46 us  [body(): lax.all_to_all(direct.reshape(cols, 2, vecs, LANE), 'col', 0, 0)]
    ppermute x0 -> x2, starting transfers between devices: none -> 9.18 us  [the longest x1 5.39 us: body(): piece = lax.ppermute(own_start, BOTH, corner)]
    all_to_all x1, waiting for transfers between devices: 12.5 us -> 3.42 us  [body(): lax.all_to_all(direct.reshape(cols, 2, vecs, LANE), 'col', 0, 0)]
    pallas_call x2 -> x1, Pallas kernels: 9.54 us -> 1.74 us  [body(): kernel_call(multiply_next, 'multiply_next', dealt, [SMEM] * 3 + [VMEM] *...]
    ppermute x0 -> x2, waiting for transfers between devices: none -> 3.22 us  [the longest x1 3.22 us: body(): piece = lax.ppermute(own_start, BOTH, corner)]
  transfers between devices with their start and end apart: 3 -> 5, of which waited for: 3 -> 4; matrix products, arithmetic and copies ran while one was open for 0% -> 0% of each run, Pallas kernels for 0% -> 0%
where the time goes in v2:
time: 301 us; the launch traced here: 299 us
  blocking collectives  195 us (65%)
  starting transfers between devices  44.7 us (15%)
  waiting for transfers between devices  35.6 us (12%)
  Pallas kernels  13.1 us (4%)
  local copies, waits for them, and re-layouts  9.39 us (3%)
    all_to_all x4, blocking collectives, swap(): moved = lax.all_to_all(x.reshape(rows * cols, width), BOTH, 0, 0)  151 us
    all_to_all x1, blocking collectives, body(): lax.all_to_all(mirror.reshape(rows, 2, vecs, LANE), 'row', 0, 0)  24.7 us
    all_to_all x1, starting transfers between devices, body(): lax.all_to_all(jnp.broadcast_to(piece, (rows, 2, vecs, LANE)), 'row', 0, 0)  23.2 us
    all_to_all x1, blocking collectives, body(): lax.all_to_all(jnp.broadcast_to(shared, (cols, 3, vecs, LANE)), 'col', 0, 0)  19.5 us
    all_to_all x1, waiting for transfers between devices, body(): lax.all_to_all(jnp.broadcast_to(piece, (rows, 2, vecs, LANE)), 'row', 0, 0)  16.4 us
    all_to_all x1, waiting for transfers between devices, body(): lax.all_to_all(jnp.broadcast_to(grams, (rows, vecs, LANE)), 'row', 0, 0)  12.5 us
    all_to_all x1, starting transfers between devices, body(): lax.all_to_all(jnp.broadcast_to(grams, (rows, vecs, LANE)), 'row', 0, 0)  6.82 us
  transfers between devices with their start and end apart: 5, of which 4 were waited for; matrix products, arithmetic and copies ran while one was open for 0% of the time, Pallas kernels for 0%

profile of v2, /device:TPU:1, one launch (start us, length us, event | category | flops | bytes accessed | tf_op | source)
XLA Modules:
  0.0 299.4 jit_solution(7529311337573772591)
XLA Ops:
  0.6 1.0 copy_bitcast_fusion
  1.6 5.4 %collective-permute-start = (f32[2,16,128]{2,1,0:T(8,128)S(1)}, f32[2,16,128]{2,1,0:T(8,128)S(1)}, u32[]{:S(2)}, u32[]{:S(2)}) collective-permute-start(f32[2,16,128]{2,1,0:T(8,128)S(1)} %get-tuple-element.11), channel_id=1, source_target_pairs={{0,0},{1,16},{2,32},{3,48},{4,64},{5,80},{6,96},{7,112},{8,128},{9... | collective-permute-start | bytes 49160 | tf_op jit(solution)/shard_map/ppermute | solution.py:259
  7.0 3.2 %collective-permute-done = f32[2,16,128]{2,1,0:T(8,128)S(1)} collective-permute-done((f32[2,16,128]{2,1,0:T(8,128)S(1)}, f32[2,16,128]{2,1,0:T(8,128)S(1)}, u32[]{:S(2)}, u32[]{:S(2)}) %collective-permute-start) | collective-permute-done | bytes 16416 | tf_op jit(solution)/shard_map/ppermute | solution.py:259
  10.3 0.8 broadcast_in_dim.12
  11.1 23.2 %all-to-all-start = ((f32[32,2,16,128]{3,2,1,0:T(8,128)}), f32[32,2,16,128]{3,2,1,0:T(8,128)S(1)}, u32[]{:S(2)}, u32[]{:S(2)}) async-start(f32[32,2,16,128]{3,2,1,0:T(8,128)} %broadcast_in_dim.12), calls=%async_computation | async-start | bytes 1048576 | tf_op jit(solution)/shard_map/all_to_all | solution.py:260
  35.0 16.4 %all-to-all-done.block_ref = f32[32,2,16,128]{3,2,1,0:T(8,128)S(1)} async-done(((f32[32,2,16,128]{3,2,1,0:T(8,128)}), f32[32,2,16,128]{3,2,1,0:T(8,128)S(1)}, u32[]{:S(2)}, u32[]{:S(2)}) %all-to-all-start) | async-done | bytes 524320 | tf_op jit(solution)/shard_map/all_to_all | solution.py:260
  51.4 0.0 copy-start
  51.4 1.9 copy-done
  53.2 0.0 copy-start.3
  53.3 0.7 copy-done.3
  53.9 0.0 copy-start.5
  53.9 0.7 copy-done.5
  54.6 4.8 %multiply_first.1 = f32[32,16,384]{2,1,0:T(8,128)S(1)} custom-call(s32[1]{0:T(128)} %bitcast.35.count_hbm, s32[96]{0:T(128)S(1)} %bitcast.56, s32[96]{0:T(128)S(1)} %bitcast.59, bf16[96,128,128]{2,1,0:T(8,128)(2,1)S(1)} %bitcast.38, f32[32,16,128]{2,1,0:T(8,128)S(1)} %get-tuple-element.13.seg_ref, f32[32,2,16,128]{3,2,1,0:T(8,128)S(1)} %all-to-all-done.block_ref), custom_call_target="tpu_custom_call" | custom-call | tf_op jit(solution)/shard_map/multiply_first/pallas_call | solution.py:262
  59.4 0.8 copy.14
  60.2 38.6 %all_to_all.61 = f32[512,1,384]{2,1,0:T(1,128)S(1)} all-to-all(f32[512,1,384]{2,1,0:T(1,128)S(1)} %copy.14), channel_id=1, replica_groups=mesh['row'=32,'col'=16] {'row','col'}, dimensions={0} | all-to-all | bytes 1572864 | tf_op jit(solution)/shard_map/all_to_all | solution.py:251
  98.8 0.1 copy.19
  98.8 0.0 copy-start.1
  98.8 0.0 copy-start.4
  98.9 0.0 copy-start.6
  98.9 0.1 sum_and_deal.2
  99.0 0.8 copy.15
  99.8 36.3 %all_to_all.62 = f32[512,1,384]{2,1,0:T(1,128)S(1)} all-to-all(f32[512,1,384]{2,1,0:T(1,128)S(1)} %copy.15), channel_id=1, replica_groups=mesh['row'=32,'col'=16] {'row','col'}, dimensions={0} | all-to-all | bytes 1572864 | tf_op jit(solution)/shard_map/all_to_all | solution.py:251
  136.2 0.1 copy.20
  136.2 0.0 copy-done.1
  136.2 0.0 copy-done.4
  136.2 0.0 copy-done.6
  136.2 1.7 multiply_next.1
  138.0 0.8 copy.16
  138.8 39.6 %all_to_all.63 = f32[512,1,384]{2,1,0:T(1,128)S(1)} all-to-all(f32[512,1,384]{2,1,0:T(1,128)S(1)} %copy.16), channel_id=1, replica_groups=mesh['row'=32,'col'=16] {'row','col'}, dimensions={0} | all-to-all | bytes 1572864 | tf_op jit(solution)/shard_map/all_to_all | solution.py:251
  178.4 0.1 copy.21
  178.4 0.1 sum_and_deal.3
  178.5 0.8 copy.17
  179.4 36.3 %all_to_all.64 = f32[512,1,384]{2,1,0:T(1,128)S(1)} all-to-all(f32[512,1,384]{2,1,0:T(1,128)S(1)} %copy.17), channel_id=1, replica_groups=mesh['row'=32,'col'=16] {'row','col'}, dimensions={0} | all-to-all | bytes 1572864 | tf_op jit(solution)/shard_map/all_to_all | solution.py:251
  215.7 0.1 copy.22
  215.8 2.4 multiply_last.1
  218.2 0.0 copy-start.7
  218.2 0.0 copy-start.2
  218.2 24.7 %all_to_all.65 = f32[32,2,16,128]{3,2,1,0:T(8,128)S(1)} all-to-all(f32[32,2,16,128]{3,2,1,0:T(8,128)S(1)} %bitcast.54), channel_id=1, replica_groups=mesh['row'=32,'col'=16] {'row'}, dimensions={0} | all-to-all | bytes 1048576 | tf_op jit(solution)/shard_map/all_to_all | solution.py:281
  242.9 5.5 %all-to-all-start.6 = ((f32[16,2,16,128]{3,2,1,0:T(8,128)}), f32[16,2,16,128]{3,2,1,0:T(8,128)S(1)}, u32[]{:S(2)}, u32[]{:S(2)}) async-start(f32[16,2,16,128]{3,2,1,0:T(8,128)} %bitcast.11), calls=%async_computation.6 | async-start | bytes 524288 | tf_op jit(solution)/shard_map/all_to_all | solution.py:284
  248.4 3.8 %collective-permute-start.1 = (f32[2,16,128]{2,1,0:T(8,128)S(1)}, f32[2,16,128]{2,1,0:T(8,128)S(1)}, u32[]{:S(2)}, u32[]{:S(2)}) collective-permute-start(f32[2,16,128]{2,1,0:T(8,128)S(1)} %reduce_sum.27), channel_id=1, source_target_pairs={{0,0},{16,1},{32,2},{48,3},{64,4},{80,5},{96,6},{112,7},{128,8},{1... | collective-permute-start | bytes 49160 | tf_op jit(solution)/shard_map/ppermute | solution.py:283
  252.2 3.4 %all-to-all-done.6 = f32[16,2,16,128]{3,2,1,0:T(8,128)S(1)} async-done(((f32[16,2,16,128]{3,2,1,0:T(8,128)}), f32[16,2,16,128]{3,2,1,0:T(8,128)S(1)}, u32[]{:S(2)}, u32[]{:S(2)}) %all-to-all-start.6) | async-done | bytes 262176 | tf_op jit(solution)/shard_map/all_to_all | solution.py:284
  255.7 0.0 collective-permute-done.1
  255.7 0.3 gram.1
  256.1 19.5 %all_to_all.66 = f32[16,3,16,128]{3,2,1,0:T(8,128)S(1)} all-to-all(f32[16,3,16,128]{3,2,1,0:T(8,128)S(1)} %broadcast_in_dim.14), channel_id=1, replica_groups=mesh['row'=32,'col'=16] {'col'}, dimensions={0} | all-to-all | bytes 786432 | tf_op jit(solution)/shard_map/all_to_all | solution.py:289
  275.6 0.7 broadcast_in_dim.15
  276.3 6.8 %all-to-all-start.8 = ((f32[32,16,128]{2,1,0:T(8,128)}), f32[32,16,128]{2,1,0:T(8,128)S(1)}, u32[]{:S(2)}, u32[]{:S(2)}) async-start(f32[32,16,128]{2,1,0:T(8,128)} %broadcast_in_dim.15), calls=%async_computation.8 | async-start | bytes 524288 | tf_op jit(solution)/shard_map/all_to_all | solution.py:292
  283.2 0.0 copy-done.7
  283.2 0.1 copy.18
  283.3 12.5 %all-to-all-done.8.grams_ref = f32[32,16,128]{2,1,0:T(8,128)S(1)} async-done(((f32[32,16,128]{2,1,0:T(8,128)}), f32[32,16,128]{2,1,0:T(8,128)S(1)}, u32[]{:S(2)}, u32[]{:S(2)}) %all-to-all-start.8) | async-done | bytes 262176 | tf_op jit(solution)/shard_map/all_to_all | solution.py:292
  295.8 0.0 copy-done.2
  295.8 3.6 %finish.1 = (f32[16,4096]{1,0:T(8,128)}, f32[16,16]{1,0:T(8,128)}) custom-call(f32[32,16,128]{2,1,0:T(8,128)S(1)} %all-to-all-done.8.grams_ref, f32[3,3,16,128]{3,2,1,0:T(8,128)S(1)} %pad.4.turn_ref, f32[16,4096]{1,0:T(8,128)S(1)} %copy-done.2, f32[32,16,384]{2,1,0:T(8,128)S(1)} %bitcast.46, f32[32,16,384]{2,1,0:T(8,128)S(1)} %bitcast.43, ...), custom_call_target="tpu_custom_call" | custom-call | tf_op jit(solution)/shard_map/finish/pallas_call | solution.py:294
  (11 shorter events, 0.2 us)
Async XLA Ops:
  1.6 8.6 %collective-permute-start = (f32[2,16,128]{2,1,0:T(8,128)S(1)}, f32[2,16,128]{2,1,0:T(8,128)S(1)}, u32[]{:S(2)}, u32[]{:S(2)}) collective-permute-start(f32[2,16,128]{2,1,0:T(8,128)S(1)} %get-tuple-element.11), channel_id=1, source_target_pairs={{0,0},{1,16},{2,32},{3,48},{4,64},{5,80},{6,96},{7,112},{8,128},{9... | collective-permute-start | bytes 49160 | tf_op jit(solution)/shard_map/ppermute | solution.py:259
  11.1 40.3 %all-to-all-start = ((f32[32,2,16,128]{3,2,1,0:T(8,128)}), f32[32,2,16,128]{3,2,1,0:T(8,128)S(1)}, u32[]{:S(2)}, u32[]{:S(2)}) async-start(f32[32,2,16,128]{3,2,1,0:T(8,128)} %broadcast_in_dim.12), calls=%async_computation | async-start | bytes 1048576 | tf_op jit(solution)/shard_map/all_to_all | solution.py:260
  51.4 1.9 copy-start
  53.2 0.7 copy-start.3
  53.9 0.7 copy-start.5
  98.8 37.4 %copy-start.1 = (bf16[1,1,96,128,128]{4,3,2,1,0:T(8,128)(2,1)S(1)}, bf16[1,1,96,128,128]{4,3,2,1,0:T(8,128)(2,1)}, u32[]{:S(2)}) copy-start(bf16[1,1,96,128,128]{4,3,2,1,0:T(8,128)(2,1)} %param.6) | copy-start | bytes 9437188
  98.8 37.4 %copy-start.4 = (s32[1,1,96]{2,1,0:T(1,128)S(1)}, s32[1,1,96]{2,1,0:T(1,128)}, u32[]{:S(2)}) copy-start(s32[1,1,96]{2,1,0:T(1,128)} %param.7) | copy-start | bytes 1156
  98.9 37.4 %copy-start.6 = (s32[1,1,96]{2,1,0:T(1,128)S(1)}, s32[1,1,96]{2,1,0:T(1,128)}, u32[]{:S(2)}) copy-start(s32[1,1,96]{2,1,0:T(1,128)} %param.8) | copy-start | bytes 1156
  218.2 65.0 %copy-start.7 = (f32[3,3,16,16]{3,2,1,0:T(8,128)S(1)}, f32[3,3,16,16]{3,2,1,0:T(8,128)}, u32[]{:S(2)}) copy-start(f32[3,3,16,16]{3,2,1,0:T(8,128)} %param.11) | copy-start | bytes 27652
  218.2 77.7 %copy-start.2 = (f32[16,4096]{1,0:T(8,128)S(1)}, f32[16,4096]{1,0:T(8,128)}, u32[]{:S(2)}) copy-start(f32[16,4096]{1,0:T(8,128)} %start_ref.1) | copy-start | bytes 786436
  242.9 12.7 %all-to-all-start.6 = ((f32[16,2,16,128]{3,2,1,0:T(8,128)}), f32[16,2,16,128]{3,2,1,0:T(8,128)S(1)}, u32[]{:S(2)}, u32[]{:S(2)}) async-start(f32[16,2,16,128]{3,2,1,0:T(8,128)} %bitcast.11), calls=%async_computation.6 | async-start | bytes 524288 | tf_op jit(solution)/shard_map/all_to_all | solution.py:284
  248.4 7.3 %collective-permute-start.1 = (f32[2,16,128]{2,1,0:T(8,128)S(1)}, f32[2,16,128]{2,1,0:T(8,128)S(1)}, u32[]{:S(2)}, u32[]{:S(2)}) collective-permute-start(f32[2,16,128]{2,1,0:T(8,128)S(1)} %reduce_sum.27), channel_id=1, source_target_pairs={{0,0},{16,1},{32,2},{48,3},{64,4},{80,5},{96,6},{112,7},{128,8},{1... | collective-permute-start | bytes 49160 | tf_op jit(solution)/shard_map/ppermute | solution.py:283
  276.3 19.5 %all-to-all-start.8 = ((f32[32,16,128]{2,1,0:T(8,128)}), f32[32,16,128]{2,1,0:T(8,128)S(1)}, u32[]{:S(2)}, u32[]{:S(2)}) async-start(f32[32,16,128]{2,1,0:T(8,128)} %broadcast_in_dim.15), calls=%async_computation.8 | async-start | bytes 524288 | tf_op jit(solution)/shard_map/all_to_all | solution.py:292

commit v3 on v2

v3 whole, which is shorter than its diff:
```python
import functools

import jax
import jax.numpy as jnp
from jax import lax
from jax.experimental import pallas as pl
from jax.experimental.pallas import tpu as pltpu
from jax.sharding import PartitionSpec as P

ITERS = 3
LANE = 128
GROUP = 8
BOTH = ("row", "col")
HIGH = lax.Precision.HIGHEST
NT = (((1,), (1,)), ((), ()))
NN = (((1,), (0,)), ((), ()))
SMEM = pl.BlockSpec(memory_space=pltpu.SMEM)
VMEM = pl.BlockSpec(memory_space=pltpu.VMEM)


def kernel_call(kernel, name, out, ins, scratch=()):
    return pl.pallas_call(
        kernel,
        name=name,
        out_shape=out,
        in_specs=ins,
        out_specs=jax.tree.map(lambda _: VMEM, out),
        scratch_shapes=scratch,
        compiler_params=pltpu.CompilerParams(vmem_limit_bytes=48 << 20),
    )


def f32(*shape):
    return jax.ShapeDtypeStruct(shape, jnp.float32)


def multiply(get_seg, get_block, index_ref, tiles_ref, refs, split, total):
    seg_tiles = total.shape[0] // 3
    vecs = total.shape[1]

    def keep(slot, values):
        high = values.astype(jnp.bfloat16)
        split[slot, 0:vecs, :] = high
        split[slot, vecs : 2 * vecs, :] = (values - high.astype(jnp.float32)).astype(jnp.bfloat16)

    for t in range(seg_tiles):
        keep(t, get_seg(refs, t))
        for half in range(2):
            keep(seg_tiles * (1 + half) + t, get_block(refs, t, half))
    total[...] = jnp.zeros_like(total)
    slots = tiles_ref.shape[0]
    count = index_ref[2 * slots]

    def group(g, carry):
        parts = []
        for j in range(GROUP):
            slot = g * GROUP + j
            row = index_ref[slot]
            col = index_ref[slots + slot] + seg_tiles
            tile = tiles_ref[slot]
            direct = lax.dot_general(split[col], tile, NT, preferred_element_type=jnp.float32)
            mirror = lax.dot_general(split[row], tile, NN, preferred_element_type=jnp.float32)
            live = slot < count
            parts.append((row, jnp.where(live, direct[:vecs] + direct[vecs:], 0.0)))
            parts.append((col, jnp.where(live, mirror[:vecs] + mirror[vecs:], 0.0)))
        for place, part in parts:
            total[place] += part
        return carry

    lax.fori_loop(0, (count + (GROUP - 1)) // GROUP, group, 0)


def line(t, vecs, part):
    return pl.ds(t * vecs * 3 + part, vecs, stride=3)


def lay_out(total, out_ref):
    seg_tiles, vecs = total.shape[0] // 3, total.shape[1]
    for t in range(seg_tiles):
        for part in range(3):
            out_ref[line(t, vecs, part), :] = total[part * seg_tiles + t]


def multiply_first(index_ref, tiles_ref, seg_ref, block_ref, out_ref, split, total):
    seg_tiles = seg_ref.shape[1] // LANE
    multiply(
        lambda refs, t: refs[0][:, t * LANE : (t + 1) * LANE],
        lambda refs, t, half: refs[1][(half * seg_tiles + t) // 2, :, (t % 2) * LANE : (t % 2 + 1) * LANE],
        index_ref, tiles_ref, (seg_ref, block_ref), split, total,
    )
    lay_out(total, out_ref)


def multiply_next(index_ref, tiles_ref, all_ref, out_ref, split, total):
    vecs = total.shape[1]
    multiply(
        lambda refs, t: refs[0][line(t, vecs, 0), :],
        lambda refs, t, half: refs[0][line(t, vecs, 1 + half), :],
        index_ref, tiles_ref, (all_ref,), split, total,
    )
    lay_out(total, out_ref)


def multiply_last(index_ref, tiles_ref, all_ref, direct_ref, mirror_ref, split, total):
    vecs = total.shape[1]
    multiply(
        lambda refs, t: refs[0][line(t, vecs, 0), :],
        lambda refs, t, half: refs[0][line(t, vecs, 1 + half), :],
        index_ref, tiles_ref, (all_ref,), split, total,
    )
    for refs, base in ((direct_ref, 0), (mirror_ref, total.shape[0] // 3)):
        for t in range(2 * refs.shape[0]):
            refs[t // 2, :, (t % 2) * LANE : (t % 2 + 1) * LANE] = total[base + t]


def sum_and_deal(rows, cols, got_ref, out_ref, sums):
    for r in range(rows):
        half = r % 2
        sums[r // 2 : r // 2 + 1, half * LANE : (half + 1) * LANE] = jnp.sum(
            got_ref[line(r, cols, 0), :], axis=0, keepdims=True
        )
    for half in range(2):
        mirror = got_ref[line(0, cols, 1 + half), :]
        for r in range(1, rows):
            mirror = mirror + got_ref[line(r, cols, 1 + half), :]
        lanes = slice(half * LANE, (half + 1) * LANE)
        sums[:, lanes] = sums[:, lanes] + mirror
    for r in range(rows):
        half = r % 2
        out_ref[line(r, cols, 0), :] = jnp.broadcast_to(
            sums[r // 2 : r // 2 + 1, half * LANE : (half + 1) * LANE], (cols, LANE)
        )
        for half in range(2):
            out_ref[line(r, cols, 1 + half), :] = sums[:, half * LANE : (half + 1) * LANE]


def gram(own_ref, three_ref, gram_ref):
    vecs = three_ref.shape[0]
    basis = [own_ref[j] for j in range(ITERS)] + [three_ref[...]]
    parts = []
    for j in range(2 * ITERS + 1):
        parts.append(
            lax.dot_general(
                basis[j // 2], basis[(j + 1) // 2], NT, precision=HIGH, preferred_element_type=jnp.float32
            )
        )
    parts.append(jnp.zeros((vecs, LANE - (2 * ITERS + 1) * vecs), jnp.float32))
    gram_ref[...] = jnp.concatenate(parts, axis=1)


def finish(states, grams_ref, turn_ref, start_ref, one_ref, two_ref, three_ref, eigen_ref, ritz_ref):
    vecs = eigen_ref.shape[0]

    def mul(a, b, dims=NN):
        full = jnp.concatenate([b, jnp.zeros((LANE - b.shape[0], b.shape[1]), jnp.float32)], axis=0)
        return lax.dot_general(a, full, dims, precision=HIGH, preferred_element_type=jnp.float32)

    moments = grams_ref[0]
    for r in range(1, grams_ref.shape[0]):
        moments = moments + grams_ref[r]
    moments = moments * (1.0 / states)
    hankel = jnp.concatenate(
        [moments] + [pltpu.roll(moments, LANE - j * vecs, 1) for j in range(1, ITERS)], axis=0
    )
    eye = lax.broadcasted_iota(jnp.int32, (vecs, LANE), 0) == lax.broadcasted_iota(jnp.int32, (vecs, LANE), 1)
    iterate = eye.astype(jnp.float32)
    search = None
    for i in range(ITERS):
        keep, step, past = (turn_ref[i, j] for j in range(3))
        weighted = mul(iterate, hankel) if i else moments
        own = mul(weighted, iterate, NT)
        theta = mul(pltpu.roll(weighted, LANE - vecs, 1), iterate, NT)
        images = mul(pltpu.roll(weighted, LANE - 2 * vecs, 1), iterate, NT)
        terms = jnp.where(eye, images, 0.0) - 2.0 * theta * theta + theta * mul(own, theta)
        spread = jnp.maximum(jnp.sum(terms, axis=0, keepdims=True), 0.0)
        scaled = step / jnp.sqrt(spread + 1e-06)
        residual = pltpu.roll(iterate, vecs, 1) - mul(theta, iterate)
        moved = mul(scaled, residual)
        if search is not None:
            moved = moved - mul(-past, search)
        iterate = moved - mul(-keep, iterate)
        search = moved
    ritz_ref[...] = theta[:, :vecs]
    for t in range(eigen_ref.shape[1] // LANE):
        lanes = slice(t * LANE, (t + 1) * LANE)
        own = slice((t % 2) * LANE, (t % 2 + 1) * LANE)
        basis = [start_ref[:, lanes], one_ref[line(t, vecs, 0), :], two_ref[line(t, vecs, 0), :]]
        basis.append(three_ref[t // 2, :, own])
        eigen_ref[:, lanes] = mul(iterate, jnp.concatenate(basis, axis=0))


def body(tiles, tile_row, tile_col, tile_counts, start, rotation):
    tiles = tiles.reshape(tiles.shape[2:])
    slots = tiles.shape[0]
    vecs, seg_rows = start.shape
    rows = lax.axis_size("row")
    cols = lax.axis_size("col")
    seg_tiles = seg_rows // LANE
    pair = 2 * LANE
    index = jnp.concatenate([tile_row.reshape(slots), tile_col.reshape(slots), tile_counts.reshape(1)])
    own_col = lax.axis_index("col")
    dealt = f32(rows * cols * 3, LANE)
    work = [
        pltpu.VMEM((3 * seg_tiles, 2 * vecs, LANE), jnp.bfloat16),
        pltpu.VMEM((3 * seg_tiles, vecs, LANE), jnp.float32),
    ]
    sums = [pltpu.VMEM((cols, pair), jnp.float32)]
    corner = []
    for r in range(rows):
        for c in range(cols):
            corner.append((r * cols + c, ((r % 2) * cols + c) * cols + r // 2))

    def swap(x):
        moved = lax.all_to_all(x.reshape(rows * cols, 3 * LANE), BOTH, 0, 0)
        return moved.reshape(rows * cols * 3, LANE)

    def own_tiles(x):
        x = lax.dynamic_slice_in_dim(x, own_col * (2 * vecs * 3), 2 * vecs * 3, 0).reshape(2, vecs, 3, LANE)
        return jnp.concatenate([x[0, :, 0], x[1, :, 0]], axis=1)

    def to_all(x, axis):
        count = lax.axis_size(axis)
        return lax.all_to_all(jnp.broadcast_to(x, (count,) + x.shape), axis, 0, 0)

    own_start = lax.dynamic_slice_in_dim(start, own_col * pair, pair, 1)
    index, piece = lax.optimization_barrier((index, lax.ppermute(own_start, BOTH, corner)))
    block = to_all(piece, "row")
    sent = kernel_call(multiply_first, "multiply_first", dealt, [SMEM] + [VMEM] * 3, work)(
        index, tiles, start, block
    )
    images = []
    for i in range(ITERS - 1):
        add = functools.partial(sum_and_deal, rows, cols)
        images.append(swap(kernel_call(add, "sum_and_deal", dealt, [VMEM], sums)(swap(sent))))
        if i < ITERS - 2:
            sent = kernel_call(multiply_next, "multiply_next", dealt, [SMEM] + [VMEM] * 2, work)(
                index, tiles, images[-1]
            )
    direct, mirror = kernel_call(
        multiply_last,
        "multiply_last",
        (f32(cols, vecs, pair), f32(rows, vecs, pair)),
        [SMEM] + [VMEM] * 2,
        work,
    )(index, tiles, images[-1])

    mirror = jnp.sum(lax.all_to_all(mirror, "row", 0, 0), axis=0)
    direct, mirror = lax.optimization_barrier((direct, mirror))
    turned_back = lax.ppermute(mirror, BOTH, [(to, at) for at, to in corner])
    last_piece = jnp.sum(lax.all_to_all(direct, "col", 0, 0), axis=0) + turned_back
    own = jnp.stack([own_start] + [own_tiles(image) for image in images])
    grams = kernel_call(gram, "gram", f32(vecs, LANE), [VMEM] * 2)(own, last_piece)
    grams = jnp.sum(to_all(grams, "row"), axis=0)
    last, grams = lax.optimization_barrier((lax.all_gather(last_piece, "col"), grams))
    grams = to_all(grams, "col")
    turned = jnp.pad(jnp.swapaxes(rotation, 2, 3), ((0, 0),) * 3 + ((0, LANE - vecs),))
    return kernel_call(
        functools.partial(finish, seg_rows * rows),
        "finish",
        (f32(vecs, seg_rows), f32(vecs, vecs)),
        [VMEM] * 6,
    )(grams, turned, start, *images, last)


def solution(mesh):
    return jax.shard_map(
        body,
        mesh=mesh,
        in_specs=(
            P("row", "col", None, None, None),
            P("row", "col", None),
            P("row", "col", None),
            P("row", "col"),
            P(None, "row"),
            P(),
        ),
        out_specs=(P(None, "row"), P()),
        check_vma=False,
    )
```

time: 301 us -> 298 us (0.990)
  blocking collectives: 195 us -> 214 us
  waiting for transfers between devices: 35.6 us -> 27.5 us
  starting transfers between devices: 44.7 us -> 38.9 us
  local copies, waits for them, and re-layouts: 9.39 us -> 5.22 us
  Pallas kernels: 13.1 us -> 9.2 us
    all_gather x0 -> x1, blocking collectives: none -> 21.7 us  [body(): lax.all_gather(last_piece, 'col')]
    all_to_all x3 -> x4, waiting for transfers between devices: 32.3 us -> 25.6 us  [the longest x1 15.9 us: body(): mirror = jnp.sum(lax.all_to_all(mirror, 'row', 0, 0), axis=0)]
    all_to_all x3 -> x4, starting transfers between devices: 35.5 us -> 30 us  [the longest x2 14.7 us: to_all(): return lax.all_to_all(jnp.broadcast_to(x, (count,) + x.shape), axis, 0, 0)]
    pallas_call x5, Pallas kernels: 9.2 us -> 5.3 us  [the longest x1 2.25 us: body(): kernel_call(multiply_last, 'multiply_last', (f32(cols, vecs, pair), f32(r...]
    all_to_all x4 -> x0, local copies, waits for them, and re-layouts: 3.24 us -> none  [swap(): moved = lax.all_to_all(x.reshape(rows * cols, width), BOTH, 0, 0)]
    all_to_all x6 -> x5, blocking collectives: 195 us -> 193 us  [the longest x4 153 us: swap(): moved = lax.all_to_all(x.reshape(rows * cols, 3 * LANE), BOTH, 0, 0)]
  transfers between devices with their start and end apart: 5 -> 6, of which waited for: 4 -> 4; matrix products, arithmetic and copies ran while one was open for 0% -> 0% of each run, Pallas kernels for 0% -> 0%
where the time goes in v3:
time: 298 us; the launch traced here: 297 us
  blocking collectives  214 us (72%)
  starting transfers between devices  38.9 us (13%)
  waiting for transfers between devices  27.5 us (9%)
  Pallas kernels  9.2 us (3%)
  local copies, waits for them, and re-layouts  5.22 us (2%)
    all_to_all x4, blocking collectives, swap(): moved = lax.all_to_all(x.reshape(rows * cols, 3 * LANE), BOTH, 0, 0)  153 us
    all_to_all x1, blocking collectives, to_all(): return lax.all_to_all(jnp.broadcast_to(x, (count,) + x.shape), axis, 0, 0)  40 us
    all_gather x1, blocking collectives, body(): lax.all_gather(last_piece, 'col')  21.7 us
    all_to_all x1, waiting for transfers between devices, body(): mirror = jnp.sum(lax.all_to_all(mirror, 'row', 0, 0), axis=0)  15.9 us
    all_to_all x2, starting transfers between devices, to_all(): return lax.all_to_all(jnp.broadcast_to(x, (count,) + x.shape), axis, 0, 0)  14.7 us
    all_to_all x1, starting transfers between devices, body(): lax.all_to_all(direct, 'col', 0, 0)  7.79 us
    all_to_all x1, starting transfers between devices, body(): mirror = jnp.sum(lax.all_to_all(mirror, 'row', 0, 0), axis=0)  7.5 us
    all_to_all x2, waiting for transfers between devices, to_all(): return lax.all_to_all(jnp.broadcast_to(x, (count,) + x.shape), axis, 0, 0)  6.12 us
  transfers between devices with their start and end apart: 6, of which 4 were waited for; matrix products, arithmetic and copies ran while one was open for 0% of the time, Pallas kernels for 0%

profile of v3, /device:TPU:1, one launch (start us, length us, event | category | flops | bytes accessed | tf_op | source)
XLA Modules:
  0.0 297.4 jit_solution(10776632793903895726)
XLA Ops:
  0.6 0.7 constant_dynamic-slice_fusion.2
  1.4 5.4 %collective-permute-start = (f32[16,256]{1,0:T(8,128)S(1)}, f32[16,256]{1,0:T(8,128)S(1)}, u32[]{:S(2)}, u32[]{:S(2)}) collective-permute-start(f32[16,256]{1,0:T(8,128)S(1)} %constant_dynamic-slice_fusion.2), channel_id=1, source_target_pairs={{0,0},{1,16},{2,32},{3,48},{4,64},{5,80},{6,96},{7,112},{8,128},{9... | collective-permute-start | bytes 49160 | tf_op jit(solution)/shard_map/ppermute | solution.py:226
  7.4 0.7 pad_add_fusion.index_ref
  8.1 1.8 collective-permute-done
  10.0 40.0 %all_to_all.61.block_ref = f32[32,16,256]{2,1,0:T(8,128)S(1)} all-to-all(f32[32,16,256]{2,1,0:T(8,128)S(1)} %broadcast_in_dim.9), channel_id=1, replica_groups=mesh['row'=32,'col'=16] {'row'}, dimensions={0} | all-to-all | bytes 1048576 | tf_op jit(solution)/shard_map/all_to_all | solution.py:223
  50.1 0.0 copy-start
  50.1 1.9 copy-done
  52.0 0.0 copy-start.2
  52.0 0.9 copy-done.2
  52.9 1.4 multiply_first.1
  54.3 0.0 copy-start.1
  54.3 41.0 %all_to_all.62 = f32[512,1,384]{2,1,0:T(1,128)S(1)} all-to-all(f32[512,1,384]{2,1,0:T(1,128)S(1)} %bitcast.42), channel_id=1, replica_groups=mesh['row'=32,'col'=16] {'row','col'}, dimensions={0} | all-to-all | bytes 1572864 | tf_op jit(solution)/shard_map/all_to_all | solution.py:214
  95.4 0.1 sum_and_deal.2
  95.5 36.3 %all_to_all.63 = f32[512,1,384]{2,1,0:T(1,128)S(1)} all-to-all(f32[512,1,384]{2,1,0:T(1,128)S(1)} %bitcast.45), channel_id=1, replica_groups=mesh['row'=32,'col'=16] {'row','col'}, dimensions={0} | all-to-all | bytes 1572864 | tf_op jit(solution)/shard_map/all_to_all | solution.py:214
  131.8 0.0 copy-done.1
  131.8 1.4 multiply_next.1
  133.3 38.5 %all_to_all.64 = f32[512,1,384]{2,1,0:T(1,128)S(1)} all-to-all(f32[512,1,384]{2,1,0:T(1,128)S(1)} %bitcast.43), channel_id=1, replica_groups=mesh['row'=32,'col'=16] {'row','col'}, dimensions={0} | all-to-all | bytes 1572864 | tf_op jit(solution)/shard_map/all_to_all | solution.py:214
  171.8 0.1 sum_and_deal.3
  171.9 0.0 copy-start.3
  171.9 36.7 %all_to_all.65 = f32[512,1,384]{2,1,0:T(1,128)S(1)} all-to-all(f32[512,1,384]{2,1,0:T(1,128)S(1)} %bitcast.47), channel_id=1, replica_groups=mesh['row'=32,'col'=16] {'row','col'}, dimensions={0} | all-to-all | bytes 1572864 | tf_op jit(solution)/shard_map/all_to_all | solution.py:214
  208.6 2.3 multiply_last.1
  210.8 0.0 copy-start.4
  210.8 7.5 %all-to-all-start.5 = ((f32[32,16,256]{2,1,0:T(8,128)}), f32[32,16,256]{2,1,0:T(8,128)S(1)}, u32[]{:S(2)}, u32[]{:S(2)}) async-start(f32[32,16,256]{2,1,0:T(8,128)} %get-tuple-element.13), calls=%async_computation.5 | async-start | bytes 1048576 | tf_op jit(solution)/shard_map/all_to_all | solution.py:247
  218.3 0.0 copy-done.3
  218.4 15.9 %all-to-all-done.5 = f32[32,16,256]{2,1,0:T(8,128)S(1)} async-done(((f32[32,16,256]{2,1,0:T(8,128)}), f32[32,16,256]{2,1,0:T(8,128)S(1)}, u32[]{:S(2)}, u32[]{:S(2)}) %all-to-all-start.5) | async-done | bytes 524320 | tf_op jit(solution)/shard_map/all_to_all | solution.py:247
  234.4 7.8 %all-to-all-start.6 = ((f32[16,16,256]{2,1,0:T(8,128)}), f32[16,16,256]{2,1,0:T(8,128)S(1)}, u32[]{:S(2)}, u32[]{:S(2)}) async-start(f32[16,16,256]{2,1,0:T(8,128)} %get-tuple-element.14), calls=%async_computation.6 | async-start | bytes 524288 | tf_op jit(solution)/shard_map/all_to_all | solution.py:250
  242.3 3.5 %collective-permute-start.1 = (f32[16,256]{1,0:T(8,128)S(1)}, f32[16,256]{1,0:T(8,128)S(1)}, u32[]{:S(2)}, u32[]{:S(2)}) collective-permute-start(f32[16,256]{1,0:T(8,128)S(1)} %reduce_sum.27), channel_id=1, source_target_pairs={{0,0},{16,1},{32,2},{48,3},{64,4},{80,5},{96,6},{112,7},{128,8},{1... | collective-permute-start | bytes 49160 | tf_op jit(solution)/shard_map/ppermute | solution.py:249
  245.8 3.6 %all-to-all-done.6 = f32[16,16,256]{2,1,0:T(8,128)S(1)} async-done(((f32[16,16,256]{2,1,0:T(8,128)}), f32[16,16,256]{2,1,0:T(8,128)S(1)}, u32[]{:S(2)}, u32[]{:S(2)}) %all-to-all-start.6) | async-done | bytes 262176 | tf_op jit(solution)/shard_map/all_to_all | solution.py:250
  249.4 0.0 collective-permute-done.1
  249.4 0.3 gram.1
  249.7 0.7 broadcast_in_dim.10
  250.5 11.3 %all-to-all-start.7 = ((f32[32,16,128]{2,1,0:T(8,128)}), f32[32,16,128]{2,1,0:T(8,128)S(1)}, u32[]{:S(2)}, u32[]{:S(2)}) async-start(f32[32,16,128]{2,1,0:T(8,128)} %broadcast_in_dim.10), calls=%async_computation.7 | async-start | bytes 524288 | tf_op jit(solution)/shard_map/all_to_all | solution.py:223
  261.8 21.7 %all-gather = f32[256,256]{1,0:T(8,128)S(1)} all-gather(f32[16,256]{1,0:T(8,128)S(1)} %add.13.three_ref), channel_id=2, replica_groups=mesh['row'=32,'col'=16] {'col'}, dimensions={0}, use_global_device_ids=true | all-gather | bytes 278528 | tf_op jit(solution)/shard_map/all_gather | solution.py:254
  283.4 0.0 all-to-all-done.7
  283.5 0.7 broadcast_in_dim.11
  284.1 3.5 %all-to-all-start.8 = ((f32[16,16,128]{2,1,0:T(8,128)}), f32[16,16,128]{2,1,0:T(8,128)S(1)}, u32[]{:S(2)}, u32[]{:S(2)}) async-start(f32[16,16,128]{2,1,0:T(8,128)} %broadcast_in_dim.11), calls=%async_computation.8 | async-start | bytes 262144 | tf_op jit(solution)/shard_map/all_to_all | solution.py:223
  287.6 0.0 copy-done.4
  287.6 0.1 copy.31
  287.7 6.1 %all-to-all-done.8.grams_ref = f32[16,16,128]{2,1,0:T(8,128)S(1)} async-done(((f32[16,16,128]{2,1,0:T(8,128)}), f32[16,16,128]{2,1,0:T(8,128)S(1)}, u32[]{:S(2)}, u32[]{:S(2)}) %all-to-all-start.8) | async-done | bytes 131104 | tf_op jit(solution)/shard_map/all_to_all | solution.py:223
  293.8 3.6 %finish.1 = (f32[16,4096]{1,0:T(8,128)}, f32[16,16]{1,0:T(8,128)}) custom-call(f32[16,16,128]{2,1,0:T(8,128)S(1)} %all-to-all-done.8.grams_ref, f32[3,3,16,128]{3,2,1,0:T(8,128)S(1)} %pad.4.turn_ref, f32[16,4096]{1,0:T(8,128)S(1)} %copy-done.3, f32[1536,128]{1,0:T(8,128)S(1)} %bitcast.38, f32[1536,128]{1,0:T(8,128)S(1)} %bitcast.41, f32[16,16,256]{2,1,0:T(8,128)S(1)} %bitcast.48), custom_call_target="tpu_custom_call" | custom-call | tf_op jit(solution)/shard_map/finish/pallas_call | solution.py:257
  (15 shorter events, 0.3 us)
Async XLA Ops:
  1.4 8.6 %collective-permute-start = (f32[16,256]{1,0:T(8,128)S(1)}, f32[16,256]{1,0:T(8,128)S(1)}, u32[]{:S(2)}, u32[]{:S(2)}) collective-permute-start(f32[16,256]{1,0:T(8,128)S(1)} %constant_dynamic-slice_fusion.2), channel_id=1, source_target_pairs={{0,0},{1,16},{2,32},{3,48},{4,64},{5,80},{6,96},{7,112},{8,128},{9... | collective-permute-start | bytes 49160 | tf_op jit(solution)/shard_map/ppermute | solution.py:226
  50.1 1.9 copy-start
  52.0 0.9 copy-start.2
  54.3 77.5 %copy-start.1 = (bf16[1,1,96,128,128]{4,3,2,1,0:T(8,128)(2,1)S(1)}, bf16[1,1,96,128,128]{4,3,2,1,0:T(8,128)(2,1)}, u32[]{:S(2)}) copy-start(bf16[1,1,96,128,128]{4,3,2,1,0:T(8,128)(2,1)} %param.6) | copy-start | bytes 9437188
  171.9 46.4 %copy-start.3 = (f32[16,4096]{1,0:T(8,128)S(1)}, f32[16,4096]{1,0:T(8,128)}, u32[]{:S(2)}) copy-start(f32[16,4096]{1,0:T(8,128)} %start_ref.1) | copy-start | bytes 786436
  210.8 76.8 %copy-start.4 = (f32[3,3,16,16]{3,2,1,0:T(8,128)S(1)}, f32[3,3,16,16]{3,2,1,0:T(8,128)}, u32[]{:S(2)}) copy-start(f32[3,3,16,16]{3,2,1,0:T(8,128)} %param.11) | copy-start | bytes 27652
  210.8 23.5 %all-to-all-start.5 = ((f32[32,16,256]{2,1,0:T(8,128)}), f32[32,16,256]{2,1,0:T(8,128)S(1)}, u32[]{:S(2)}, u32[]{:S(2)}) async-start(f32[32,16,256]{2,1,0:T(8,128)} %get-tuple-element.13), calls=%async_computation.5 | async-start | bytes 1048576 | tf_op jit(solution)/shard_map/all_to_all | solution.py:247
  234.4 15.0 %all-to-all-start.6 = ((f32[16,16,256]{2,1,0:T(8,128)}), f32[16,16,256]{2,1,0:T(8,128)S(1)}, u32[]{:S(2)}, u32[]{:S(2)}) async-start(f32[16,16,256]{2,1,0:T(8,128)} %get-tuple-element.14), calls=%async_computation.6 | async-start | bytes 524288 | tf_op jit(solution)/shard_map/all_to_all | solution.py:250
  242.3 7.1 %collective-permute-start.1 = (f32[16,256]{1,0:T(8,128)S(1)}, f32[16,256]{1,0:T(8,128)S(1)}, u32[]{:S(2)}, u32[]{:S(2)}) collective-permute-start(f32[16,256]{1,0:T(8,128)S(1)} %reduce_sum.27), channel_id=1, source_target_pairs={{0,0},{16,1},{32,2},{48,3},{64,4},{80,5},{96,6},{112,7},{128,8},{1... | collective-permute-start | bytes 49160 | tf_op jit(solution)/shard_map/ppermute | solution.py:249
  250.5 33.0 %all-to-all-start.7 = ((f32[32,16,128]{2,1,0:T(8,128)}), f32[32,16,128]{2,1,0:T(8,128)S(1)}, u32[]{:S(2)}, u32[]{:S(2)}) async-start(f32[32,16,128]{2,1,0:T(8,128)} %broadcast_in_dim.10), calls=%async_computation.7 | async-start | bytes 524288 | tf_op jit(solution)/shard_map/all_to_all | solution.py:223
  284.1 9.7 %all-to-all-start.8 = ((f32[16,16,128]{2,1,0:T(8,128)}), f32[16,16,128]{2,1,0:T(8,128)S(1)}, u32[]{:S(2)}, u32[]{:S(2)}) async-start(f32[16,16,128]{2,1,0:T(8,128)} %broadcast_in_dim.11), calls=%async_computation.8 | async-start | bytes 262144 | tf_op jit(solution)/shard_map/all_to_all | solution.py:223

commit v4 on v3

v4 whole, which is shorter than its diff:
```python
import functools

import jax
import jax.numpy as jnp
from jax import lax
from jax.experimental import pallas as pl
from jax.experimental.pallas import tpu as pltpu
from jax.sharding import PartitionSpec as P

ITERS = 3
LANE = 128
GROUP = 32
BOTH = ("row", "col")
HIGH = lax.Precision.HIGHEST
NT = (((1,), (1,)), ((), ()))
NN = (((1,), (0,)), ((), ()))
SMEM = pl.BlockSpec(memory_space=pltpu.SMEM)
VMEM = pl.BlockSpec(memory_space=pltpu.VMEM)


def kernel_call(kernel, name, out, ins, scratch=()):
    return pl.pallas_call(
        kernel,
        name=name,
        out_shape=out,
        in_specs=ins,
        out_specs=jax.tree.map(lambda _: VMEM, out),
        scratch_shapes=scratch,
        compiler_params=pltpu.CompilerParams(vmem_limit_bytes=16 << 20),
    )


def f32(*shape):
    return jax.ShapeDtypeStruct(shape, jnp.float32)


def line(t, vecs, part):
    return pl.ds(t * vecs * 3 + part, vecs, stride=3)


def keep(split, slot, values):
    vecs = values.shape[0]
    high = values.astype(jnp.bfloat16)
    split[slot, 0:vecs, :] = high
    split[slot, vecs : 2 * vecs, :] = (values - high.astype(jnp.float32)).astype(jnp.bfloat16)


def multiply(index_ref, tiles_ref, split, total, direct, mirror):
    seg_tiles = total.shape[0] // 3
    vecs = total.shape[1]
    slots = tiles_ref.shape[0]
    count = index_ref[2 * slots]
    size = GROUP if slots % GROUP == 0 else slots
    total[...] = jnp.zeros_like(total)

    def group(g, carry):
        parts = []
        for j in range(size):
            slot = g * size + j
            row = index_ref[slot]
            col = index_ref[slots + slot] + seg_tiles
            tile = tiles_ref[slot]
            live = slot < count
            for wanted, taken, place, dims in ((direct, col, row, NT), (mirror, row, col, NN)):
                if wanted:
                    part = lax.dot_general(split[taken], tile, dims, preferred_element_type=jnp.float32)
                    parts.append((place, jnp.where(live, part[:vecs] + part[vecs:], 0.0)))
        for place, part in parts:
            total[place] += part
        return carry

    lax.fori_loop(0, (count + (size - 1)) // size, group, 0)


def first_mirror(index_ref, tiles_ref, seg_ref, out_ref, split, total):
    seg_tiles = total.shape[0] // 3
    for t in range(seg_tiles):
        keep(split, t, seg_ref[:, t * LANE : (t + 1) * LANE])
    multiply(index_ref, tiles_ref, split, total, False, True)
    out_ref[...] = total[seg_tiles : 3 * seg_tiles]


def first_direct(index_ref, tiles_ref, block_ref, mirrored_ref, out_ref, split, total):
    seg_tiles, vecs = total.shape[0] // 3, total.shape[1]
    for t in range(2 * seg_tiles):
        keep(split, seg_tiles + t, block_ref[t // 2, :, (t % 2) * LANE : (t % 2 + 1) * LANE])
    multiply(index_ref, tiles_ref, split, total, True, False)
    for t in range(seg_tiles):
        out_ref[line(t, vecs, 0), :] = total[t]
        for half in range(2):
            out_ref[line(t, vecs, 1 + half), :] = mirrored_ref[half * seg_tiles + t]


def multiply_next(index_ref, tiles_ref, all_ref, out_ref, split, total):
    seg_tiles, vecs = total.shape[0] // 3, total.shape[1]
    for t in range(seg_tiles):
        for part in range(3):
            keep(split, part * seg_tiles + t, all_ref[line(t, vecs, part), :])
    multiply(index_ref, tiles_ref, split, total, True, True)
    for t in range(seg_tiles):
        for part in range(3):
            out_ref[line(t, vecs, part), :] = total[part * seg_tiles + t]


def add_up(rows, cols, got_ref, sums):
    for r in range(rows):
        half = r % 2
        sums[r // 2 : r // 2 + 1, half * LANE : (half + 1) * LANE] = jnp.sum(
            got_ref[line(r, cols, 0), :], axis=0, keepdims=True
        )
    for half in range(2):
        mirror = got_ref[line(0, cols, 1 + half), :]
        for r in range(1, rows):
            mirror = mirror + got_ref[line(r, cols, 1 + half), :]
        lanes = slice(half * LANE, (half + 1) * LANE)
        sums[:, lanes] = sums[:, lanes] + mirror


def sum_and_deal(rows, cols, got_ref, out_ref, own_ref, sums):
    add_up(rows, cols, got_ref, sums)
    for half in range(2):
        own_ref[pl.ds(half, cols, stride=2), :] = sums[:, half * LANE : (half + 1) * LANE]
    for r in range(rows):
        half = r % 2
        out_ref[line(r, cols, 0), :] = jnp.broadcast_to(
            sums[r // 2 : r // 2 + 1, half * LANE : (half + 1) * LANE], (cols, LANE)
        )
        for half in range(2):
            out_ref[line(r, cols, 1 + half), :] = sums[:, half * LANE : (half + 1) * LANE]


def sum_and_show(rows, cols, got_ref, two_ref, out_ref, sums):
    add_up(rows, cols, got_ref, sums)
    for c in range(cols):
        out_ref[c, 0:rows, :] = two_ref[...]
        for half in range(2):
            out_ref[c, pl.ds(rows + half, cols, stride=2), :] = sums[:, half * LANE : (half + 1) * LANE]


def dots(a, b):
    return lax.dot_general(a, b, NT, precision=HIGH, preferred_element_type=jnp.float32)


def gram_known(start_ref, one_ref, two_ref, gram_ref, basis):
    vecs = start_ref.shape[0]
    for t in range(start_ref.shape[1] // LANE):
        lanes = slice(t * LANE, (t + 1) * LANE)
        basis[0:vecs, lanes] = one_ref[line(t, vecs, 0), :]
        basis[vecs : 2 * vecs, lanes] = two_ref[line(t, vecs, 0), :]
    held = [start_ref[...], basis[0:vecs, :], basis[vecs : 2 * vecs, :]]
    parts = [dots(held[j // 2], held[(j + 1) // 2]) for j in range(2 * ITERS - 1)]
    parts.append(jnp.zeros((vecs, LANE - (2 * ITERS - 1) * vecs), jnp.float32))
    gram_ref[...] = jnp.concatenate(parts, axis=1)


def gram_last(rows, known_ref, shown_ref, out_ref, basis):
    vecs = known_ref.shape[0]
    for s in range(rows):
        lanes = slice(s * LANE, (s + 1) * LANE)
        basis[0:vecs, lanes] = shown_ref[pl.ds(s, vecs, stride=2 * rows), :]
        three = shown_ref[pl.ds(rows + s, vecs, stride=2 * rows), :]
        basis[vecs : 2 * vecs, lanes] = three
        out_ref[s, 0] = three
    two, three = basis[0:vecs, :], basis[vecs : 2 * vecs, :]
    width = (2 * ITERS - 1) * vecs
    parts = [known_ref[...][:, :width], dots(two, three), dots(three, three)]
    parts.append(jnp.zeros((vecs, LANE - (2 * ITERS + 1) * vecs), jnp.float32))
    grams = jnp.concatenate(parts, axis=1)
    for s in range(rows):
        out_ref[s, 1] = grams


def finish(states, last_ref, turn_ref, start_ref, one_ref, two_ref, eigen_ref, ritz_ref):
    vecs = eigen_ref.shape[0]

    def mul(a, b, dims=NN):
        full = jnp.concatenate([b, jnp.zeros((LANE - b.shape[0], b.shape[1]), jnp.float32)], axis=0)
        return lax.dot_general(a, full, dims, precision=HIGH, preferred_element_type=jnp.float32)

    moments = last_ref[0, 1]
    for r in range(1, last_ref.shape[0]):
        moments = moments + last_ref[r, 1]
    moments = moments * (1.0 / states)
    hankel = jnp.concatenate(
        [moments] + [pltpu.roll(moments, LANE - j * vecs, 1) for j in range(1, ITERS)], axis=0
    )
    eye = lax.broadcasted_iota(jnp.int32, (vecs, LANE), 0) == lax.broadcasted_iota(jnp.int32, (vecs, LANE), 1)
    iterate = eye.astype(jnp.float32)
    search = None
    for i in range(ITERS):
        keep_turn, step, past = (turn_ref[i, j] for j in range(3))
        weighted = mul(iterate, hankel) if i else moments
        own = mul(weighted, iterate, NT)
        theta = mul(pltpu.roll(weighted, LANE - vecs, 1), iterate, NT)
        images = mul(pltpu.roll(weighted, LANE - 2 * vecs, 1), iterate, NT)
        terms = jnp.where(eye, images, 0.0) - 2.0 * theta * theta + theta * mul(own, theta)
        spread = jnp.maximum(jnp.sum(terms, axis=0, keepdims=True), 0.0)
        scaled = step / jnp.sqrt(spread + 1e-06)
        residual = pltpu.roll(iterate, vecs, 1) - mul(theta, iterate)
        moved = mul(scaled, residual)
        if search is not None:
            moved = moved - mul(-past, search)
        iterate = moved - mul(-keep_turn, iterate)
        search = moved
    ritz_ref[...] = theta[:, :vecs]
    for t in range(eigen_ref.shape[1] // LANE):
        lanes = slice(t * LANE, (t + 1) * LANE)
        basis = [start_ref[:, lanes], one_ref[line(t, vecs, 0), :], two_ref[line(t, vecs, 0), :], last_ref[t, 0]]
        eigen_ref[:, lanes] = mul(iterate, jnp.concatenate(basis, axis=0))


def body(tiles, tile_row, tile_col, tile_counts, start, rotation):
    tiles = tiles.reshape(tiles.shape[2:])
    slots = tiles.shape[0]
    vecs, seg_rows = start.shape
    rows = lax.axis_size("row")
    cols = lax.axis_size("col")
    seg_tiles = seg_rows // LANE
    pair = 2 * LANE
    index = jnp.concatenate([tile_row.reshape(slots), tile_col.reshape(slots), tile_counts.reshape(1)])
    own_col = lax.axis_index("col")
    dealt = f32(rows * cols * 3, LANE)
    work = [
        pltpu.VMEM((3 * seg_tiles, 2 * vecs, LANE), jnp.bfloat16),
        pltpu.VMEM((3 * seg_tiles, vecs, LANE), jnp.float32),
    ]
    sums = [pltpu.VMEM((cols, pair), jnp.float32)]
    basis = [pltpu.VMEM((2 * vecs, seg_rows), jnp.float32)]
    corner = []
    for r in range(rows):
        for c in range(cols):
            corner.append((r * cols + c, ((r % 2) * cols + c) * cols + r // 2))

    def swap(x):
        moved = lax.all_to_all(x.reshape(rows * cols, 3 * LANE), BOTH, 0, 0)
        return moved.reshape(rows * cols * 3, LANE)

    own_start = lax.dynamic_slice_in_dim(start, own_col * pair, pair, 1)
    index, piece = lax.optimization_barrier((index, lax.ppermute(own_start, BOTH, corner)))
    block = lax.all_to_all(jnp.broadcast_to(piece, (rows, vecs, pair)), "row", 0, 0)
    mirrored = kernel_call(
        first_mirror, "first_mirror", f32(2 * seg_tiles, vecs, LANE), [SMEM] + [VMEM] * 2, work
    )(index, tiles, start)
    sent = kernel_call(first_direct, "first_direct", dealt, [SMEM] + [VMEM] * 3, work)(
        index, tiles, block, mirrored
    )
    images = []
    for _ in range(ITERS - 1):
        given, own = kernel_call(
            functools.partial(sum_and_deal, rows, cols), "sum_and_deal", (dealt, f32(rows, LANE)), [VMEM], sums
        )(swap(sent))
        images.append(swap(given))
        sent = kernel_call(multiply_next, "multiply_next", dealt, [SMEM] + [VMEM] * 2, work)(
            index, tiles, images[-1]
        )
    shown = kernel_call(
        functools.partial(sum_and_show, rows, cols), "sum_and_show", f32(cols, 2 * rows, LANE), [VMEM] * 2, sums
    )(swap(sent), own)
    shown = lax.all_to_all(shown, "col", 0, 0).reshape(cols * 2 * rows, LANE)
    known = kernel_call(gram_known, "gram_known", f32(vecs, LANE), [VMEM] * 3, basis)(start, *images)
    last = kernel_call(
        functools.partial(gram_last, rows), "gram_last", f32(rows, 2, vecs, LANE), [VMEM] * 2, basis
    )(known, shown)
    last = lax.all_to_all(last, "row", 0, 0)
    turned = jnp.pad(jnp.swapaxes(rotation, 2, 3), ((0, 0),) * 3 + ((0, LANE - vecs),))
    return kernel_call(
        functools.partial(finish, seg_rows * rows), "finish", (f32(vecs, seg_rows), f32(vecs, vecs)), [VMEM] * 5
    )(last, turned, start, *images)


def solution(mesh):
    return jax.shard_map(
        body,
        mesh=mesh,
        in_specs=(
            P("row", "col", None, None, None),
            P("row", "col", None),
            P("row", "col", None),
            P("row", "col"),
            P(None, "row"),
            P(),
        ),
        out_specs=(P(None, "row"), P()),
        check_vma=False,
    )
```

time: 298 us -> 291 us (0.977); the launches traced: 297 us -> 287 us
  blocking collectives: 214 us -> 188 us
  waiting for transfers between devices: 27.5 us -> 36.1 us
  Pallas kernels: 9.2 us -> 15.2 us
    all_to_all x1 -> x0, blocking collectives: 40 us -> none  [to_all(): return lax.all_to_all(jnp.broadcast_to(x, (count,) + x.shape), axis, 0, 0)]
    all_to_all x4 -> x5, blocking collectives: 153 us -> 188 us  [swap(): moved = lax.all_to_all(x.reshape(rows * cols, 3 * LANE), BOTH, 0, 0)]
    all_gather x1 -> x0, blocking collectives: 21.7 us -> none  [body(): lax.all_gather(last_piece, 'col')]
    all_to_all x4 -> x3, waiting for transfers between devices: 25.6 us -> 34.3 us  [the longest x1 15.1 us: body(): last = lax.all_to_all(last, 'row', 0, 0)]
    pallas_call x5 -> x7, Pallas kernels: 4.22 us -> 8.14 us  [the longest x1 1.86 us: body(): kernel_call(first_direct, 'first_direct', dealt, [SMEM] + [VMEM] * 3, work)]
    ppermute x1 -> x0, starting transfers between devices: 3.49 us -> none  [body(): turned_back = lax.ppermute(mirror, BOTH, [(to, at) for at, to in corner])]
    unnamed x11 -> x25, local copies, waits for them, and re-layouts: 2.93 us -> 5.91 us
    all_to_all x4 -> x3, starting transfers between devices: 30 us -> 32.1 us  [the longest x1 23.3 us: body(): lax.all_to_all(jnp.broadcast_to(piece, (rows, vecs, pair)), 'row', 0, 0)]
  transfers between devices with their start and end apart: 6 -> 4, of which waited for: 4 -> 4; matrix products, arithmetic and copies ran while one was open for 0% -> 0% of each run, Pallas kernels for 0% -> 1%
where the time goes in v4:
time: 291 us; the launch traced here: 287 us
  blocking collectives  188 us (65%)
  starting transfers between devices  37.5 us (13%)
  waiting for transfers between devices  36.1 us (12%)
  Pallas kernels  15.2 us (5%)
  local copies, waits for them, and re-layouts  7.5 us (3%)
    all_to_all x5, blocking collectives, swap(): moved = lax.all_to_all(x.reshape(rows * cols, 3 * LANE), BOTH, 0, 0)  188 us
    all_to_all x1, starting transfers between devices, body(): lax.all_to_all(jnp.broadcast_to(piece, (rows, vecs, pair)), 'row', 0, 0)  23.3 us
    all_to_all x1, waiting for transfers between devices, body(): last = lax.all_to_all(last, 'row', 0, 0)  15.1 us
    all_to_all x1, waiting for transfers between devices, body(): lax.all_to_all(jnp.broadcast_to(piece, (rows, vecs, pair)), 'row', 0, 0)  12.3 us
    all_to_all x1, waiting for transfers between devices, body(): shown = lax.all_to_all(shown, 'col', 0, 0).reshape(cols * 2 * rows, LANE)  6.93 us
    unnamed x25, local copies, waits for them, and re-layouts  5.91 us
  transfers between devices with their start and end apart: 4, of which 4 were waited for; matrix products, arithmetic and copies ran while one was open for 0% of the time, Pallas kernels for 1%

profile of v4, /device:TPU:1, one launch (start us, length us, event | category | flops | bytes accessed | tf_op | source)
XLA Modules:
  0.0 286.8 jit_solution(13376560213626369862)
XLA Ops:
  0.6 0.7 constant_dynamic-slice_fusion
  1.4 5.4 %collective-permute-start = (f32[16,256]{1,0:T(8,128)S(1)}, f32[16,256]{1,0:T(8,128)S(1)}, u32[]{:S(2)}, u32[]{:S(2)}) collective-permute-start(f32[16,256]{1,0:T(8,128)S(1)} %constant_dynamic-slice_fusion), channel_id=1, source_target_pairs={{0,0},{1,16},{2,32},{3,48},{4,64},{5,80},{6,96},{7,112},{8,128},{9... | collective-permute-start | bytes 49160 | tf_op jit(solution)/shard_map/ppermute | solution.py:239
  7.4 0.7 pad_add_fusion.index_ref
  8.1 1.8 collective-permute-done
  10.0 0.9 broadcast_in_dim.3
  10.8 23.3 %all-to-all-start = ((f32[32,16,256]{2,1,0:T(8,128)}), f32[32,16,256]{2,1,0:T(8,128)}, u32[]{:S(2)}, u32[]{:S(2)}) async-start(f32[32,16,256]{2,1,0:T(8,128)} %broadcast_in_dim.3), calls=%async_computation | async-start | bytes 1048576 | tf_op jit(solution)/shard_map/all_to_all | solution.py:240
  34.2 0.0 copy-start
  34.2 1.9 copy-done
  36.1 0.0 copy-start.7
  36.1 0.9 copy-done.7
  37.0 0.0 copy-start.1
  37.0 1.1 first_mirror.1.mirrored_ref
  38.1 0.0 copy-start.9
  38.1 0.8 copy-done.9
  38.9 12.3 %all-to-all-done.block_ref = f32[32,16,256]{2,1,0:T(8,128)} async-done(((f32[32,16,256]{2,1,0:T(8,128)}), f32[32,16,256]{2,1,0:T(8,128)}, u32[]{:S(2)}, u32[]{:S(2)}) %all-to-all-start) | async-done | bytes 524320 | tf_op jit(solution)/shard_map/all_to_all | solution.py:240
  51.2 0.0 copy-done.1
  51.2 0.0 copy-start.10
  51.2 1.0 copy-done.10
  52.2 1.9 first_direct.1
  54.1 39.9 %all_to_all.60 = f32[512,1,384]{2,1,0:T(1,128)S(1)} all-to-all(f32[512,1,384]{2,1,0:T(1,128)S(1)} %bitcast.32), channel_id=1, replica_groups=mesh['row'=32,'col'=16] {'row','col'}, dimensions={0} | all-to-all | bytes 1572864 | tf_op jit(solution)/shard_map/all_to_all | solution.py:235
  94.0 0.7 sum_and_deal.2
  94.7 36.3 %all_to_all.61 = f32[512,1,384]{2,1,0:T(1,128)S(1)} all-to-all(f32[512,1,384]{2,1,0:T(1,128)S(1)} %bitcast.34), channel_id=1, replica_groups=mesh['row'=32,'col'=16] {'row','col'}, dimensions={0} | all-to-all | bytes 1572864 | tf_op jit(solution)/shard_map/all_to_all | solution.py:235
  131.0 0.0 copy-start.2
  131.0 1.7 multiply_next.2
  132.8 37.8 %all_to_all.62 = f32[512,1,384]{2,1,0:T(1,128)S(1)} all-to-all(f32[512,1,384]{2,1,0:T(1,128)S(1)} %bitcast.28), channel_id=1, replica_groups=mesh['row'=32,'col'=16] {'row','col'}, dimensions={0} | all-to-all | bytes 1572864 | tf_op jit(solution)/shard_map/all_to_all | solution.py:235
  170.6 0.0 copy-done.2
  170.6 0.1 sum_and_deal.3
  170.7 36.5 %all_to_all.63 = f32[512,1,384]{2,1,0:T(1,128)S(1)} all-to-all(f32[512,1,384]{2,1,0:T(1,128)S(1)} %bitcast.35), channel_id=1, replica_groups=mesh['row'=32,'col'=16] {'row','col'}, dimensions={0} | all-to-all | bytes 1572864 | tf_op jit(solution)/shard_map/all_to_all | solution.py:235
  207.2 0.0 copy-start.4
  207.2 1.7 multiply_next.3
  208.9 0.0 copy-start.3
  208.9 0.0 copy-start.8
  209.0 37.8 %all_to_all.64 = f32[512,1,384]{2,1,0:T(1,128)S(1)} all-to-all(f32[512,1,384]{2,1,0:T(1,128)S(1)} %bitcast.27), channel_id=1, replica_groups=mesh['row'=32,'col'=16] {'row','col'}, dimensions={0} | all-to-all | bytes 1572864 | tf_op jit(solution)/shard_map/all_to_all | solution.py:235
  246.7 0.0 copy-done.4
  246.7 0.0 copy-start.11
  246.7 0.0 copy-start.6
  246.7 0.9 sum_and_show.1
  247.7 4.3 %all-to-all-start.6 = ((f32[16,64,128]{2,1,0:T(8,128)}), f32[16,64,128]{2,1,0:T(8,128)S(1)}, u32[]{:S(2)}, u32[]{:S(2)}) async-start(f32[16,64,128]{2,1,0:T(8,128)} %sum_and_show.1), calls=%async_computation.6 | async-start | bytes 1048576 | tf_op jit(solution)/shard_map/all_to_all | solution.py:259
  251.9 0.0 copy-done.3
  252.0 0.0 copy-done.8
  252.0 0.0 copy-start.5
  252.0 1.1 copy-done.5
  253.1 1.7 gram_known.1.known_ref
  254.8 6.9 %all-to-all-done.6 = f32[16,64,128]{2,1,0:T(8,128)S(1)} async-done(((f32[16,64,128]{2,1,0:T(8,128)}), f32[16,64,128]{2,1,0:T(8,128)S(1)}, u32[]{:S(2)}, u32[]{:S(2)}) %all-to-all-start.6) | async-done | bytes 524320 | tf_op jit(solution)/shard_map/all_to_all | solution.py:259
  261.8 1.7 gram_last.1
  263.5 4.5 %all-to-all-start.7 = ((f32[32,2,16,128]{3,2,1,0:T(8,128)}), f32[32,2,16,128]{3,2,1,0:T(8,128)S(1)}, u32[]{:S(2)}, u32[]{:S(2)}) async-start(f32[32,2,16,128]{3,2,1,0:T(8,128)} %gram_last.1), calls=%async_computation.7 | async-start | bytes 1048576 | tf_op jit(solution)/shard_map/all_to_all | solution.py:264
  268.0 0.0 copy-done.11
  268.0 0.1 copy.14
  268.1 15.1 %all-to-all-done.7.last_ref = f32[32,2,16,128]{3,2,1,0:T(8,128)S(1)} async-done(((f32[32,2,16,128]{3,2,1,0:T(8,128)}), f32[32,2,16,128]{3,2,1,0:T(8,128)S(1)}, u32[]{:S(2)}, u32[]{:S(2)}) %all-to-all-start.7) | async-done | bytes 524320 | tf_op jit(solution)/shard_map/all_to_all | solution.py:264
  283.2 0.0 copy-done.6
  283.2 3.6 %finish.1 = (f32[16,4096]{1,0:T(8,128)}, f32[16,16]{1,0:T(8,128)}) custom-call(f32[32,2,16,128]{3,2,1,0:T(8,128)S(1)} %all-to-all-done.7.last_ref, f32[3,3,16,128]{3,2,1,0:T(8,128)S(1)} %pad.4.turn_ref, f32[16,4096]{1,0:T(8,128)S(1)} %copy-done.8, f32[1536,128]{1,0:T(8,128)S(1)} %bitcast.23, f32[1536,128]{1,0:T(8,128)S(1)} %bitcast.26), custom_call_target="tpu_custom_call" | custom-call | tf_op jit(solution)/shard_map/finish/pallas_call | solution.py:266
  (1 shorter events, 0.0 us)
Async XLA Ops:
  1.4 8.6 %collective-permute-start = (f32[16,256]{1,0:T(8,128)S(1)}, f32[16,256]{1,0:T(8,128)S(1)}, u32[]{:S(2)}, u32[]{:S(2)}) collective-permute-start(f32[16,256]{1,0:T(8,128)S(1)} %constant_dynamic-slice_fusion), channel_id=1, source_target_pairs={{0,0},{1,16},{2,32},{3,48},{4,64},{5,80},{6,96},{7,112},{8,128},{9... | collective-permute-start | bytes 49160 | tf_op jit(solution)/shard_map/ppermute | solution.py:239
  10.8 40.4 %all-to-all-start = ((f32[32,16,256]{2,1,0:T(8,128)}), f32[32,16,256]{2,1,0:T(8,128)}, u32[]{:S(2)}, u32[]{:S(2)}) async-start(f32[32,16,256]{2,1,0:T(8,128)} %broadcast_in_dim.3), calls=%async_computation | async-start | bytes 1048576 | tf_op jit(solution)/shard_map/all_to_all | solution.py:240
  34.2 1.9 copy-start
  36.1 0.9 copy-start.7
  37.0 14.2 %copy-start.1 = (bf16[1,1,96,128,128]{4,3,2,1,0:T(8,128)(2,1)S(1)}, bf16[1,1,96,128,128]{4,3,2,1,0:T(8,128)(2,1)}, u32[]{:S(2)}) copy-start(bf16[1,1,96,128,128]{4,3,2,1,0:T(8,128)(2,1)} %param.6) | copy-start | bytes 9437188
  38.1 0.8 copy-start.9
  51.2 1.0 copy-start.10
  131.0 39.5 %copy-start.2 = (f32[512,1,384]{2,1,0:T(1,128)}, f32[512,1,384]{2,1,0:T(1,128)S(1)}, u32[]{:S(2)}) copy-start(f32[512,1,384]{2,1,0:T(1,128)S(1)} %all_to_all.61) | copy-start | bytes 2359300
  207.2 39.5 %copy-start.4 = (f32[512,1,384]{2,1,0:T(1,128)}, f32[512,1,384]{2,1,0:T(1,128)S(1)}, u32[]{:S(2)}) copy-start(f32[512,1,384]{2,1,0:T(1,128)S(1)} %all_to_all.63) | copy-start | bytes 2359300
  208.9 43.0 %copy-start.3 = (f32[512,1,384]{2,1,0:T(1,128)S(1)}, f32[512,1,384]{2,1,0:T(1,128)}, u32[]{:S(2)}) copy-start(f32[512,1,384]{2,1,0:T(1,128)} %copy-done.2) | copy-start | bytes 2359300
  208.9 43.0 %copy-start.8 = (f32[16,4096]{1,0:T(8,128)S(1)}, f32[16,4096]{1,0:T(8,128)}, u32[]{:S(2)}) copy-start(f32[16,4096]{1,0:T(8,128)} %start_ref.3) | copy-start | bytes 786436
  246.7 21.2 %copy-start.11 = (f32[3,3,16,16]{3,2,1,0:T(8,128)S(1)}, f32[3,3,16,16]{3,2,1,0:T(8,128)}, u32[]{:S(2)}) copy-start(f32[3,3,16,16]{3,2,1,0:T(8,128)} %param.11) | copy-start | bytes 27652
  246.7 36.4 %copy-start.6 = (f32[512,1,384]{2,1,0:T(1,128)S(1)}, f32[512,1,384]{2,1,0:T(1,128)}, u32[]{:S(2)}) copy-start(f32[512,1,384]{2,1,0:T(1,128)} %copy-done.4) | copy-start | bytes 2359300
  247.7 14.1 %all-to-all-start.6 = ((f32[16,64,128]{2,1,0:T(8,128)}), f32[16,64,128]{2,1,0:T(8,128)S(1)}, u32[]{:S(2)}, u32[]{:S(2)}) async-start(f32[16,64,128]{2,1,0:T(8,128)} %sum_and_show.1), calls=%async_computation.6 | async-start | bytes 1048576 | tf_op jit(solution)/shard_map/all_to_all | solution.py:259
  252.0 1.1 copy-start.5
  263.5 19.7 %all-to-all-start.7 = ((f32[32,2,16,128]{3,2,1,0:T(8,128)}), f32[32,2,16,128]{3,2,1,0:T(8,128)S(1)}, u32[]{:S(2)}, u32[]{:S(2)}) async-start(f32[32,2,16,128]{3,2,1,0:T(8,128)} %gram_last.1), calls=%async_computation.7 | async-start | bytes 1048576 | tf_op jit(solution)/shard_map/all_to_all | solution.py:264

commit v5 on v4

--- a/solution.py
+++ b/solution.py
@@ -102,39 +102,51 @@
             out_ref[line(t, vecs, part), :] = total[part * seg_tiles + t]
 
 
-def add_up(rows, cols, got_ref, sums):
-    for r in range(rows):
-        half = r % 2
-        sums[r // 2 : r // 2 + 1, half * LANE : (half + 1) * LANE] = jnp.sum(
-            got_ref[line(r, cols, 0), :], axis=0, keepdims=True
-        )
-    for half in range(2):
-        mirror = got_ref[line(0, cols, 1 + half), :]
-        for r in range(1, rows):
-            mirror = mirror + got_ref[line(r, cols, 1 + half), :]
-        lanes = slice(half * LANE, (half + 1) * LANE)
-        sums[:, lanes] = sums[:, lanes] + mirror
-
-
-def sum_and_deal(rows, cols, got_ref, out_ref, own_ref, sums):
-    add_up(rows, cols, got_ref, sums)
-    for half in range(2):
-        own_ref[pl.ds(half, cols, stride=2), :] = sums[:, half * LANE : (half + 1) * LANE]
-    for r in range(rows):
-        half = r % 2
-        out_ref[line(r, cols, 0), :] = jnp.broadcast_to(
-            sums[r // 2 : r // 2 + 1, half * LANE : (half + 1) * LANE], (cols, LANE)
-        )
-        for half in range(2):
-            out_ref[line(r, cols, 1 + half), :] = sums[:, half * LANE : (half + 1) * LANE]
-
-
-def sum_and_show(rows, cols, got_ref, two_ref, out_ref, sums):
-    add_up(rows, cols, got_ref, sums)
-    for c in range(cols):
-        out_ref[c, 0:rows, :] = two_ref[...]
-        for half in range(2):
-            out_ref[c, pl.ds(rows + half, cols, stride=2), :] = sums[:, half * LANE : (half + 1) * LANE]
+def line_pair(r, half, which, part):
+    return pl.ds(r * half * 6 + which * 3 + part, half, stride=6)
+
+
+def add_up(rows, half, index_ref, got_ref, sums_ref):
+    odd = index_ref[index_ref.shape[0] - 1] == 1
+    for which in range(2):
+        base = which * rows
+        for r in range(rows):
+            sums_ref[base + r : base + r + 1, :] = jnp.sum(
+                got_ref[line_pair(r, half, which, 0), :], axis=0, keepdims=True
+            )
+        for part in range(2):
+            mirror = got_ref[line_pair(0, half, which, 1 + part), :]
+            for r in range(1, rows):
+                mirror = mirror + got_ref[line_pair(r, half, which, 1 + part), :]
+            for core in range(2):
+                place = pl.ds(base + 2 * core + part, half, stride=4)
+                sums_ref[place, :] = sums_ref[place, :] + jnp.where(odd == (core == 1), mirror, 0.0)
+
+
+def deal(rows, half, index_ref, mine_ref, other_ref, out_ref, own_ref):
+    odd = index_ref[index_ref.shape[0] - 1] == 1
+    own_ref[...] = mine_ref[...] + other_ref[...]
+    for which in range(2):
+        base = which * rows
+        blocks = []
+        for part in range(2):
+            even_rows = own_ref[pl.ds(base + part, half, stride=4), :]
+            odd_rows = own_ref[pl.ds(base + 2 + part, half, stride=4), :]
+            blocks.append(jnp.where(odd, odd_rows, even_rows))
+        for r in range(rows):
+            out_ref[line_pair(r, half, which, 0), :] = jnp.broadcast_to(
+                own_ref[base + r : base + r + 1, :], (half, LANE)
+            )
+            for part in range(2):
+                out_ref[line_pair(r, half, which, 1 + part), :] = blocks[part]
+
+
+def show(mine_ref, other_ref, two_ref, out_ref):
+    three = mine_ref[...] + other_ref[...]
+    size = three.shape[0]
+    for c in range(out_ref.shape[0]):
+        out_ref[c, 0:size, :] = two_ref[...]
+        out_ref[c, size : 2 * size, :] = three
 
 
 def dots(a, b):
@@ -157,10 +169,11 @@
     vecs = known_ref.shape[0]
     for s in range(rows):
         lanes = slice(s * LANE, (s + 1) * LANE)
-        basis[0:vecs, lanes] = shown_ref[pl.ds(s, vecs, stride=2 * rows), :]
-        three = shown_ref[pl.ds(rows + s, vecs, stride=2 * rows), :]
-        basis[vecs : 2 * vecs, lanes] = three
-        out_ref[s, 0] = three
+        for j in range(2):
+            for which in range(2):
+                taken = shown_ref[pl.ds((j * 2 + which) * rows + s, vecs // 2, stride=4 * rows), :]
+                out_ref[s, 1 - j, pl.ds(which, vecs // 2, stride=2), :] = taken
+            basis[j * vecs : (j + 1) * vecs, lanes] = out_ref[s, 1 - j]
     two, three = basis[0:vecs, :], basis[vecs : 2 * vecs, :]
     width = (2 * ITERS - 1) * vecs
     parts = [known_ref[...][:, :width], dots(two, three), dots(three, three)]
@@ -217,14 +230,18 @@
     cols = lax.axis_size("col")
     seg_tiles = seg_rows // LANE
     pair = 2 * LANE
-    index = jnp.concatenate([tile_row.reshape(slots), tile_col.reshape(slots), tile_counts.reshape(1)])
+    half = cols // 2
     own_col = lax.axis_index("col")
+    index = [tile_row.reshape(slots), tile_col.reshape(slots), tile_counts.reshape(1), (own_col % 2).reshape(1)]
+    index = jnp.concatenate(index)
     dealt = f32(rows * cols * 3, LANE)
     work = [
         pltpu.VMEM((3 * seg_tiles, 2 * vecs, LANE), jnp.bfloat16),
         pltpu.VMEM((3 * seg_tiles, vecs, LANE), jnp.float32),
     ]
-    sums = [pltpu.VMEM((cols, pair), jnp.float32)]
+    summed = f32(2 * rows, LANE)
+    same_core = [[core + 2 * c for c in range(half)] for core in range(2)]
+    all_same_core = [[r * cols + c for r in range(rows) for c in group] for group in same_core]
     basis = [pltpu.VMEM((2 * vecs, seg_rows), jnp.float32)]
     corner = []
     for r in range(rows):
@@ -232,8 +249,14 @@
             corner.append((r * cols + c, ((r % 2) * cols + c) * cols + r // 2))
 
     def swap(x):
-        moved = lax.all_to_all(x.reshape(rows * cols, 3 * LANE), BOTH, 0, 0)
-        return moved.reshape(rows * cols * 3, LANE)
+        x = x.reshape(rows * half, 6 * LANE)
+        x = lax.all_to_all(x, BOTH, 0, 0, axis_index_groups=all_same_core)
+        return x.reshape(rows * cols * 3, LANE)
+
+    def reduced(x):
+        add = functools.partial(add_up, rows, half)
+        mine = kernel_call(add, "add_up", summed, [SMEM, VMEM])(index, swap(x))
+        return mine, lax.ppermute(mine, "col", [(c, c ^ 1) for c in range(cols)])
 
     own_start = lax.dynamic_slice_in_dim(start, own_col * pair, pair, 1)
     index, piece = lax.optimization_barrier((index, lax.ppermute(own_start, BOTH, corner)))
@@ -247,16 +270,14 @@
     images = []
     for _ in range(ITERS - 1):
         given, own = kernel_call(
-            functools.partial(sum_and_deal, rows, cols), "sum_and_deal", (dealt, f32(rows, LANE)), [VMEM], sums
-        )(swap(sent))
+            functools.partial(deal, rows, half), "deal", (dealt, summed), [SMEM] + [VMEM] * 2
+        )(index, *reduced(sent))
         images.append(swap(given))
         sent = kernel_call(multiply_next, "multiply_next", dealt, [SMEM] + [VMEM] * 2, work)(
             index, tiles, images[-1]
         )
-    shown = kernel_call(
-        functools.partial(sum_and_show, rows, cols), "sum_and_show", f32(cols, 2 * rows, LANE), [VMEM] * 2, sums
-    )(swap(sent), own)
-    shown = lax.all_to_all(shown, "col", 0, 0).reshape(cols * 2 * rows, LANE)
+    shown = kernel_call(show, "show", f32(half, 4 * rows, LANE), [VMEM] * 3)(*reduced(sent), own)
+    shown = lax.all_to_all(shown, "col", 0, 0, axis_index_groups=same_core).reshape(half * 4 * rows, LANE)
     known = kernel_call(gram_known, "gram_known", f32(vecs, LANE), [VMEM] * 3, basis)(start, *images)
     last = kernel_call(
         functools.partial(gram_last, rows), "gram_last", f32(rows, 2, vecs, LANE), [VMEM] * 2, basis

time: 291 us -> 297 us (1.021)
  starting transfers between devices: 37.5 us -> 51.9 us
  blocking collectives: 188 us -> 175 us
    ppermute x0 -> x3, starting transfers between devices: none -> 15.8 us  [reduced(): return (mine, lax.ppermute(mine, 'col', [(c, c ^ 1) for c in range(cols)]))]
    all_to_all x5, blocking collectives: 188 us -> 175 us  [swap(): x = lax.all_to_all(x, BOTH, 0, 0, axis_index_groups=all_same_core)]
  transfers between devices with their start and end apart: 4 -> 7, of which waited for: 4 -> 7; matrix products, arithmetic and copies ran while one was open for 0% -> 0% of each run, Pallas kernels for 1% -> 1%
where the time goes in v5:
time: 297 us; the launch traced here: 291 us
  blocking collectives  175 us (59%)
  starting transfers between devices  51.9 us (17%)
  waiting for transfers between devices  36.5 us (12%)
  Pallas kernels  17.9 us (6%)
  local copies, waits for them, and re-layouts  7.49 us (3%)
    all_to_all x5, blocking collectives, swap(): x = lax.all_to_all(x, BOTH, 0, 0, axis_index_groups=all_same_core)  175 us
    all_to_all x1, starting transfers between devices, body(): lax.all_to_all(jnp.broadcast_to(piece, (rows, vecs, pair)), 'row', 0, 0)  23.3 us
    ppermute x3, starting transfers between devices, reduced(): return (mine, lax.ppermute(mine, 'col', [(c, c ^ 1) for c in range(cols)]))  15.8 us
    all_to_all x1, waiting for transfers between devices, body(): last = lax.all_to_all(last, 'row', 0, 0)  14.3 us
    all_to_all x1, waiting for transfers between devices, body(): lax.all_to_all(jnp.broadcast_to(piece, (rows, vecs, pair)), 'row', 0, 0)  12.3 us
  transfers between devices with their start and end apart: 7, of which 7 were waited for; matrix products, arithmetic and copies ran while one was open for 0% of the time, Pallas kernels for 1%

profile of v5, /device:TPU:1, one launch (start us, length us, event | category | flops | bytes accessed | tf_op | source)
XLA Modules:
  0.0 291.3 jit_solution(1978043096521872385)
XLA Ops:
  0.6 0.7 constant_dynamic-slice_fusion
  1.4 5.4 %collective-permute-start = (f32[16,256]{1,0:T(8,128)S(1)}, f32[16,256]{1,0:T(8,128)S(1)}, u32[]{:S(2)}, u32[]{:S(2)}) collective-permute-start(f32[16,256]{1,0:T(8,128)S(1)} %constant_dynamic-slice_fusion), channel_id=1, source_target_pairs={{0,0},{1,16},{2,32},{3,48},{4,64},{5,80},{6,96},{7,112},{8,128},{9... | collective-permute-start | bytes 49160 | tf_op jit(solution)/shard_map/ppermute | solution.py:262
  7.4 0.7 pad_add_fusion.index_ref
  8.1 1.8 collective-permute-done
  10.0 0.9 broadcast_in_dim.3
  10.8 23.3 %all-to-all-start = ((f32[32,16,256]{2,1,0:T(8,128)}), f32[32,16,256]{2,1,0:T(8,128)}, u32[]{:S(2)}, u32[]{:S(2)}) async-start(f32[32,16,256]{2,1,0:T(8,128)} %broadcast_in_dim.3), calls=%async_computation | async-start | bytes 1048576 | tf_op jit(solution)/shard_map/all_to_all | solution.py:263
  34.2 0.0 copy-start
  34.2 1.9 copy-done
  36.1 0.0 copy-start.7
  36.1 0.9 copy-done.7
  37.0 0.0 copy-start.1
  37.0 1.1 first_mirror.1.mirrored_ref
  38.1 0.0 copy-start.9
  38.1 0.8 copy-done.9
  38.9 12.3 %all-to-all-done.block_ref = f32[32,16,256]{2,1,0:T(8,128)} async-done(((f32[32,16,256]{2,1,0:T(8,128)}), f32[32,16,256]{2,1,0:T(8,128)}, u32[]{:S(2)}, u32[]{:S(2)}) %all-to-all-start) | async-done | bytes 524320 | tf_op jit(solution)/shard_map/all_to_all | solution.py:263
  51.2 0.0 copy-done.1
  51.2 0.0 copy-start.10
  51.2 1.0 copy-done.10
  52.2 1.9 first_direct.1
  54.1 37.3 %all_to_all.60 = f32[256,1,768]{2,1,0:T(1,128)S(1)} all-to-all(f32[256,1,768]{2,1,0:T(1,128)S(1)} %bitcast.33), channel_id=1, replica_groups={{0,2,4,6,8,10,12,14,16,18,20,22,24,26,28,30,32,34,36,38,40,42,44,46,48,..., dimensions={0} | all-to-all | bytes 1572864 | tf_op jit(solution)/shard_map/all_to_all | solution.py:253
  91.4 0.6 add_up.3.mine_ref
  92.0 5.1 %collective-permute-start.1 = (f32[64,128]{1,0:T(8,128)S(1)}, f32[64,128]{1,0:T(8,128)S(1)}, u32[]{:S(2)}, u32[]{:S(2)}) collective-permute-start(f32[64,128]{1,0:T(8,128)S(1)} %add_up.3.mine_ref), channel_id=1, source_target_pairs={{0,1},{1,0},{2,3},{3,2},{4,5},{5,4},{6,7},{7,6},{8,9},{9,8},{10,11... | collective-permute-start | bytes 98312 | tf_op jit(solution)/shard_map/ppermute | solution.py:259
  97.1 0.8 collective-permute-done.1.other_ref
  97.9 1.2 deal.2
  99.1 34.0 %all_to_all.61 = f32[256,1,768]{2,1,0:T(1,128)S(1)} all-to-all(f32[256,1,768]{2,1,0:T(1,128)S(1)} %bitcast.35), channel_id=1, replica_groups={{0,2,4,6,8,10,12,14,16,18,20,22,24,26,28,30,32,34,36,38,40,42,44,46,48,..., dimensions={0} | all-to-all | bytes 1572864 | tf_op jit(solution)/shard_map/all_to_all | solution.py:253
  133.1 0.0 copy-start.2
  133.1 1.7 multiply_next.2
  134.8 35.0 %all_to_all.62 = f32[256,1,768]{2,1,0:T(1,128)S(1)} all-to-all(f32[256,1,768]{2,1,0:T(1,128)S(1)} %bitcast.28), channel_id=1, replica_groups={{0,2,4,6,8,10,12,14,16,18,20,22,24,26,28,30,32,34,36,38,40,42,44,46,48,..., dimensions={0} | all-to-all | bytes 1572864 | tf_op jit(solution)/shard_map/all_to_all | solution.py:253
  169.8 0.0 copy-done.2
  169.8 0.6 add_up.4.mine_ref
  170.5 5.3 %collective-permute-start.2 = (f32[64,128]{1,0:T(8,128)S(1)}, f32[64,128]{1,0:T(8,128)S(1)}, u32[]{:S(2)}, u32[]{:S(2)}) collective-permute-start(f32[64,128]{1,0:T(8,128)S(1)} %add_up.4.mine_ref), channel_id=1, source_target_pairs={{0,1},{1,0},{2,3},{3,2},{4,5},{5,4},{6,7},{7,6},{8,9},{9,8},{10,11... | collective-permute-start | bytes 98312 | tf_op jit(solution)/shard_map/ppermute | solution.py:259
  175.8 0.8 collective-permute-done.2.other_ref
  176.6 0.6 deal.3
  177.2 34.0 %all_to_all.63 = f32[256,1,768]{2,1,0:T(1,128)S(1)} all-to-all(f32[256,1,768]{2,1,0:T(1,128)S(1)} %bitcast.36), channel_id=1, replica_groups={{0,2,4,6,8,10,12,14,16,18,20,22,24,26,28,30,32,34,36,38,40,42,44,46,48,..., dimensions={0} | all-to-all | bytes 1572864 | tf_op jit(solution)/shard_map/all_to_all | solution.py:253
  211.2 0.0 copy-start.4
  211.2 1.7 multiply_next.3
  213.0 0.0 copy-start.3
  213.0 0.0 copy-start.8
  213.0 35.0 %all_to_all.64 = f32[256,1,768]{2,1,0:T(1,128)S(1)} all-to-all(f32[256,1,768]{2,1,0:T(1,128)S(1)} %bitcast.29), channel_id=1, replica_groups={{0,2,4,6,8,10,12,14,16,18,20,22,24,26,28,30,32,34,36,38,40,42,44,46,48,..., dimensions={0} | all-to-all | bytes 1572864 | tf_op jit(solution)/shard_map/all_to_all | solution.py:253
  248.0 0.0 copy-done.4
  248.0 0.0 copy-start.11
  248.0 0.6 add_up.5.mine_ref
  248.6 0.0 copy-start.6
  248.6 5.4 %collective-permute-start.3 = (f32[64,128]{1,0:T(8,128)S(1)}, f32[64,128]{1,0:T(8,128)S(1)}, u32[]{:S(2)}, u32[]{:S(2)}) collective-permute-start(f32[64,128]{1,0:T(8,128)S(1)} %add_up.5.mine_ref), channel_id=1, source_target_pairs={{0,1},{1,0},{2,3},{3,2},{4,5},{5,4},{6,7},{7,6},{8,9},{9,8},{10,11... | collective-permute-start | bytes 98312 | tf_op jit(solution)/shard_map/ppermute | solution.py:259
  254.1 0.8 collective-permute-done.3.other_ref
  254.9 0.8 show.1
  255.8 3.5 %all-to-all-start.6 = ((f32[8,128,128]{2,1,0:T(8,128)}), f32[8,128,128]{2,1,0:T(8,128)S(1)}, u32[]{:S(2)}, u32[]{:S(2)}) async-start(f32[8,128,128]{2,1,0:T(8,128)} %show.1), calls=%async_computation.6 | async-start | bytes 1048576 | tf_op jit(solution)/shard_map/all_to_all | solution.py:280
  259.3 0.0 copy-done.3
  259.3 0.0 copy-done.8
  259.3 0.0 copy-start.5
  259.3 1.1 copy-done.5
  260.4 1.7 gram_known.1.known_ref
  262.1 5.6 %all-to-all-done.6 = f32[8,128,128]{2,1,0:T(8,128)S(1)} async-done(((f32[8,128,128]{2,1,0:T(8,128)}), f32[8,128,128]{2,1,0:T(8,128)S(1)}, u32[]{:S(2)}, u32[]{:S(2)}) %all-to-all-start.6) | async-done | bytes 524320 | tf_op jit(solution)/shard_map/all_to_all | solution.py:280
  267.7 1.7 gram_last.1
  269.4 3.9 %all-to-all-start.7 = ((f32[32,2,16,128]{3,2,1,0:T(8,128)}), f32[32,2,16,128]{3,2,1,0:T(8,128)S(1)}, u32[]{:S(2)}, u32[]{:S(2)}) async-start(f32[32,2,16,128]{3,2,1,0:T(8,128)} %gram_last.1), calls=%async_computation.7 | async-start | bytes 1048576 | tf_op jit(solution)/shard_map/all_to_all | solution.py:285
  273.3 0.0 copy-done.11
  273.3 0.1 copy.14
  273.4 14.3 %all-to-all-done.7.last_ref = f32[32,2,16,128]{3,2,1,0:T(8,128)S(1)} async-done(((f32[32,2,16,128]{3,2,1,0:T(8,128)}), f32[32,2,16,128]{3,2,1,0:T(8,128)S(1)}, u32[]{:S(2)}, u32[]{:S(2)}) %all-to-all-start.7) | async-done | bytes 524320 | tf_op jit(solution)/shard_map/all_to_all | solution.py:285
  287.8 0.0 copy-done.6
  287.8 3.6 %finish.1 = (f32[16,4096]{1,0:T(8,128)}, f32[16,16]{1,0:T(8,128)}) custom-call(f32[32,2,16,128]{3,2,1,0:T(8,128)S(1)} %all-to-all-done.7.last_ref, f32[3,3,16,128]{3,2,1,0:T(8,128)S(1)} %pad.4.turn_ref, f32[16,4096]{1,0:T(8,128)S(1)} %copy-done.8, f32[1536,128]{1,0:T(8,128)S(1)} %bitcast.24, f32[1536,128]{1,0:T(8,128)S(1)} %bitcast.27), custom_call_target="tpu_custom_call" | custom-call | tf_op jit(solution)/shard_map/finish/pallas_call | solution.py:287
  (1 shorter events, 0.0 us)
Async XLA Ops:
  1.4 8.6 %collective-permute-start = (f32[16,256]{1,0:T(8,128)S(1)}, f32[16,256]{1,0:T(8,128)S(1)}, u32[]{:S(2)}, u32[]{:S(2)}) collective-permute-start(f32[16,256]{1,0:T(8,128)S(1)} %constant_dynamic-slice_fusion), channel_id=1, source_target_pairs={{0,0},{1,16},{2,32},{3,48},{4,64},{5,80},{6,96},{7,112},{8,128},{9... | collective-permute-start | bytes 49160 | tf_op jit(solution)/shard_map/ppermute | solution.py:262
  10.8 40.4 %all-to-all-start = ((f32[32,16,256]{2,1,0:T(8,128)}), f32[32,16,256]{2,1,0:T(8,128)}, u32[]{:S(2)}, u32[]{:S(2)}) async-start(f32[32,16,256]{2,1,0:T(8,128)} %broadcast_in_dim.3), calls=%async_computation | async-start | bytes 1048576 | tf_op jit(solution)/shard_map/all_to_all | solution.py:263
  34.2 1.9 copy-start
  36.1 0.9 copy-start.7
  37.0 14.2 %copy-start.1 = (bf16[1,1,96,128,128]{4,3,2,1,0:T(8,128)(2,1)S(1)}, bf16[1,1,96,128,128]{4,3,2,1,0:T(8,128)(2,1)}, u32[]{:S(2)}) copy-start(bf16[1,1,96,128,128]{4,3,2,1,0:T(8,128)(2,1)} %param.6) | copy-start | bytes 9437188
  38.1 0.8 copy-start.9
  51.2 1.0 copy-start.10
  92.0 5.9 %collective-permute-start.1 = (f32[64,128]{1,0:T(8,128)S(1)}, f32[64,128]{1,0:T(8,128)S(1)}, u32[]{:S(2)}, u32[]{:S(2)}) collective-permute-start(f32[64,128]{1,0:T(8,128)S(1)} %add_up.3.mine_ref), channel_id=1, source_target_pairs={{0,1},{1,0},{2,3},{3,2},{4,5},{5,4},{6,7},{7,6},{8,9},{9,8},{10,11... | collective-permute-start | bytes 98312 | tf_op jit(solution)/shard_map/ppermute | solution.py:259
  133.1 36.8 %copy-start.2 = (f32[256,1,768]{2,1,0:T(1,128)}, f32[256,1,768]{2,1,0:T(1,128)S(1)}, u32[]{:S(2)}) copy-start(f32[256,1,768]{2,1,0:T(1,128)S(1)} %all_to_all.61) | copy-start | bytes 2359300
  170.5 6.1 %collective-permute-start.2 = (f32[64,128]{1,0:T(8,128)S(1)}, f32[64,128]{1,0:T(8,128)S(1)}, u32[]{:S(2)}, u32[]{:S(2)}) collective-permute-start(f32[64,128]{1,0:T(8,128)S(1)} %add_up.4.mine_ref), channel_id=1, source_target_pairs={{0,1},{1,0},{2,3},{3,2},{4,5},{5,4},{6,7},{7,6},{8,9},{9,8},{10,11... | collective-permute-start | bytes 98312 | tf_op jit(solution)/shard_map/ppermute | solution.py:259
  211.2 36.7 %copy-start.4 = (f32[256,1,768]{2,1,0:T(1,128)}, f32[256,1,768]{2,1,0:T(1,128)S(1)}, u32[]{:S(2)}) copy-start(f32[256,1,768]{2,1,0:T(1,128)S(1)} %all_to_all.63) | copy-start | bytes 2359300
  213.0 46.3 %copy-start.3 = (f32[256,1,768]{2,1,0:T(1,128)S(1)}, f32[256,1,768]{2,1,0:T(1,128)}, u32[]{:S(2)}) copy-start(f32[256,1,768]{2,1,0:T(1,128)} %copy-done.2) | copy-start | bytes 2359300
  213.0 46.3 %copy-start.8 = (f32[16,4096]{1,0:T(8,128)S(1)}, f32[16,4096]{1,0:T(8,128)}, u32[]{:S(2)}) copy-start(f32[16,4096]{1,0:T(8,128)} %start_ref.3) | copy-start | bytes 786436
  248.0 25.3 %copy-start.11 = (f32[3,3,16,16]{3,2,1,0:T(8,128)S(1)}, f32[3,3,16,16]{3,2,1,0:T(8,128)}, u32[]{:S(2)}) copy-start(f32[3,3,16,16]{3,2,1,0:T(8,128)} %param.11) | copy-start | bytes 27652
  248.6 39.1 %copy-start.6 = (f32[256,1,768]{2,1,0:T(1,128)S(1)}, f32[256,1,768]{2,1,0:T(1,128)}, u32[]{:S(2)}) copy-start(f32[256,1,768]{2,1,0:T(1,128)} %copy-done.4) | copy-start | bytes 2359300
  248.6 6.3 %collective-permute-start.3 = (f32[64,128]{1,0:T(8,128)S(1)}, f32[64,128]{1,0:T(8,128)S(1)}, u32[]{:S(2)}, u32[]{:S(2)}) collective-permute-start(f32[64,128]{1,0:T(8,128)S(1)} %add_up.5.mine_ref), channel_id=1, source_target_pairs={{0,1},{1,0},{2,3},{3,2},{4,5},{5,4},{6,7},{7,6},{8,9},{9,8},{10,11... | collective-permute-start | bytes 98312 | tf_op jit(solution)/shard_map/ppermute | solution.py:259
  255.8 11.9 %all-to-all-start.6 = ((f32[8,128,128]{2,1,0:T(8,128)}), f32[8,128,128]{2,1,0:T(8,128)S(1)}, u32[]{:S(2)}, u32[]{:S(2)}) async-start(f32[8,128,128]{2,1,0:T(8,128)} %show.1), calls=%async_computation.6 | async-start | bytes 1048576 | tf_op jit(solution)/shard_map/all_to_all | solution.py:280
  259.3 1.1 copy-start.5
  269.4 18.3 %all-to-all-start.7 = ((f32[32,2,16,128]{3,2,1,0:T(8,128)}), f32[32,2,16,128]{3,2,1,0:T(8,128)S(1)}, u32[]{:S(2)}, u32[]{:S(2)}) async-start(f32[32,2,16,128]{3,2,1,0:T(8,128)} %gram_last.1), calls=%async_computation.7 | async-start | bytes 1048576 | tf_op jit(solution)/shard_map/all_to_all | solution.py:285

commit v6 on v4

--- a/solution.py
+++ b/solution.py
@@ -9,7 +9,7 @@
 
 ITERS = 3
 LANE = 128
-GROUP = 32
+GROUP = 96
 BOTH = ("row", "col")
 HIGH = lax.Precision.HIGHEST
 NT = (((1,), (1,)), ((), ()))
@@ -161,9 +161,9 @@
         three = shown_ref[pl.ds(rows + s, vecs, stride=2 * rows), :]
         basis[vecs : 2 * vecs, lanes] = three
         out_ref[s, 0] = three
-    two, three = basis[0:vecs, :], basis[vecs : 2 * vecs, :]
     width = (2 * ITERS - 1) * vecs
-    parts = [known_ref[...][:, :width], dots(two, three), dots(three, three)]
+    both = dots(basis[...], basis[vecs : 2 * vecs, :])
+    parts = [known_ref[...][:, :width], both[:vecs], both[vecs:]]
     parts.append(jnp.zeros((vecs, LANE - (2 * ITERS + 1) * vecs), jnp.float32))
     grams = jnp.concatenate(parts, axis=1)
     for s in range(rows):
@@ -203,10 +203,23 @@
         iterate = moved - mul(-keep_turn, iterate)
         search = moved
     ritz_ref[...] = theta[:, :vecs]
+    used = (ITERS + 1) * vecs
+    terms = []
+    rest = iterate[:, :used]
+    for _ in range(3):
+        terms.append(rest.astype(jnp.bfloat16))
+        rest = rest - terms[-1].astype(jnp.float32)
+    factors = jnp.concatenate(terms, axis=0)
     for t in range(eigen_ref.shape[1] // LANE):
         lanes = slice(t * LANE, (t + 1) * LANE)
         basis = [start_ref[:, lanes], one_ref[line(t, vecs, 0), :], two_ref[line(t, vecs, 0), :], last_ref[t, 0]]
-        eigen_ref[:, lanes] = mul(iterate, jnp.concatenate(basis, axis=0))
+        basis = jnp.concatenate(basis, axis=0)
+        high = basis.astype(jnp.bfloat16)
+        low = (basis - high.astype(jnp.float32)).astype(jnp.bfloat16)
+        large = lax.dot_general(factors, high, NN, preferred_element_type=jnp.float32)
+        small = lax.dot_general(factors[: 2 * vecs], low, NN, preferred_element_type=jnp.float32)
+        small = small[:vecs] + small[vecs:] + large[2 * vecs :]
+        eigen_ref[:, lanes] = large[:vecs] + (large[vecs : 2 * vecs] + small)
 
 
 def body(tiles, tile_row, tile_col, tile_counts, start, rotation):

time: 291 us -> 291 us (level)
  Pallas kernels: 15.2 us -> 19.7 us
  blocking collectives: 188 us -> 184 us
    all_to_all x5, blocking collectives: 188 us -> 184 us  [swap(): moved = lax.all_to_all(x.reshape(rows * cols, 3 * LANE), BOTH, 0, 0)]
    pallas_call x2, Pallas kernels: 3.43 us -> 6.89 us  [body(): kernel_call(multiply_next, 'multiply_next', dealt, [SMEM] + [VMEM] * 2, w...]
where the time goes in v6:
time: 291 us; the launch traced here: 287 us
  blocking collectives  184 us (63%)
  starting transfers between devices  37.5 us (13%)
  waiting for transfers between devices  35.6 us (12%)
  Pallas kernels  19.7 us (7%)
  local copies, waits for them, and re-layouts  7.5 us (3%)
    all_to_all x5, blocking collectives, swap(): moved = lax.all_to_all(x.reshape(rows * cols, 3 * LANE), BOTH, 0, 0)  184 us
    all_to_all x1, starting transfers between devices, body(): lax.all_to_all(jnp.broadcast_to(piece, (rows, vecs, pair)), 'row', 0, 0)  23.3 us
    all_to_all x1, waiting for transfers between devices, body(): last = lax.all_to_all(last, 'row', 0, 0)  15.1 us
    all_to_all x1, waiting for transfers between devices, body(): lax.all_to_all(jnp.broadcast_to(piece, (rows, vecs, pair)), 'row', 0, 0)  11.7 us
    all_to_all x1, waiting for transfers between devices, body(): shown = lax.all_to_all(shown, 'col', 0, 0).reshape(cols * 2 * rows, LANE)  6.93 us
    pallas_call x2, Pallas kernels, body(): kernel_call(multiply_next, 'multiply_next', dealt, [SMEM] + [VMEM] * 2, w...  6.89 us
    unnamed x25, local copies, waits for them, and re-layouts  5.91 us
  transfers between devices with their start and end apart: 4, of which 4 were waited for; matrix products, arithmetic and copies ran while one was open for 0% of the time, Pallas kernels for 1%

profile of v6, /device:TPU:1, one launch (start us, length us, event | category | flops | bytes accessed | tf_op | source)
XLA Modules:
  0.0 286.7 jit_solution(17360051666336694113)
XLA Ops:
  0.6 0.7 constant_dynamic-slice_fusion
  1.4 5.4 %collective-permute-start = (f32[16,256]{1,0:T(8,128)S(1)}, f32[16,256]{1,0:T(8,128)S(1)}, u32[]{:S(2)}, u32[]{:S(2)}) collective-permute-start(f32[16,256]{1,0:T(8,128)S(1)} %constant_dynamic-slice_fusion), channel_id=1, source_target_pairs={{0,0},{1,16},{2,32},{3,48},{4,64},{5,80},{6,96},{7,112},{8,128},{9... | collective-permute-start | bytes 49160 | tf_op jit(solution)/shard_map/ppermute | solution.py:252
  7.4 0.7 pad_add_fusion.index_ref
  8.1 1.8 collective-permute-done
  10.0 0.9 broadcast_in_dim.3
  10.8 23.3 %all-to-all-start = ((f32[32,16,256]{2,1,0:T(8,128)}), f32[32,16,256]{2,1,0:T(8,128)}, u32[]{:S(2)}, u32[]{:S(2)}) async-start(f32[32,16,256]{2,1,0:T(8,128)} %broadcast_in_dim.3), calls=%async_computation | async-start | bytes 1048576 | tf_op jit(solution)/shard_map/all_to_all | solution.py:253
  34.2 0.0 copy-start
  34.2 1.9 copy-done
  36.1 0.0 copy-start.7
  36.1 0.9 copy-done.7
  37.0 0.0 copy-start.1
  37.0 1.6 first_mirror.1.mirrored_ref
  38.6 0.0 copy-start.9
  38.6 0.8 copy-done.9
  39.5 11.7 %all-to-all-done.block_ref = f32[32,16,256]{2,1,0:T(8,128)} async-done(((f32[32,16,256]{2,1,0:T(8,128)}), f32[32,16,256]{2,1,0:T(8,128)}, u32[]{:S(2)}, u32[]{:S(2)}) %all-to-all-start) | async-done | bytes 524320 | tf_op jit(solution)/shard_map/all_to_all | solution.py:253
  51.2 0.0 copy-done.1
  51.2 0.0 copy-start.10
  51.2 1.0 copy-done.10
  52.2 3.0 %first_direct.1 = f32[1536,128]{1,0:T(8,128)S(1)} custom-call(s32[193]{0:T(256)S(1)} %pad_add_fusion.index_ref, bf16[96,128,128]{2,1,0:T(8,128)(2,1)S(1)} %bitcast.18, f32[32,16,256]{2,1,0:T(8,128)} %all-to-all-done.block_ref, f32[64,16,128]{2,1,0:T(8,128)S(1)} %copy-done.10), custom_call_target="tpu_custom_call" | custom-call | tf_op jit(solution)/shard_map/first_direct/pallas_call | solution.py:257
  55.2 38.6 %all_to_all.60 = f32[512,1,384]{2,1,0:T(1,128)S(1)} all-to-all(f32[512,1,384]{2,1,0:T(1,128)S(1)} %bitcast.32), channel_id=1, replica_groups=mesh['row'=32,'col'=16] {'row','col'}, dimensions={0} | all-to-all | bytes 1572864 | tf_op jit(solution)/shard_map/all_to_all | solution.py:248
  93.8 0.7 sum_and_deal.2
  94.5 36.3 %all_to_all.61 = f32[512,1,384]{2,1,0:T(1,128)S(1)} all-to-all(f32[512,1,384]{2,1,0:T(1,128)S(1)} %bitcast.34), channel_id=1, replica_groups=mesh['row'=32,'col'=16] {'row','col'}, dimensions={0} | all-to-all | bytes 1572864 | tf_op jit(solution)/shard_map/all_to_all | solution.py:248
  130.8 0.0 copy-start.2
  130.8 3.4 %multiply_next.2 = f32[1536,128]{1,0:T(8,128)S(1)} custom-call(s32[193]{0:T(256)S(1)} %pad_add_fusion.index_ref, bf16[96,128,128]{2,1,0:T(8,128)(2,1)S(1)} %bitcast.19, f32[1536,128]{1,0:T(8,128)S(1)} %bitcast.21), custom_call_target="tpu_custom_call" | custom-call | tf_op jit(solution)/shard_map/multiply_next/pallas_call | solution.py:266
  134.3 36.5 %all_to_all.62 = f32[512,1,384]{2,1,0:T(1,128)S(1)} all-to-all(f32[512,1,384]{2,1,0:T(1,128)S(1)} %bitcast.28), channel_id=1, replica_groups=mesh['row'=32,'col'=16] {'row','col'}, dimensions={0} | all-to-all | bytes 1572864 | tf_op jit(solution)/shard_map/all_to_all | solution.py:248
  170.8 0.0 copy-done.2
  170.8 0.1 sum_and_deal.3
  170.9 36.3 %all_to_all.63 = f32[512,1,384]{2,1,0:T(1,128)S(1)} all-to-all(f32[512,1,384]{2,1,0:T(1,128)S(1)} %bitcast.35), channel_id=1, replica_groups=mesh['row'=32,'col'=16] {'row','col'}, dimensions={0} | all-to-all | bytes 1572864 | tf_op jit(solution)/shard_map/all_to_all | solution.py:248
  207.3 0.0 copy-start.4
  207.3 3.4 %multiply_next.3 = f32[1536,128]{1,0:T(8,128)S(1)} custom-call(s32[193]{0:T(256)S(1)} %pad_add_fusion.index_ref, bf16[96,128,128]{2,1,0:T(8,128)(2,1)S(1)} %bitcast.20, f32[1536,128]{1,0:T(8,128)S(1)} %bitcast.24), custom_call_target="tpu_custom_call" | custom-call | tf_op jit(solution)/shard_map/multiply_next/pallas_call | solution.py:266
  210.7 0.0 copy-start.3
  210.7 0.0 copy-start.8
  210.7 36.5 %all_to_all.64 = f32[512,1,384]{2,1,0:T(1,128)S(1)} all-to-all(f32[512,1,384]{2,1,0:T(1,128)S(1)} %bitcast.27), channel_id=1, replica_groups=mesh['row'=32,'col'=16] {'row','col'}, dimensions={0} | all-to-all | bytes 1572864 | tf_op jit(solution)/shard_map/all_to_all | solution.py:248
  247.2 0.0 copy-done.4
  247.2 0.0 copy-start.11
  247.2 0.0 copy-start.6
  247.2 0.9 sum_and_show.1
  248.1 4.3 %all-to-all-start.6 = ((f32[16,64,128]{2,1,0:T(8,128)}), f32[16,64,128]{2,1,0:T(8,128)S(1)}, u32[]{:S(2)}, u32[]{:S(2)}) async-start(f32[16,64,128]{2,1,0:T(8,128)} %sum_and_show.1), calls=%async_computation.6 | async-start | bytes 1048576 | tf_op jit(solution)/shard_map/all_to_all | solution.py:272
  252.4 0.0 copy-done.3
  252.4 0.0 copy-done.8
  252.4 0.0 copy-start.5
  252.4 1.1 copy-done.5
  253.6 1.7 gram_known.1.known_ref
  255.3 6.9 %all-to-all-done.6 = f32[16,64,128]{2,1,0:T(8,128)S(1)} async-done(((f32[16,64,128]{2,1,0:T(8,128)}), f32[16,64,128]{2,1,0:T(8,128)S(1)}, u32[]{:S(2)}, u32[]{:S(2)}) %all-to-all-start.6) | async-done | bytes 524320 | tf_op jit(solution)/shard_map/all_to_all | solution.py:272
  262.2 1.5 gram_last.1
  263.7 4.5 %all-to-all-start.7 = ((f32[32,2,16,128]{3,2,1,0:T(8,128)}), f32[32,2,16,128]{3,2,1,0:T(8,128)S(1)}, u32[]{:S(2)}, u32[]{:S(2)}) async-start(f32[32,2,16,128]{3,2,1,0:T(8,128)} %gram_last.1), calls=%async_computation.7 | async-start | bytes 1048576 | tf_op jit(solution)/shard_map/all_to_all | solution.py:277
  268.2 0.0 copy-done.11
  268.2 0.1 copy.14
  268.3 15.1 %all-to-all-done.7.last_ref = f32[32,2,16,128]{3,2,1,0:T(8,128)S(1)} async-done(((f32[32,2,16,128]{3,2,1,0:T(8,128)}), f32[32,2,16,128]{3,2,1,0:T(8,128)S(1)}, u32[]{:S(2)}, u32[]{:S(2)}) %all-to-all-start.7) | async-done | bytes 524320 | tf_op jit(solution)/shard_map/all_to_all | solution.py:277
  283.4 0.0 copy-done.6
  283.4 3.2 %finish.1 = (f32[16,4096]{1,0:T(8,128)}, f32[16,16]{1,0:T(8,128)}) custom-call(f32[32,2,16,128]{3,2,1,0:T(8,128)S(1)} %all-to-all-done.7.last_ref, f32[3,3,16,128]{3,2,1,0:T(8,128)S(1)} %pad.4.turn_ref, f32[16,4096]{1,0:T(8,128)S(1)} %copy-done.8, f32[1536,128]{1,0:T(8,128)S(1)} %bitcast.23, f32[1536,128]{1,0:T(8,128)S(1)} %bitcast.26), custom_call_target="tpu_custom_call" | custom-call | tf_op jit(solution)/shard_map/finish/pallas_call | solution.py:279
  (1 shorter events, 0.0 us)
Async XLA Ops:
  1.4 8.6 %collective-permute-start = (f32[16,256]{1,0:T(8,128)S(1)}, f32[16,256]{1,0:T(8,128)S(1)}, u32[]{:S(2)}, u32[]{:S(2)}) collective-permute-start(f32[16,256]{1,0:T(8,128)S(1)} %constant_dynamic-slice_fusion), channel_id=1, source_target_pairs={{0,0},{1,16},{2,32},{3,48},{4,64},{5,80},{6,96},{7,112},{8,128},{9... | collective-permute-start | bytes 49160 | tf_op jit(solution)/shard_map/ppermute | solution.py:252
  10.8 40.4 %all-to-all-start = ((f32[32,16,256]{2,1,0:T(8,128)}), f32[32,16,256]{2,1,0:T(8,128)}, u32[]{:S(2)}, u32[]{:S(2)}) async-start(f32[32,16,256]{2,1,0:T(8,128)} %broadcast_in_dim.3), calls=%async_computation | async-start | bytes 1048576 | tf_op jit(solution)/shard_map/all_to_all | solution.py:253
  34.2 1.9 copy-start
  36.1 0.9 copy-start.7
  37.0 14.2 %copy-start.1 = (bf16[1,1,96,128,128]{4,3,2,1,0:T(8,128)(2,1)S(1)}, bf16[1,1,96,128,128]{4,3,2,1,0:T(8,128)(2,1)}, u32[]{:S(2)}) copy-start(bf16[1,1,96,128,128]{4,3,2,1,0:T(8,128)(2,1)} %param.6) | copy-start | bytes 9437188
  38.6 0.8 copy-start.9
  51.2 1.0 copy-start.10
  130.8 40.0 %copy-start.2 = (f32[512,1,384]{2,1,0:T(1,128)}, f32[512,1,384]{2,1,0:T(1,128)S(1)}, u32[]{:S(2)}) copy-start(f32[512,1,384]{2,1,0:T(1,128)S(1)} %all_to_all.61) | copy-start | bytes 2359300
  207.3 40.0 %copy-start.4 = (f32[512,1,384]{2,1,0:T(1,128)}, f32[512,1,384]{2,1,0:T(1,128)S(1)}, u32[]{:S(2)}) copy-start(f32[512,1,384]{2,1,0:T(1,128)S(1)} %all_to_all.63) | copy-start | bytes 2359300
  210.7 41.7 %copy-start.3 = (f32[512,1,384]{2,1,0:T(1,128)S(1)}, f32[512,1,384]{2,1,0:T(1,128)}, u32[]{:S(2)}) copy-start(f32[512,1,384]{2,1,0:T(1,128)} %copy-done.2) | copy-start | bytes 2359300
  210.7 41.7 %copy-start.8 = (f32[16,4096]{1,0:T(8,128)S(1)}, f32[16,4096]{1,0:T(8,128)}, u32[]{:S(2)}) copy-start(f32[16,4096]{1,0:T(8,128)} %start_ref.3) | copy-start | bytes 786436
  247.2 21.0 %copy-start.11 = (f32[3,3,16,16]{3,2,1,0:T(8,128)S(1)}, f32[3,3,16,16]{3,2,1,0:T(8,128)}, u32[]{:S(2)}) copy-start(f32[3,3,16,16]{3,2,1,0:T(8,128)} %param.11) | copy-start | bytes 27652
  247.2 36.2 %copy-start.6 = (f32[512,1,384]{2,1,0:T(1,128)S(1)}, f32[512,1,384]{2,1,0:T(1,128)}, u32[]{:S(2)}) copy-start(f32[512,1,384]{2,1,0:T(1,128)} %copy-done.4) | copy-start | bytes 2359300
  248.1 14.1 %all-to-all-start.6 = ((f32[16,64,128]{2,1,0:T(8,128)}), f32[16,64,128]{2,1,0:T(8,128)S(1)}, u32[]{:S(2)}, u32[]{:S(2)}) async-start(f32[16,64,128]{2,1,0:T(8,128)} %sum_and_show.1), calls=%async_computation.6 | async-start | bytes 1048576 | tf_op jit(solution)/shard_map/all_to_all | solution.py:272
  252.4 1.1 copy-start.5
  263.7 19.7 %all-to-all-start.7 = ((f32[32,2,16,128]{3,2,1,0:T(8,128)}), f32[32,2,16,128]{3,2,1,0:T(8,128)S(1)}, u32[]{:S(2)}, u32[]{:S(2)}) async-start(f32[32,2,16,128]{3,2,1,0:T(8,128)} %gram_last.1), calls=%async_computation.7 | async-start | bytes 1048576 | tf_op jit(solution)/shard_map/all_to_all | solution.py:277

commit v7 on v6

--- a/solution.py
+++ b/solution.py
@@ -9,7 +9,7 @@
 
 ITERS = 3
 LANE = 128
-GROUP = 96
+GROUP = 32
 BOTH = ("row", "col")
 HIGH = lax.Precision.HIGHEST
 NT = (((1,), (1,)), ((), ()))
@@ -91,15 +91,27 @@
             out_ref[line(t, vecs, 1 + half), :] = mirrored_ref[half * seg_tiles + t]
 
 
-def multiply_next(index_ref, tiles_ref, all_ref, out_ref, split, total):
+def multiply_all(index_ref, tiles_ref, all_ref, split, total):
     seg_tiles, vecs = total.shape[0] // 3, total.shape[1]
     for t in range(seg_tiles):
         for part in range(3):
             keep(split, part * seg_tiles + t, all_ref[line(t, vecs, part), :])
     multiply(index_ref, tiles_ref, split, total, True, True)
+
+
+def multiply_next(index_ref, tiles_ref, all_ref, out_ref, split, total):
+    seg_tiles, vecs = total.shape[0] // 3, total.shape[1]
+    multiply_all(index_ref, tiles_ref, all_ref, split, total)
     for t in range(seg_tiles):
         for part in range(3):
             out_ref[line(t, vecs, part), :] = total[part * seg_tiles + t]
+
+
+def multiply_last(index_ref, tiles_ref, all_ref, direct_ref, mirror_ref, split, total):
+    multiply_all(index_ref, tiles_ref, all_ref, split, total)
+    for refs, base in ((direct_ref, 0), (mirror_ref, total.shape[0] // 3)):
+        for t in range(2 * refs.shape[0]):
+            refs[t // 2, :, (t % 2) * LANE : (t % 2 + 1) * LANE] = total[base + t]
 
 
 def add_up(rows, cols, got_ref, sums):
@@ -116,10 +128,8 @@
         sums[:, lanes] = sums[:, lanes] + mirror
 
 
-def sum_and_deal(rows, cols, got_ref, out_ref, own_ref, sums):
+def sum_and_deal(rows, cols, got_ref, out_ref, sums):
     add_up(rows, cols, got_ref, sums)
-    for half in range(2):
-        own_ref[pl.ds(half, cols, stride=2), :] = sums[:, half * LANE : (half + 1) * LANE]
     for r in range(rows):
         half = r % 2
         out_ref[line(r, cols, 0), :] = jnp.broadcast_to(
@@ -129,45 +139,17 @@
             out_ref[line(r, cols, 1 + half), :] = sums[:, half * LANE : (half + 1) * LANE]
 
 
-def sum_and_show(rows, cols, got_ref, two_ref, out_ref, sums):
-    add_up(rows, cols, got_ref, sums)
-    for c in range(cols):
-        out_ref[c, 0:rows, :] = two_ref[...]
-        for half in range(2):
-            out_ref[c, pl.ds(rows + half, cols, stride=2), :] = sums[:, half * LANE : (half + 1) * LANE]
-
-
-def dots(a, b):
-    return lax.dot_general(a, b, NT, precision=HIGH, preferred_element_type=jnp.float32)
-
-
-def gram_known(start_ref, one_ref, two_ref, gram_ref, basis):
-    vecs = start_ref.shape[0]
-    for t in range(start_ref.shape[1] // LANE):
-        lanes = slice(t * LANE, (t + 1) * LANE)
-        basis[0:vecs, lanes] = one_ref[line(t, vecs, 0), :]
-        basis[vecs : 2 * vecs, lanes] = two_ref[line(t, vecs, 0), :]
-    held = [start_ref[...], basis[0:vecs, :], basis[vecs : 2 * vecs, :]]
-    parts = [dots(held[j // 2], held[(j + 1) // 2]) for j in range(2 * ITERS - 1)]
-    parts.append(jnp.zeros((vecs, LANE - (2 * ITERS - 1) * vecs), jnp.float32))
+def gram(zero_ref, one_ref, two_ref, three_ref, gram_ref):
+    vecs = three_ref.shape[0]
+    basis = [zero_ref[...], one_ref[...], two_ref[...], three_ref[...]]
+    parts = []
+    for j in range(ITERS + 1):
+        others = jnp.concatenate(basis[j : j + 2], axis=0)
+        parts.append(
+            lax.dot_general(basis[j], others, NT, precision=HIGH, preferred_element_type=jnp.float32)
+        )
+    parts.append(jnp.zeros((vecs, LANE - (2 * ITERS + 1) * vecs), jnp.float32))
     gram_ref[...] = jnp.concatenate(parts, axis=1)
-
-
-def gram_last(rows, known_ref, shown_ref, out_ref, basis):
-    vecs = known_ref.shape[0]
-    for s in range(rows):
-        lanes = slice(s * LANE, (s + 1) * LANE)
-        basis[0:vecs, lanes] = shown_ref[pl.ds(s, vecs, stride=2 * rows), :]
-        three = shown_ref[pl.ds(rows + s, vecs, stride=2 * rows), :]
-        basis[vecs : 2 * vecs, lanes] = three
-        out_ref[s, 0] = three
-    width = (2 * ITERS - 1) * vecs
-    both = dots(basis[...], basis[vecs : 2 * vecs, :])
-    parts = [known_ref[...][:, :width], both[:vecs], both[vecs:]]
-    parts.append(jnp.zeros((vecs, LANE - (2 * ITERS + 1) * vecs), jnp.float32))
-    grams = jnp.concatenate(parts, axis=1)
-    for s in range(rows):
-        out_ref[s, 1] = grams
 
 
 def finish(states, last_ref, turn_ref, start_ref, one_ref, two_ref, eigen_ref, ritz_ref):
@@ -177,9 +159,9 @@
         full = jnp.concatenate([b, jnp.zeros((LANE - b.shape[0], b.shape[1]), jnp.float32)], axis=0)
         return lax.dot_general(a, full, dims, precision=HIGH, preferred_element_type=jnp.float32)
 
-    moments = last_ref[0, 1]
-    for r in range(1, last_ref.shape[0]):
-        moments = moments + last_ref[r, 1]
+    moments = last_ref[0, 2]
+    for c in range(1, last_ref.shape[0]):
+        moments = moments + last_ref[c, 2]
     moments = moments * (1.0 / states)
     hankel = jnp.concatenate(
         [moments] + [pltpu.roll(moments, LANE - j * vecs, 1) for j in range(1, ITERS)], axis=0
@@ -212,7 +194,7 @@
     factors = jnp.concatenate(terms, axis=0)
     for t in range(eigen_ref.shape[1] // LANE):
         lanes = slice(t * LANE, (t + 1) * LANE)
-        basis = [start_ref[:, lanes], one_ref[line(t, vecs, 0), :], two_ref[line(t, vecs, 0), :], last_ref[t, 0]]
+        basis = [start_ref[:, lanes], one_ref[line(t, vecs, 0), :], two_ref[line(t, vecs, 0), :], last_ref[t // 2, t % 2]]
         basis = jnp.concatenate(basis, axis=0)
         high = basis.astype(jnp.bfloat16)
         low = (basis - high.astype(jnp.float32)).astype(jnp.bfloat16)
@@ -238,7 +220,6 @@
         pltpu.VMEM((3 * seg_tiles, vecs, LANE), jnp.float32),
     ]
     sums = [pltpu.VMEM((cols, pair), jnp.float32)]
-    basis = [pltpu.VMEM((2 * vecs, seg_rows), jnp.float32)]
     corner = []
     for r in range(rows):
         for c in range(cols):
@@ -248,9 +229,21 @@
         moved = lax.all_to_all(x.reshape(rows * cols, 3 * LANE), BOTH, 0, 0)
         return moved.reshape(rows * cols * 3, LANE)
 
+    def own_block_piece(x):
+        pairs = seg_tiles // 2
+        own_row = lax.axis_index("row")
+        size = 2 * vecs * 3
+        x = lax.dynamic_slice_in_dim(x, (own_row % pairs) * size, size, 0).reshape(2, vecs, 3, LANE)
+        x = jnp.where(own_row < pairs, x[:, :, 1], x[:, :, 2])
+        return jnp.concatenate([x[0], x[1]], axis=1)
+
+    def to_all(x, axis):
+        count = lax.axis_size(axis)
+        return lax.all_to_all(jnp.broadcast_to(x, (count,) + x.shape), axis, 0, 0)
+
     own_start = lax.dynamic_slice_in_dim(start, own_col * pair, pair, 1)
     index, piece = lax.optimization_barrier((index, lax.ppermute(own_start, BOTH, corner)))
-    block = lax.all_to_all(jnp.broadcast_to(piece, (rows, vecs, pair)), "row", 0, 0)
+    block = to_all(piece, "row")
     mirrored = kernel_call(
         first_mirror, "first_mirror", f32(2 * seg_tiles, vecs, LANE), [SMEM] + [VMEM] * 2, work
     )(index, tiles, start)
@@ -258,23 +251,28 @@
         index, tiles, block, mirrored
     )
     images = []
-    for _ in range(ITERS - 1):
-        given, own = kernel_call(
-            functools.partial(sum_and_deal, rows, cols), "sum_and_deal", (dealt, f32(rows, LANE)), [VMEM], sums
+    for i in range(ITERS - 1):
+        given = kernel_call(
+            functools.partial(sum_and_deal, rows, cols), "sum_and_deal", dealt, [VMEM], sums
         )(swap(sent))
         images.append(swap(given))
-        sent = kernel_call(multiply_next, "multiply_next", dealt, [SMEM] + [VMEM] * 2, work)(
-            index, tiles, images[-1]
-        )
-    shown = kernel_call(
-        functools.partial(sum_and_show, rows, cols), "sum_and_show", f32(cols, 2 * rows, LANE), [VMEM] * 2, sums
-    )(swap(sent), own)
-    shown = lax.all_to_all(shown, "col", 0, 0).reshape(cols * 2 * rows, LANE)
-    known = kernel_call(gram_known, "gram_known", f32(vecs, LANE), [VMEM] * 3, basis)(start, *images)
-    last = kernel_call(
-        functools.partial(gram_last, rows), "gram_last", f32(rows, 2, vecs, LANE), [VMEM] * 2, basis
-    )(known, shown)
-    last = lax.all_to_all(last, "row", 0, 0)
+        if i < ITERS - 2:
+            sent = kernel_call(multiply_next, "multiply_next", dealt, [SMEM] + [VMEM] * 2, work)(
+                index, tiles, images[-1]
+            )
+    direct, mirror = kernel_call(
+        multiply_last, "multiply_last", (f32(cols, vecs, pair), f32(rows, vecs, pair)), [SMEM] + [VMEM] * 2, work
+    )(index, tiles, images[-1])
+
+    direct = jnp.sum(lax.all_to_all(direct, "col", 0, 0), axis=0)
+    direct, mirror = lax.optimization_barrier((direct, mirror))
+    direct = lax.ppermute(direct, BOTH, corner)
+    last = jnp.sum(lax.all_to_all(mirror, "row", 0, 0), axis=0) + direct
+    own = [own_block_piece(image) for image in images]
+    grams = kernel_call(gram, "gram", f32(vecs, LANE), [VMEM] * 4)(piece, *own, last)
+    last = lax.ppermute(last, BOTH, [(to, at) for at, to in corner])
+    grams = jnp.sum(to_all(grams, "row"), axis=0)
+    last = to_all(jnp.stack([last[:, :LANE], last[:, LANE:], grams]), "col")
     turned = jnp.pad(jnp.swapaxes(rotation, 2, 3), ((0, 0),) * 3 + ((0, LANE - vecs),))
     return kernel_call(
         functools.partial(finish, seg_rows * rows), "finish", (f32(vecs, seg_rows), f32(vecs, vecs)), [VMEM] * 5

time: 291 us -> 288 us (0.990)
  blocking collectives: 184 us -> 146 us
  starting transfers between devices: 37.5 us -> 68 us
  waiting for transfers between devices: 35.6 us -> 42.7 us
  local copies, waits for them, and re-layouts: 7.5 us -> 10.5 us
    all_to_all x5 -> x4, blocking collectives: 184 us -> 146 us  [swap(): moved = lax.all_to_all(x.reshape(rows * cols, 3 * LANE), BOTH, 0, 0)]
    all_to_all x3 -> x5, starting transfers between devices: 32.1 us -> 50.8 us  [the longest x3 42.2 us: to_all(): return lax.all_to_all(jnp.broadcast_to(x, (count,) + x.shape), axis, 0, 0)]
    ppermute x0 -> x2, starting transfers between devices: none -> 11.7 us  [the longest x1 7.17 us: body(): last = lax.ppermute(last, BOTH, [(to, at) for at, to in corner])]
    all_to_all x3 -> x5, waiting for transfers between devices: 33.7 us -> 38.4 us  [the longest x3 22.4 us: to_all(): return lax.all_to_all(jnp.broadcast_to(x, (count,) + x.shape), axis, 0, 0)]
    pallas_call x2 -> x1, Pallas kernels: 6.89 us -> 3.69 us  [body(): kernel_call(multiply_next, 'multiply_next', dealt, [SMEM] + [VMEM] * 2, w...]
  transfers between devices with their start and end apart: 4 -> 8, of which waited for: 4 -> 7; matrix products, arithmetic and copies ran while one was open for 0% -> 1% of each run, Pallas kernels for 1% -> 1%
where the time goes in v7:
time: 288 us; the launch traced here: 286 us
  blocking collectives  146 us (51%)
  starting transfers between devices  68 us (24%)
  waiting for transfers between devices  42.7 us (15%)
  Pallas kernels  16.8 us (6%)
  local copies, waits for them, and re-layouts  10.5 us (4%)
    all_to_all x4, blocking collectives, swap(): moved = lax.all_to_all(x.reshape(rows * cols, 3 * LANE), BOTH, 0, 0)  146 us
    all_to_all x3, starting transfers between devices, to_all(): return lax.all_to_all(jnp.broadcast_to(x, (count,) + x.shape), axis, 0, 0)  42.2 us
    all_to_all x3, waiting for transfers between devices, to_all(): return lax.all_to_all(jnp.broadcast_to(x, (count,) + x.shape), axis, 0, 0)  22.4 us
    all_to_all x1, waiting for transfers between devices, body(): last = jnp.sum(lax.all_to_all(mirror, 'row', 0, 0), axis=0) + direct  10.6 us
    ppermute x1, starting transfers between devices, body(): last = lax.ppermute(last, BOTH, [(to, at) for at, to in corner])  7.17 us
  transfers between devices with their start and end apart: 8, of which 7 were waited for; matrix products, arithmetic and copies ran while one was open for 1% of the time, Pallas kernels for 1%

profile of v7, /device:TPU:1, one launch (start us, length us, event | category | flops | bytes accessed | tf_op | source)
XLA Modules:
  0.0 286.5 jit_solution(7230705712001988509)
XLA Ops:
  0.6 0.7 constant_dynamic-slice_fusion.2
  1.4 5.4 %collective-permute-start = (f32[16,256]{1,0:T(8,128)S(1)}, f32[16,256]{1,0:T(8,128)S(1)}, u32[]{:S(2)}, u32[]{:S(2)}) collective-permute-start(f32[16,256]{1,0:T(8,128)S(1)} %constant_dynamic-slice_fusion.2), channel_id=1, source_target_pairs={{0,0},{1,16},{2,32},{3,48},{4,64},{5,80},{6,96},{7,112},{8,128},{9... | collective-permute-start | bytes 49160 | tf_op jit(solution)/shard_map/ppermute | solution.py:245
  7.4 0.7 pad_add_fusion.index_ref
  8.1 1.8 collective-permute-done.zero_ref
  10.0 0.9 broadcast_in_dim.9
  10.8 23.3 %all-to-all-start = ((f32[32,16,256]{2,1,0:T(8,128)}), f32[32,16,256]{2,1,0:T(8,128)}, u32[]{:S(2)}, u32[]{:S(2)}) async-start(f32[32,16,256]{2,1,0:T(8,128)} %broadcast_in_dim.9), calls=%async_computation | async-start | bytes 1048576 | tf_op jit(solution)/shard_map/all_to_all | solution.py:242
  34.2 0.0 copy-start
  34.2 1.9 copy-done
  36.1 0.0 copy-start.8
  36.1 0.9 copy-done.8
  37.0 0.0 copy-start.1
  37.0 1.8 first_mirror.1.mirrored_ref
  38.9 0.0 copy-start.6
  38.9 0.8 copy-done.6
  39.7 11.5 %all-to-all-done.block_ref = f32[32,16,256]{2,1,0:T(8,128)} async-done(((f32[32,16,256]{2,1,0:T(8,128)}), f32[32,16,256]{2,1,0:T(8,128)}, u32[]{:S(2)}, u32[]{:S(2)}) %all-to-all-start) | async-done | bytes 524320 | tf_op jit(solution)/shard_map/all_to_all | solution.py:242
  51.2 0.0 copy-done.1
  51.2 0.0 copy-start.7
  51.2 1.0 copy-done.7
  52.2 3.2 %first_direct.1 = f32[1536,128]{1,0:T(8,128)S(1)} custom-call(s32[193]{0:T(256)S(1)} %pad_add_fusion.index_ref, bf16[96,128,128]{2,1,0:T(8,128)(2,1)S(1)} %bitcast.32, f32[32,16,256]{2,1,0:T(8,128)} %all-to-all-done.block_ref, f32[64,16,128]{2,1,0:T(8,128)S(1)} %copy-done.7), custom_call_target="tpu_custom_call" | custom-call | tf_op jit(solution)/shard_map/first_direct/pallas_call | solution.py:250
  55.4 38.0 %all_to_all.61 = f32[512,1,384]{2,1,0:T(1,128)S(1)} all-to-all(f32[512,1,384]{2,1,0:T(1,128)S(1)} %bitcast.46), channel_id=1, replica_groups=mesh['row'=32,'col'=16] {'row','col'}, dimensions={0} | all-to-all | bytes 1572864 | tf_op jit(solution)/shard_map/all_to_all | solution.py:229
  93.5 0.1 sum_and_deal.2
  93.6 36.3 %all_to_all.62 = f32[512,1,384]{2,1,0:T(1,128)S(1)} all-to-all(f32[512,1,384]{2,1,0:T(1,128)S(1)} %bitcast.43), channel_id=1, replica_groups=mesh['row'=32,'col'=16] {'row','col'}, dimensions={0} | all-to-all | bytes 1572864 | tf_op jit(solution)/shard_map/all_to_all | solution.py:229
  129.9 0.0 copy-start.2
  129.9 3.7 %multiply_next.1 = f32[1536,128]{1,0:T(8,128)S(1)} custom-call(s32[193]{0:T(256)S(1)} %pad_add_fusion.index_ref, bf16[96,128,128]{2,1,0:T(8,128)(2,1)S(1)} %bitcast.33, f32[1536,128]{1,0:T(8,128)S(1)} %bitcast.35), custom_call_target="tpu_custom_call" | custom-call | tf_op jit(solution)/shard_map/multiply_next/pallas_call | solution.py:260
  133.6 35.3 %all_to_all.63 = f32[512,1,384]{2,1,0:T(1,128)S(1)} all-to-all(f32[512,1,384]{2,1,0:T(1,128)S(1)} %bitcast.41), channel_id=1, replica_groups=mesh['row'=32,'col'=16] {'row','col'}, dimensions={0} | all-to-all | bytes 1572864 | tf_op jit(solution)/shard_map/all_to_all | solution.py:229
  169.0 0.0 copy-done.2
  169.0 0.1 sum_and_deal.3
  169.1 36.5 %all_to_all.64 = f32[512,1,384]{2,1,0:T(1,128)S(1)} all-to-all(f32[512,1,384]{2,1,0:T(1,128)S(1)} %bitcast.45), channel_id=1, replica_groups=mesh['row'=32,'col'=16] {'row','col'}, dimensions={0} | all-to-all | bytes 1572864 | tf_op jit(solution)/shard_map/all_to_all | solution.py:229
  205.6 0.0 copy-start.4
  205.6 4.4 %multiply_last.1 = (f32[16,16,256]{2,1,0:T(8,128)}, f32[32,16,256]{2,1,0:T(8,128)S(1)}) custom-call(s32[193]{0:T(256)S(1)} %pad_add_fusion.index_ref, bf16[96,128,128]{2,1,0:T(8,128)(2,1)S(1)} %bitcast.34, f32[1536,128]{1,0:T(8,128)S(1)} %bitcast.38), custom_call_target="tpu_custom_call" | custom-call | tf_op jit(solution)/shard_map/multiply_last/pallas_call | solution.py:263
  210.0 0.0 copy-done.4
  210.0 0.0 copy-start.10
  210.0 0.8 copy-done.10
  210.8 0.0 copy-start.11
  210.8 0.0 copy-start.3
  210.8 0.0 copy-start.9
  210.8 0.0 copy-start.5
  210.8 3.6 %all-to-all-start.5 = ((f32[16,16,256]{2,1,0:T(8,128)}), f32[16,16,256]{2,1,0:T(8,128)S(1)}, u32[]{:S(2)}, u32[]{:S(2)}) async-start(f32[16,16,256]{2,1,0:T(8,128)} %get-tuple-element.10), calls=%async_computation.5 | async-start | bytes 524288 | tf_op jit(solution)/shard_map/all_to_all | solution.py:267
  214.4 0.8 constant_dynamic-slice_fusion.1
  215.3 0.8 constant_dynamic-slice_fusion
  216.1 5.5 %all-to-all-done.5 = f32[16,16,256]{2,1,0:T(8,128)S(1)} async-done(((f32[16,16,256]{2,1,0:T(8,128)}), f32[16,16,256]{2,1,0:T(8,128)S(1)}, u32[]{:S(2)}, u32[]{:S(2)}) %all-to-all-start.5) | async-done | bytes 262176 | tf_op jit(solution)/shard_map/all_to_all | solution.py:267
  221.6 5.0 %all-to-all-start.6 = ((f32[32,16,256]{2,1,0:T(8,128)}), f32[32,16,256]{2,1,0:T(8,128)S(1)}, u32[]{:S(2)}, u32[]{:S(2)}) async-start(f32[32,16,256]{2,1,0:T(8,128)} %copy-done.10), calls=%async_computation.6 | async-start | bytes 1048576 | tf_op jit(solution)/shard_map/all_to_all | solution.py:270
  226.7 4.6 %collective-permute-start.1 = (f32[16,256]{1,0:T(8,128)S(1)}, f32[16,256]{1,0:T(8,128)S(1)}, u32[]{:S(2)}, u32[]{:S(2)}) collective-permute-start(f32[16,256]{1,0:T(8,128)S(1)} %reduce_sum.27), channel_id=1, source_target_pairs={{0,0},{1,16},{2,32},{3,48},{4,64},{5,80},{6,96},{7,112},{8,128},{9... | collective-permute-start | bytes 49160 | tf_op jit(solution)/shard_map/ppermute | solution.py:269
  231.3 10.6 %all-to-all-done.6 = f32[32,16,256]{2,1,0:T(8,128)S(1)} async-done(((f32[32,16,256]{2,1,0:T(8,128)}), f32[32,16,256]{2,1,0:T(8,128)S(1)}, u32[]{:S(2)}, u32[]{:S(2)}) %all-to-all-start.6) | async-done | bytes 524320 | tf_op jit(solution)/shard_map/all_to_all | solution.py:270
  241.9 0.0 collective-permute-done.1
  241.9 0.3 gram.1
  242.2 0.8 broadcast_in_dim.10
  243.0 11.1 %all-to-all-start.7 = ((f32[32,16,128]{2,1,0:T(8,128)}), f32[32,16,128]{2,1,0:T(8,128)S(1)}, u32[]{:S(2)}, u32[]{:S(2)}) async-start(f32[32,16,128]{2,1,0:T(8,128)} %broadcast_in_dim.10), calls=%async_computation.7 | async-start | bytes 524288 | tf_op jit(solution)/shard_map/all_to_all | solution.py:242
  254.1 7.2 %collective-permute-start.2 = (f32[16,256]{1,0:T(8,128)S(1)}, f32[16,256]{1,0:T(8,128)S(1)}, u32[]{:S(2)}, u32[]{:S(2)}) collective-permute-start(f32[16,256]{1,0:T(8,128)S(1)} %add.18.three_ref), channel_id=1, source_target_pairs={{0,0},{16,1},{32,2},{48,3},{64,4},{80,5},{96,6},{112,7},{128,8},{1... | collective-permute-start | bytes 49160 | tf_op jit(solution)/shard_map/ppermute | solution.py:273
  261.3 2.5 collective-permute-done.2
  263.7 2.6 all-to-all-done.7
  266.3 0.8 broadcast_in_dim.11
  267.1 7.7 %all-to-all-start.8 = ((f32[16,3,16,128]{3,2,1,0:T(8,128)}), f32[16,3,16,128]{3,2,1,0:T(8,128)S(1)}, u32[]{:S(2)}, u32[]{:S(2)}) async-start(f32[16,3,16,128]{3,2,1,0:T(8,128)} %broadcast_in_dim.11), calls=%async_computation.8 | async-start | bytes 786432 | tf_op jit(solution)/shard_map/all_to_all | solution.py:242
  274.9 0.0 copy-done.11
  274.9 0.1 copy.31
  275.0 8.3 %all-to-all-done.8.last_ref = f32[16,3,16,128]{3,2,1,0:T(8,128)S(1)} async-done(((f32[16,3,16,128]{3,2,1,0:T(8,128)}), f32[16,3,16,128]{3,2,1,0:T(8,128)S(1)}, u32[]{:S(2)}, u32[]{:S(2)}) %all-to-all-start.8) | async-done | bytes 393248 | tf_op jit(solution)/shard_map/all_to_all | solution.py:242
  283.3 0.0 copy-done.3
  283.3 0.0 copy-done.9
  283.3 0.0 copy-done.5
  283.3 3.2 %finish.1 = (f32[16,4096]{1,0:T(8,128)}, f32[16,16]{1,0:T(8,128)}) custom-call(f32[16,3,16,128]{3,2,1,0:T(8,128)S(1)} %all-to-all-done.8.last_ref, f32[3,3,16,128]{3,2,1,0:T(8,128)S(1)} %pad.4.turn_ref, f32[16,4096]{1,0:T(8,128)S(1)} %copy-done.9, f32[1536,128]{1,0:T(8,128)S(1)} %bitcast.37, f32[1536,128]{1,0:T(8,128)S(1)} %bitcast.40), custom_call_target="tpu_custom_call" | custom-call | tf_op jit(solution)/shard_map/finish/pallas_call | solution.py:277
  (16 shorter events, 0.3 us)
Async XLA Ops:
  1.4 8.6 %collective-permute-start = (f32[16,256]{1,0:T(8,128)S(1)}, f32[16,256]{1,0:T(8,128)S(1)}, u32[]{:S(2)}, u32[]{:S(2)}) collective-permute-start(f32[16,256]{1,0:T(8,128)S(1)} %constant_dynamic-slice_fusion.2), channel_id=1, source_target_pairs={{0,0},{1,16},{2,32},{3,48},{4,64},{5,80},{6,96},{7,112},{8,128},{9... | collective-permute-start | bytes 49160 | tf_op jit(solution)/shard_map/ppermute | solution.py:245
  10.8 40.4 %all-to-all-start = ((f32[32,16,256]{2,1,0:T(8,128)}), f32[32,16,256]{2,1,0:T(8,128)}, u32[]{:S(2)}, u32[]{:S(2)}) async-start(f32[32,16,256]{2,1,0:T(8,128)} %broadcast_in_dim.9), calls=%async_computation | async-start | bytes 1048576 | tf_op jit(solution)/shard_map/all_to_all | solution.py:242
  34.2 1.9 copy-start
  36.1 0.9 copy-start.8
  37.0 14.2 %copy-start.1 = (bf16[1,1,96,128,128]{4,3,2,1,0:T(8,128)(2,1)S(1)}, bf16[1,1,96,128,128]{4,3,2,1,0:T(8,128)(2,1)}, u32[]{:S(2)}) copy-start(bf16[1,1,96,128,128]{4,3,2,1,0:T(8,128)(2,1)} %param.6) | copy-start | bytes 9437188
  38.9 0.8 copy-start.6
  51.2 1.0 copy-start.7
  129.9 39.0 %copy-start.2 = (f32[512,1,384]{2,1,0:T(1,128)}, f32[512,1,384]{2,1,0:T(1,128)S(1)}, u32[]{:S(2)}) copy-start(f32[512,1,384]{2,1,0:T(1,128)S(1)} %all_to_all.62) | copy-start | bytes 2359300
  205.6 4.4 %copy-start.4 = (f32[512,1,384]{2,1,0:T(1,128)}, f32[512,1,384]{2,1,0:T(1,128)S(1)}, u32[]{:S(2)}) copy-start(f32[512,1,384]{2,1,0:T(1,128)S(1)} %all_to_all.64) | copy-start | bytes 2359300
  210.0 0.8 copy-start.10
  210.8 64.1 %copy-start.11 = (f32[3,3,16,16]{3,2,1,0:T(8,128)S(1)}, f32[3,3,16,16]{3,2,1,0:T(8,128)}, u32[]{:S(2)}) copy-start(f32[3,3,16,16]{3,2,1,0:T(8,128)} %param.11) | copy-start | bytes 27652
  210.8 72.5 %copy-start.3 = (f32[512,1,384]{2,1,0:T(1,128)S(1)}, f32[512,1,384]{2,1,0:T(1,128)}, u32[]{:S(2)}) copy-start(f32[512,1,384]{2,1,0:T(1,128)} %copy-done.2) | copy-start | bytes 2359300
  210.8 72.5 %copy-start.9 = (f32[16,4096]{1,0:T(8,128)S(1)}, f32[16,4096]{1,0:T(8,128)}, u32[]{:S(2)}) copy-start(f32[16,4096]{1,0:T(8,128)} %start_ref.1) | copy-start | bytes 786436
  210.8 72.5 %copy-start.5 = (f32[512,1,384]{2,1,0:T(1,128)S(1)}, f32[512,1,384]{2,1,0:T(1,128)}, u32[]{:S(2)}) copy-start(f32[512,1,384]{2,1,0:T(1,128)} %copy-done.4) | copy-start | bytes 2359300
  210.8 10.8 %all-to-all-start.5 = ((f32[16,16,256]{2,1,0:T(8,128)}), f32[16,16,256]{2,1,0:T(8,128)S(1)}, u32[]{:S(2)}, u32[]{:S(2)}) async-start(f32[16,16,256]{2,1,0:T(8,128)} %get-tuple-element.10), calls=%async_computation.5 | async-start | bytes 524288 | tf_op jit(solution)/shard_map/all_to_all | solution.py:267
  221.6 20.2 %all-to-all-start.6 = ((f32[32,16,256]{2,1,0:T(8,128)}), f32[32,16,256]{2,1,0:T(8,128)S(1)}, u32[]{:S(2)}, u32[]{:S(2)}) async-start(f32[32,16,256]{2,1,0:T(8,128)} %copy-done.10), calls=%async_computation.6 | async-start | bytes 1048576 | tf_op jit(solution)/shard_map/all_to_all | solution.py:270
  226.7 15.2 %collective-permute-start.1 = (f32[16,256]{1,0:T(8,128)S(1)}, f32[16,256]{1,0:T(8,128)S(1)}, u32[]{:S(2)}, u32[]{:S(2)}) collective-permute-start(f32[16,256]{1,0:T(8,128)S(1)} %reduce_sum.27), channel_id=1, source_target_pairs={{0,0},{1,16},{2,32},{3,48},{4,64},{5,80},{6,96},{7,112},{8,128},{9... | collective-permute-start | bytes 49160 | tf_op jit(solution)/shard_map/ppermute | solution.py:269
  243.0 23.3 %all-to-all-start.7 = ((f32[32,16,128]{2,1,0:T(8,128)}), f32[32,16,128]{2,1,0:T(8,128)S(1)}, u32[]{:S(2)}, u32[]{:S(2)}) async-start(f32[32,16,128]{2,1,0:T(8,128)} %broadcast_in_dim.10), calls=%async_computation.7 | async-start | bytes 524288 | tf_op jit(solution)/shard_map/all_to_all | solution.py:242
  254.1 9.6 %collective-permute-start.2 = (f32[16,256]{1,0:T(8,128)S(1)}, f32[16,256]{1,0:T(8,128)S(1)}, u32[]{:S(2)}, u32[]{:S(2)}) collective-permute-start(f32[16,256]{1,0:T(8,128)S(1)} %add.18.three_ref), channel_id=1, source_target_pairs={{0,0},{16,1},{32,2},{48,3},{64,4},{80,5},{96,6},{112,7},{128,8},{1... | collective-permute-start | bytes 49160 | tf_op jit(solution)/shard_map/ppermute | solution.py:273
  267.1 16.1 %all-to-all-start.8 = ((f32[16,3,16,128]{3,2,1,0:T(8,128)}), f32[16,3,16,128]{3,2,1,0:T(8,128)S(1)}, u32[]{:S(2)}, u32[]{:S(2)}) async-start(f32[16,3,16,128]{3,2,1,0:T(8,128)} %broadcast_in_dim.11), calls=%async_computation.8 | async-start | bytes 786432 | tf_op jit(solution)/shard_map/all_to_all | solution.py:242

commit v8 on v7

v8 whole, which is shorter than its diff:
```python
import functools

import jax
import jax.numpy as jnp
from jax import lax
from jax.experimental import pallas as pl
from jax.experimental.pallas import tpu as pltpu
from jax.sharding import PartitionSpec as P

ITERS = 3
LANE = 128
GROUP = 32
BOTH = ("row", "col")
HIGH = lax.Precision.HIGHEST
NT = (((1,), (1,)), ((), ()))
NN = (((1,), (0,)), ((), ()))
SMEM = pl.BlockSpec(memory_space=pltpu.SMEM)
VMEM = pl.BlockSpec(memory_space=pltpu.VMEM)


def kernel_call(kernel, name, out, ins, scratch=()):
    return pl.pallas_call(
        kernel,
        name=name,
        out_shape=out,
        in_specs=ins,
        out_specs=jax.tree.map(lambda _: VMEM, out),
        scratch_shapes=scratch,
        compiler_params=pltpu.CompilerParams(vmem_limit_bytes=16 << 20),
    )


def f32(*shape):
    return jax.ShapeDtypeStruct(shape, jnp.float32)


def keep(split, slot, values):
    vecs = values.shape[0]
    high = values.astype(jnp.bfloat16)
    split[slot, 0:vecs, :] = high
    split[slot, vecs : 2 * vecs, :] = (values - high.astype(jnp.float32)).astype(jnp.bfloat16)


def multiply(index_ref, tiles_ref, split, total, direct, mirror):
    seg_tiles = total.shape[0] // 3
    vecs = total.shape[1]
    slots = tiles_ref.shape[0]
    count = index_ref[2 * slots]
    size = GROUP if slots % GROUP == 0 else slots
    total[...] = jnp.zeros_like(total)

    def group(g, carry):
        parts = []
        for j in range(size):
            slot = g * size + j
            row = index_ref[slot]
            col = index_ref[slots + slot] + seg_tiles
            tile = tiles_ref[slot]
            live = slot < count
            for wanted, taken, place, dims in ((direct, col, row, NT), (mirror, row, col, NN)):
                if wanted:
                    part = lax.dot_general(split[taken], tile, dims, preferred_element_type=jnp.float32)
                    parts.append((place, jnp.where(live, part[:vecs] + part[vecs:], 0.0)))
        for place, part in parts:
            total[place] += part
        return carry

    lax.fori_loop(0, (count + (size - 1)) // size, group, 0)


def halves(ref, t):
    return ref.at[t // 2, :, (t % 2) * LANE : (t % 2 + 1) * LANE]


def first_mirror(index_ref, tiles_ref, seg_ref, mirror_ref, split, total):
    seg_tiles = total.shape[0] // 3
    for t in range(seg_tiles):
        keep(split, t, seg_ref[:, t * LANE : (t + 1) * LANE])
    multiply(index_ref, tiles_ref, split, total, False, True)
    for t in range(2 * seg_tiles):
        halves(mirror_ref, t)[...] = total[seg_tiles + t]


def first_direct(index_ref, tiles_ref, block_ref, direct_ref, split, total):
    seg_tiles = total.shape[0] // 3
    for t in range(2 * seg_tiles):
        keep(split, seg_tiles + t, halves(block_ref, t)[...])
    multiply(index_ref, tiles_ref, split, total, True, False)
    for t in range(seg_tiles):
        halves(direct_ref, t)[...] = total[t]


def multiply_both(index_ref, tiles_ref, seg_ref, block_ref, direct_ref, mirror_ref, split, total):
    seg_tiles = total.shape[0] // 3
    for t in range(seg_tiles):
        keep(split, t, halves(seg_ref, t)[...])
    for t in range(2 * seg_tiles):
        keep(split, seg_tiles + t, halves(block_ref, t)[...])
    multiply(index_ref, tiles_ref, split, total, True, True)
    for t in range(seg_tiles):
        halves(direct_ref, t)[...] = total[t]
    for t in range(2 * seg_tiles):
        halves(mirror_ref, t)[...] = total[seg_tiles + t]


def gram(zero_ref, one_ref, two_ref, three_ref, gram_ref):
    vecs = three_ref.shape[0]
    basis = [zero_ref[...], one_ref[...], two_ref[...], three_ref[...]]
    parts = []
    for j in range(ITERS + 1):
        others = jnp.concatenate(basis[j : j + 2], axis=0)
        parts.append(
            lax.dot_general(basis[j], others, NT, precision=HIGH, preferred_element_type=jnp.float32)
        )
    parts.append(jnp.zeros((vecs, LANE - (2 * ITERS + 1) * vecs), jnp.float32))
    gram_ref[...] = jnp.concatenate(parts, axis=1)


def finish(states, last_ref, turn_ref, start_ref, one_ref, two_ref, eigen_ref, ritz_ref):
    vecs = eigen_ref.shape[0]

    def mul(a, b, dims=NN):
        full = jnp.concatenate([b, jnp.zeros((LANE - b.shape[0], b.shape[1]), jnp.float32)], axis=0)
        return lax.dot_general(a, full, dims, precision=HIGH, preferred_element_type=jnp.float32)

    moments = last_ref[0, 2]
    for c in range(1, last_ref.shape[0]):
        moments = moments + last_ref[c, 2]
    moments = moments * (1.0 / states)
    hankel = jnp.concatenate(
        [moments] + [pltpu.roll(moments, LANE - j * vecs, 1) for j in range(1, ITERS)], axis=0
    )
    eye = lax.broadcasted_iota(jnp.int32, (vecs, LANE), 0) == lax.broadcasted_iota(jnp.int32, (vecs, LANE), 1)
    iterate = eye.astype(jnp.float32)
    search = None
    for i in range(ITERS):
        keep_turn, step, past = (turn_ref[i, j] for j in range(3))
        weighted = mul(iterate, hankel) if i else moments
        own = mul(weighted, iterate, NT)
        theta = mul(pltpu.roll(weighted, LANE - vecs, 1), iterate, NT)
        images = mul(pltpu.roll(weighted, LANE - 2 * vecs, 1), iterate, NT)
        terms = jnp.where(eye, images, 0.0) - 2.0 * theta * theta + theta * mul(own, theta)
        spread = jnp.maximum(jnp.sum(terms, axis=0, keepdims=True), 0.0)
        scaled = step / jnp.sqrt(spread + 1e-06)
        residual = pltpu.roll(iterate, vecs, 1) - mul(theta, iterate)
        moved = mul(scaled, residual)
        if search is not None:
            moved = moved - mul(-past, search)
        iterate = moved - mul(-keep_turn, iterate)
        search = moved
    ritz_ref[...] = theta[:, :vecs]
    used = (ITERS + 1) * vecs
    terms = []
    rest = iterate[:, :used]
    for _ in range(3):
        terms.append(rest.astype(jnp.bfloat16))
        rest = rest - terms[-1].astype(jnp.float32)
    factors = jnp.concatenate(terms, axis=0)
    for t in range(eigen_ref.shape[1] // LANE):
        lanes = slice(t * LANE, (t + 1) * LANE)
        basis = [start_ref[:, lanes], halves(one_ref, t)[...], halves(two_ref, t)[...], last_ref[t // 2, t % 2]]
        basis = jnp.concatenate(basis, axis=0)
        high = basis.astype(jnp.bfloat16)
        low = (basis - high.astype(jnp.float32)).astype(jnp.bfloat16)
        large = lax.dot_general(factors, high, NN, preferred_element_type=jnp.float32)
        small = lax.dot_general(factors[: 2 * vecs], low, NN, preferred_element_type=jnp.float32)
        small = small[:vecs] + small[vecs:] + large[2 * vecs :]
        eigen_ref[:, lanes] = large[:vecs] + (large[vecs : 2 * vecs] + small)


def body(tiles, tile_row, tile_col, tile_counts, start, rotation):
    tiles = tiles.reshape(tiles.shape[2:])
    slots = tiles.shape[0]
    vecs, seg_rows = start.shape
    rows = lax.axis_size("row")
    cols = lax.axis_size("col")
    seg_tiles = seg_rows // LANE
    pair = 2 * LANE
    index = jnp.concatenate([tile_row.reshape(slots), tile_col.reshape(slots), tile_counts.reshape(1)])
    own_col = lax.axis_index("col")
    direct_shape, mirror_shape = f32(cols, vecs, pair), f32(rows, vecs, pair)
    work = [
        pltpu.VMEM((3 * seg_tiles, 2 * vecs, LANE), jnp.bfloat16),
        pltpu.VMEM((3 * seg_tiles, vecs, LANE), jnp.float32),
    ]
    corner = []
    for r in range(rows):
        for c in range(cols):
            corner.append((r * cols + c, ((r % 2) * cols + c) * cols + r // 2))
    back = [(to, at) for at, to in corner]

    def to_block(piece):
        return lax.ppermute(piece, BOTH, corner)

    def to_seg(piece):
        return lax.ppermute(piece, BOTH, back)

    def summed(x, axis):
        return jnp.sum(lax.all_to_all(x, axis, 0, 0), axis=0)

    def to_all(x, axis):
        count = lax.axis_size(axis)
        return lax.all_to_all(jnp.broadcast_to(x, (count,) + x.shape), axis, 0, 0)

    def both(seg, block):
        return kernel_call(
            multiply_both, "multiply_both", (direct_shape, mirror_shape), [SMEM] + [VMEM] * 3, work
        )(index, tiles, seg, block)

    zero = to_block(lax.dynamic_slice_in_dim(start, own_col * pair, pair, 1))
    mirror = kernel_call(first_mirror, "first_mirror", mirror_shape, [SMEM] + [VMEM] * 2, work)(index, tiles, start)
    mirror, zero = lax.optimization_barrier((summed(mirror, "row"), zero))
    block, mirror_back = lax.optimization_barrier((to_all(zero, "row"), to_seg(mirror)))
    direct = kernel_call(first_direct, "first_direct", direct_shape, [SMEM] + [VMEM] * 2, work)(index, tiles, block)
    direct = summed(direct, "col")
    one_seg = to_all(direct + mirror_back, "col")
    one_seg, one = lax.optimization_barrier((one_seg, mirror + to_block(direct)))
    direct, mirror = both(one_seg, to_all(one, "row"))

    direct, mirror = lax.optimization_barrier((summed(direct, "col"), mirror))
    two = to_block(direct) + summed(mirror, "row")
    block, two_seg = lax.optimization_barrier((to_all(two, "row"), to_seg(two)))
    two_seg = to_all(two_seg, "col")
    direct, mirror = both(two_seg, block)

    direct, mirror = lax.optimization_barrier((summed(direct, "col"), mirror))
    three = to_block(direct) + summed(mirror, "row")
    grams = kernel_call(gram, "gram", f32(vecs, LANE), [VMEM] * 4)(zero, one, two, three)
    grams = jnp.sum(to_all(grams, "row"), axis=0)
    three = to_seg(three)
    last = to_all(jnp.stack([three[:, :LANE], three[:, LANE:], grams]), "col")
    turned = jnp.pad(jnp.swapaxes(rotation, 2, 3), ((0, 0),) * 3 + ((0, LANE - vecs),))
    return kernel_call(
        functools.partial(finish, seg_rows * rows), "finish", (f32(vecs, seg_rows), f32(vecs, vecs)), [VMEM] * 5
    )(last, turned, start, one_seg, two_seg)


def solution(mesh):
    return jax.shard_map(
        body,
        mesh=mesh,
        in_specs=(
            P("row", "col", None, None, None),
            P("row", "col", None),
            P("row", "col", None),
            P("row", "col"),
            P(None, "row"),
            P(),
        ),
        out_specs=(P(None, "row"), P()),
        check_vma=False,
    )
```

time: 288 us -> 300 us (1.042)
  blocking collectives: 146 us -> 92.8 us
  starting transfers between devices: 68 us -> 108 us
  waiting for transfers between devices: 42.7 us -> 71.3 us
  Pallas kernels: 16.8 us -> 10.4 us
  other arithmetic: 0.88 us -> 5 us
    all_to_all x4 -> x5, blocking collectives: 146 us -> 92.8 us  [the longest x3 50.3 us: summed(): return jnp.sum(lax.all_to_all(x, axis, 0, 0), axis=0)]
    all_to_all x2 -> x3, starting transfers between devices: 8.62 us -> 30.9 us  [summed(): return jnp.sum(lax.all_to_all(x, axis, 0, 0), axis=0)]
    all_to_all x2 -> x3, waiting for transfers between devices: 16 us -> 36.7 us  [summed(): return jnp.sum(lax.all_to_all(x, axis, 0, 0), axis=0)]
    ppermute x3 -> x7, starting transfers between devices: 17.1 us -> 37.5 us  [the longest x3 20.6 us: to_seg(): return lax.ppermute(piece, BOTH, back)]
    ppermute x3 -> x7, waiting for transfers between devices: 4.28 us -> 12.5 us  [the longest x3 10.3 us: to_seg(): return lax.ppermute(piece, BOTH, back)]
    pallas_call x7 -> x5, Pallas kernels: 13.6 us -> 7.17 us  [the longest x2 4.02 us: both(): kernel_call(multiply_both, 'multiply_both', (direct_shape, mirror_shape),...]
    reduce_sum x2 -> x6, other arithmetic: 0.07 us -> 4.19 us  [summed(): return jnp.sum(lax.all_to_all(x, axis, 0, 0), axis=0)]
    all_to_all x3 -> x5, starting transfers between devices: 42.2 us -> 39.7 us  [to_all(): return lax.all_to_all(jnp.broadcast_to(x, (count,) + x.shape), axis, 0, 0)]
  transfers between devices with their start and end apart: 8 -> 15, of which waited for: 7 -> 12; matrix products, arithmetic and copies ran while one was open for 1% -> 1% of each run, Pallas kernels for 1% -> 0%
where the time goes in v8:
time: 300 us; the launch traced here: 298 us
  starting transfers between devices  108 us (36%)
  blocking collectives  92.8 us (31%)
  waiting for transfers between devices  71.3 us (24%)
  Pallas kernels  10.4 us (3%)
  local copies, waits for them, and re-layouts  9.36 us (3%)
  other arithmetic  5 us (2%)
    all_to_all x3, blocking collectives, summed(): return jnp.sum(lax.all_to_all(x, axis, 0, 0), axis=0)  50.3 us
    all_to_all x2, blocking collectives, to_all(): return lax.all_to_all(jnp.broadcast_to(x, (count,) + x.shape), axis, 0, 0)  42.4 us
    all_to_all x5, starting transfers between devices, to_all(): return lax.all_to_all(jnp.broadcast_to(x, (count,) + x.shape), axis, 0, 0)  39.7 us
    all_to_all x3, waiting for transfers between devices, summed(): return jnp.sum(lax.all_to_all(x, axis, 0, 0), axis=0)  36.7 us
    all_to_all x3, starting transfers between devices, summed(): return jnp.sum(lax.all_to_all(x, axis, 0, 0), axis=0)  30.9 us
    all_to_all x5, waiting for transfers between devices, to_all(): return lax.all_to_all(jnp.broadcast_to(x, (count,) + x.shape), axis, 0, 0)  22.1 us
    ppermute x3, starting transfers between devices, to_seg(): return lax.ppermute(piece, BOTH, back)  20.6 us
    ppermute x4, starting transfers between devices, to_block(): return lax.ppermute(piece, BOTH, corner)  16.9 us
  transfers between devices with their start and end apart: 15, of which 12 were waited for; matrix products, arithmetic and copies ran while one was open for 1% of the time, Pallas kernels for 0%

profile of v8, /device:TPU:1, one launch (start us, length us, event | category | flops | bytes accessed | tf_op | source)
XLA Modules:
  0.0 298.4 jit_solution(541409525210220779)
XLA Ops:
  1.3 0.7 pad_add_fusion.index_ref
  2.0 1.9 copy-done
  3.9 0.9 copy-done.5
  4.9 1.1 first_mirror.1
  5.9 0.0 copy-start.4
  5.9 0.8 copy-done.4
  6.7 17.4 %all-to-all-start = ((f32[32,16,256]{2,1,0:T(8,128)}), f32[32,16,256]{2,1,0:T(8,128)}, u32[]{:S(2)}, u32[]{:S(2)}) async-start(f32[32,16,256]{2,1,0:T(8,128)} %copy-done.4), calls=%async_computation | async-start | bytes 1048576 | tf_op jit(solution)/shard_map/all_to_all | solution.py:199
  24.2 3.8 %collective-permute-start = (f32[16,256]{1,0:T(8,128)S(1)}, f32[16,256]{1,0:T(8,128)S(1)}, u32[]{:S(2)}, u32[]{:S(2)}) collective-permute-start(f32[16,256]{1,0:T(8,128)S(1)} %constant_dynamic-slice_fusion), channel_id=1, source_target_pairs={{0,0},{1,16},{2,32},{3,48},{4,64},{5,80},{6,96},{7,112},{8,128},{9... | collective-permute-start | bytes 49160 | tf_op jit(solution)/shard_map/ppermute | solution.py:193
  28.0 15.5 %all-to-all-done = f32[32,16,256]{2,1,0:T(8,128)} async-done(((f32[32,16,256]{2,1,0:T(8,128)}), f32[32,16,256]{2,1,0:T(8,128)}, u32[]{:S(2)}, u32[]{:S(2)}) %all-to-all-start) | async-done | bytes 524320 | tf_op jit(solution)/shard_map/all_to_all | solution.py:199
  43.5 1.1 reduce_sum.63
  44.6 0.0 collective-permute-done.zero_ref
  44.6 0.9 broadcast_in_dim.21
  45.5 6.4 %all-to-all-start.1 = ((f32[32,16,256]{2,1,0:T(8,128)}), f32[32,16,256]{2,1,0:T(8,128)}, u32[]{:S(2)}, u32[]{:S(2)}) async-start(f32[32,16,256]{2,1,0:T(8,128)} %broadcast_in_dim.21), calls=%async_computation.1 | async-start | bytes 1048576 | tf_op jit(solution)/shard_map/all_to_all | solution.py:203
  51.8 6.4 %collective-permute-start.1 = (f32[16,256]{1,0:T(8,128)S(1)}, f32[16,256]{1,0:T(8,128)S(1)}, u32[]{:S(2)}, u32[]{:S(2)}) collective-permute-start(f32[16,256]{1,0:T(8,128)S(1)} %reduce_sum.63), channel_id=1, source_target_pairs={{0,0},{16,1},{32,2},{48,3},{64,4},{80,5},{96,6},{112,7},{128,8},{1... | collective-permute-start | bytes 49160 | tf_op jit(solution)/shard_map/ppermute | solution.py:196
  58.2 4.7 %collective-permute-done.1 = f32[16,256]{1,0:T(8,128)S(1)} collective-permute-done((f32[16,256]{1,0:T(8,128)S(1)}, f32[16,256]{1,0:T(8,128)S(1)}, u32[]{:S(2)}, u32[]{:S(2)}) %collective-permute-start.1) | collective-permute-done | bytes 16416 | tf_op jit(solution)/shard_map/ppermute | solution.py:196
  62.9 3.5 %all-to-all-done.1.block_ref = f32[32,16,256]{2,1,0:T(8,128)} async-done(((f32[32,16,256]{2,1,0:T(8,128)}), f32[32,16,256]{2,1,0:T(8,128)}, u32[]{:S(2)}, u32[]{:S(2)}) %all-to-all-start.1) | async-done | bytes 524320 | tf_op jit(solution)/shard_map/all_to_all | solution.py:203
  66.4 0.0 copy-done.1
  66.4 1.8 first_direct.1
  68.2 18.5 %all_to_all.65 = f32[16,16,256]{2,1,0:T(8,128)} all-to-all(f32[16,16,256]{2,1,0:T(8,128)S(1)} %first_direct.1), channel_id=1, replica_groups=mesh['row'=32,'col'=16] {'col'}, dimensions={0} | all-to-all | bytes 524288 | tf_op jit(solution)/shard_map/all_to_all | solution.py:199
  86.7 1.0 reduce_sum.64
  87.7 0.7 broadcast_in_dim.22
  88.4 4.3 %all-to-all-start.3 = ((f32[16,16,256]{2,1,0:T(8,128)}), f32[16,16,256]{2,1,0:T(8,128)S(1)}, u32[]{:S(2)}, u32[]{:S(2)}) async-start(f32[16,16,256]{2,1,0:T(8,128)} %broadcast_in_dim.22), calls=%async_computation.3 | async-start | bytes 524288 | tf_op jit(solution)/shard_map/all_to_all | solution.py:203
  92.7 4.1 %collective-permute-start.2 = (f32[16,256]{1,0:T(8,128)S(1)}, f32[16,256]{1,0:T(8,128)S(1)}, u32[]{:S(2)}, u32[]{:S(2)}) collective-permute-start(f32[16,256]{1,0:T(8,128)S(1)} %reduce_sum.64), channel_id=1, source_target_pairs={{0,0},{1,16},{2,32},{3,48},{4,64},{5,80},{6,96},{7,112},{8,128},{9... | collective-permute-start | bytes 49160 | tf_op jit(solution)/shard_map/ppermute | solution.py:193
  96.8 2.2 collective-permute-done.2
  99.0 1.0 all-to-all-done.3.seg_ref.one_ref
  100.0 28.2 %all_to_all.66.block_ref = f32[32,16,256]{2,1,0:T(8,128)S(1)} all-to-all(f32[32,16,256]{2,1,0:T(8,128)S(1)} %broadcast_in_dim.23), channel_id=1, replica_groups=mesh['row'=32,'col'=16] {'row'}, dimensions={0} | all-to-all | bytes 1048576 | tf_op jit(solution)/shard_map/all_to_all | solution.py:203
  128.3 1.7 multiply_both.2
  130.0 0.0 copy-start.8
  130.0 0.8 copy-done.8
  130.8 19.5 %all_to_all.67 = f32[16,16,256]{2,1,0:T(8,128)} all-to-all(f32[16,16,256]{2,1,0:T(8,128)S(1)} %get-tuple-element.24), channel_id=1, replica_groups=mesh['row'=32,'col'=16] {'col'}, dimensions={0} | all-to-all | bytes 524288 | tf_op jit(solution)/shard_map/all_to_all | solution.py:199
  150.3 1.0 reduce_sum.65
  151.3 5.5 %all-to-all-start.6 = ((f32[32,16,256]{2,1,0:T(8,128)}), f32[32,16,256]{2,1,0:T(8,128)}, u32[]{:S(2)}, u32[]{:S(2)}) async-start(f32[32,16,256]{2,1,0:T(8,128)} %copy-done.8), calls=%async_computation.6 | async-start | bytes 1048576 | tf_op jit(solution)/shard_map/all_to_all | solution.py:199
  156.8 4.5 %collective-permute-start.3 = (f32[16,256]{1,0:T(8,128)S(1)}, f32[16,256]{1,0:T(8,128)S(1)}, u32[]{:S(2)}, u32[]{:S(2)}) collective-permute-start(f32[16,256]{1,0:T(8,128)S(1)} %reduce_sum.65), channel_id=1, source_target_pairs={{0,0},{1,16},{2,32},{3,48},{4,64},{5,80},{6,96},{7,112},{8,128},{9... | collective-permute-start | bytes 49160 | tf_op jit(solution)/shard_map/ppermute | solution.py:193
  161.3 10.6 %all-to-all-done.6 = f32[32,16,256]{2,1,0:T(8,128)} async-done(((f32[32,16,256]{2,1,0:T(8,128)}), f32[32,16,256]{2,1,0:T(8,128)}, u32[]{:S(2)}, u32[]{:S(2)}) %all-to-all-start.6) | async-done | bytes 524320 | tf_op jit(solution)/shard_map/all_to_all | solution.py:199
  171.9 1.1 reduce_sum.66
  173.0 0.0 collective-permute-done.3
  173.0 0.9 broadcast_in_dim.24
  173.9 10.2 %all-to-all-start.7 = ((f32[32,16,256]{2,1,0:T(8,128)}), f32[32,16,256]{2,1,0:T(8,128)}, u32[]{:S(2)}, u32[]{:S(2)}) async-start(f32[32,16,256]{2,1,0:T(8,128)} %broadcast_in_dim.24), calls=%async_computation.7 | async-start | bytes 1048576 | tf_op jit(solution)/shard_map/all_to_all | solution.py:203
  184.1 7.1 %collective-permute-start.4 = (f32[16,256]{1,0:T(8,128)S(1)}, f32[16,256]{1,0:T(8,128)S(1)}, u32[]{:S(2)}, u32[]{:S(2)}) collective-permute-start(f32[16,256]{1,0:T(8,128)S(1)} %add.20.two_ref), channel_id=1, source_target_pairs={{0,0},{16,1},{32,2},{48,3},{64,4},{80,5},{96,6},{112,7},{128,8},{1... | collective-permute-start | bytes 49160 | tf_op jit(solution)/shard_map/ppermute | solution.py:196
  191.2 3.3 %collective-permute-done.4 = f32[16,256]{1,0:T(8,128)S(1)} collective-permute-done((f32[16,256]{1,0:T(8,128)S(1)}, f32[16,256]{1,0:T(8,128)S(1)}, u32[]{:S(2)}, u32[]{:S(2)}) %collective-permute-start.4) | collective-permute-done | bytes 16416 | tf_op jit(solution)/shard_map/ppermute | solution.py:196
  194.5 6.5 %all-to-all-done.7.block_ref = f32[32,16,256]{2,1,0:T(8,128)} async-done(((f32[32,16,256]{2,1,0:T(8,128)}), f32[32,16,256]{2,1,0:T(8,128)}, u32[]{:S(2)}, u32[]{:S(2)}) %all-to-all-start.7) | async-done | bytes 524320 | tf_op jit(solution)/shard_map/all_to_all | solution.py:203
  201.0 14.2 %all_to_all.68.seg_ref.two_ref = f32[16,16,256]{2,1,0:T(8,128)S(1)} all-to-all(f32[16,16,256]{2,1,0:T(8,128)S(1)} %broadcast_in_dim.25), channel_id=1, replica_groups=mesh['row'=32,'col'=16] {'col'}, dimensions={0} | all-to-all | bytes 524288 | tf_op jit(solution)/shard_map/all_to_all | solution.py:203
  215.2 2.3 multiply_both.3
  217.5 0.0 copy-done.2
  217.5 0.0 copy-start.7
  217.5 0.8 copy-done.7
  218.3 12.3 %all_to_all.69 = f32[16,16,256]{2,1,0:T(8,128)S(1)} all-to-all(f32[16,16,256]{2,1,0:T(8,128)S(1)} %get-tuple-element.30), channel_id=1, replica_groups=mesh['row'=32,'col'=16] {'col'}, dimensions={0} | all-to-all | bytes 524288 | tf_op jit(solution)/shard_map/all_to_all | solution.py:199
  230.7 8.0 %all-to-all-start.10 = ((f32[32,16,256]{2,1,0:T(8,128)}), f32[32,16,256]{2,1,0:T(8,128)S(1)}, u32[]{:S(2)}, u32[]{:S(2)}) async-start(f32[32,16,256]{2,1,0:T(8,128)} %copy-done.7), calls=%async_computation.10 | async-start | bytes 1048576 | tf_op jit(solution)/shard_map/all_to_all | solution.py:199
  238.6 4.6 %collective-permute-start.5 = (f32[16,256]{1,0:T(8,128)S(1)}, f32[16,256]{1,0:T(8,128)S(1)}, u32[]{:S(2)}, u32[]{:S(2)}) collective-permute-start(f32[16,256]{1,0:T(8,128)S(1)} %reduce_sum.67), channel_id=1, source_target_pairs={{0,0},{1,16},{2,32},{3,48},{4,64},{5,80},{6,96},{7,112},{8,128},{9... | collective-permute-start | bytes 49160 | tf_op jit(solution)/shard_map/ppermute | solution.py:193
  243.2 10.5 %all-to-all-done.10 = f32[32,16,256]{2,1,0:T(8,128)S(1)} async-done(((f32[32,16,256]{2,1,0:T(8,128)}), f32[32,16,256]{2,1,0:T(8,128)S(1)}, u32[]{:S(2)}, u32[]{:S(2)}) %all-to-all-start.10) | async-done | bytes 524320 | tf_op jit(solution)/shard_map/all_to_all | solution.py:199
  253.8 0.0 collective-permute-done.5
  253.8 0.3 gram.1
  254.1 0.8 broadcast_in_dim.26
  254.9 11.2 %all-to-all-start.11 = ((f32[32,16,128]{2,1,0:T(8,128)}), f32[32,16,128]{2,1,0:T(8,128)S(1)}, u32[]{:S(2)}, u32[]{:S(2)}) async-start(f32[32,16,128]{2,1,0:T(8,128)} %broadcast_in_dim.26), calls=%async_computation.11 | async-start | bytes 524288 | tf_op jit(solution)/shard_map/all_to_all | solution.py:203
  266.0 7.2 %collective-permute-start.6 = (f32[16,256]{1,0:T(8,128)S(1)}, f32[16,256]{1,0:T(8,128)S(1)}, u32[]{:S(2)}, u32[]{:S(2)}) collective-permute-start(f32[16,256]{1,0:T(8,128)S(1)} %add.21.three_ref), channel_id=1, source_target_pairs={{0,0},{16,1},{32,2},{48,3},{64,4},{80,5},{96,6},{112,7},{128,8},{1... | collective-permute-start | bytes 49160 | tf_op jit(solution)/shard_map/ppermute | solution.py:196
  273.2 2.4 collective-permute-done.6
  275.5 2.8 all-to-all-done.11
  278.4 0.8 broadcast_in_dim.27
  279.2 7.6 %all-to-all-start.12 = ((f32[16,3,16,128]{3,2,1,0:T(8,128)}), f32[16,3,16,128]{3,2,1,0:T(8,128)S(1)}, u32[]{:S(2)}, u32[]{:S(2)}) async-start(f32[16,3,16,128]{3,2,1,0:T(8,128)} %broadcast_in_dim.27), calls=%async_computation.12 | async-start | bytes 786432 | tf_op jit(solution)/shard_map/all_to_all | solution.py:203
  286.8 0.0 copy-done.9
  286.8 0.1 copy.9
  286.9 8.3 %all-to-all-done.12.last_ref = f32[16,3,16,128]{3,2,1,0:T(8,128)S(1)} async-done(((f32[16,3,16,128]{3,2,1,0:T(8,128)}), f32[16,3,16,128]{3,2,1,0:T(8,128)S(1)}, u32[]{:S(2)}, u32[]{:S(2)}) %all-to-all-start.12) | async-done | bytes 393248 | tf_op jit(solution)/shard_map/all_to_all | solution.py:203
  295.2 0.0 copy-done.3
  295.2 3.2 %finish.1 = (f32[16,4096]{1,0:T(8,128)}, f32[16,16]{1,0:T(8,128)}) custom-call(f32[16,3,16,128]{3,2,1,0:T(8,128)S(1)} %all-to-all-done.12.last_ref, f32[3,3,16,128]{3,2,1,0:T(8,128)S(1)} %pad.4.turn_ref, f32[16,4096]{1,0:T(8,128)S(1)} %copy-done.6, f32[16,16,256]{2,1,0:T(8,128)S(1)} %all-to-all-done.3.seg_ref.one_ref, f32[16,16,256]{2,1,0:T(8,128)S(1)} %copy-done.3), custom_call_target="tpu_custom_call" | custom-call | tf_op jit(solution)/shard_map/finish/pallas_call | solution.py:233
  (21 shorter events, 0.2 us)
Async XLA Ops:
  2.0 1.9 copy-start
  3.9 0.9 copy-start.5
  4.9 61.5 %copy-start.1 = (bf16[1,1,96,128,128]{4,3,2,1,0:T(8,128)(2,1)S(1)}, bf16[1,1,96,128,128]{4,3,2,1,0:T(8,128)(2,1)}, u32[]{:S(2)}) copy-start(bf16[1,1,96,128,128]{4,3,2,1,0:T(8,128)(2,1)} %param.6) | copy-start | bytes 9437188
  5.9 0.8 copy-start.4
  6.7 36.8 %all-to-all-start = ((f32[32,16,256]{2,1,0:T(8,128)}), f32[32,16,256]{2,1,0:T(8,128)}, u32[]{:S(2)}, u32[]{:S(2)}) async-start(f32[32,16,256]{2,1,0:T(8,128)} %copy-done.4), calls=%async_computation | async-start | bytes 1048576 | tf_op jit(solution)/shard_map/all_to_all | solution.py:199
  24.2 20.4 %collective-permute-start = (f32[16,256]{1,0:T(8,128)S(1)}, f32[16,256]{1,0:T(8,128)S(1)}, u32[]{:S(2)}, u32[]{:S(2)}) collective-permute-start(f32[16,256]{1,0:T(8,128)S(1)} %constant_dynamic-slice_fusion), channel_id=1, source_target_pairs={{0,0},{1,16},{2,32},{3,48},{4,64},{5,80},{6,96},{7,112},{8,128},{9... | collective-permute-start | bytes 49160 | tf_op jit(solution)/shard_map/ppermute | solution.py:193
  45.5 20.9 %all-to-all-start.1 = ((f32[32,16,256]{2,1,0:T(8,128)}), f32[32,16,256]{2,1,0:T(8,128)}, u32[]{:S(2)}, u32[]{:S(2)}) async-start(f32[32,16,256]{2,1,0:T(8,128)} %broadcast_in_dim.21), calls=%async_computation.1 | async-start | bytes 1048576 | tf_op jit(solution)/shard_map/all_to_all | solution.py:203
  51.8 11.0 %collective-permute-start.1 = (f32[16,256]{1,0:T(8,128)S(1)}, f32[16,256]{1,0:T(8,128)S(1)}, u32[]{:S(2)}, u32[]{:S(2)}) collective-permute-start(f32[16,256]{1,0:T(8,128)S(1)} %reduce_sum.63), channel_id=1, source_target_pairs={{0,0},{16,1},{32,2},{48,3},{64,4},{80,5},{96,6},{112,7},{128,8},{1... | collective-permute-start | bytes 49160 | tf_op jit(solution)/shard_map/ppermute | solution.py:196
  88.4 11.5 %all-to-all-start.3 = ((f32[16,16,256]{2,1,0:T(8,128)}), f32[16,16,256]{2,1,0:T(8,128)S(1)}, u32[]{:S(2)}, u32[]{:S(2)}) async-start(f32[16,16,256]{2,1,0:T(8,128)} %broadcast_in_dim.22), calls=%async_computation.3 | async-start | bytes 524288 | tf_op jit(solution)/shard_map/all_to_all | solution.py:203
  92.7 6.2 %collective-permute-start.2 = (f32[16,256]{1,0:T(8,128)S(1)}, f32[16,256]{1,0:T(8,128)S(1)}, u32[]{:S(2)}, u32[]{:S(2)}) collective-permute-start(f32[16,256]{1,0:T(8,128)S(1)} %reduce_sum.64), channel_id=1, source_target_pairs={{0,0},{1,16},{2,32},{3,48},{4,64},{5,80},{6,96},{7,112},{8,128},{9... | collective-permute-start | bytes 49160 | tf_op jit(solution)/shard_map/ppermute | solution.py:193
  130.0 0.8 copy-start.8
  151.3 20.6 %all-to-all-start.6 = ((f32[32,16,256]{2,1,0:T(8,128)}), f32[32,16,256]{2,1,0:T(8,128)}, u32[]{:S(2)}, u32[]{:S(2)}) async-start(f32[32,16,256]{2,1,0:T(8,128)} %copy-done.8), calls=%async_computation.6 | async-start | bytes 1048576 | tf_op jit(solution)/shard_map/all_to_all | solution.py:199
  156.8 16.2 %collective-permute-start.3 = (f32[16,256]{1,0:T(8,128)S(1)}, f32[16,256]{1,0:T(8,128)S(1)}, u32[]{:S(2)}, u32[]{:S(2)}) collective-permute-start(f32[16,256]{1,0:T(8,128)S(1)} %reduce_sum.65), channel_id=1, source_target_pairs={{0,0},{1,16},{2,32},{3,48},{4,64},{5,80},{6,96},{7,112},{8,128},{9... | collective-permute-start | bytes 49160 | tf_op jit(solution)/shard_map/ppermute | solution.py:193
  173.9 27.1 %all-to-all-start.7 = ((f32[32,16,256]{2,1,0:T(8,128)}), f32[32,16,256]{2,1,0:T(8,128)}, u32[]{:S(2)}, u32[]{:S(2)}) async-start(f32[32,16,256]{2,1,0:T(8,128)} %broadcast_in_dim.24), calls=%async_computation.7 | async-start | bytes 1048576 | tf_op jit(solution)/shard_map/all_to_all | solution.py:203
  184.1 10.3 %collective-permute-start.4 = (f32[16,256]{1,0:T(8,128)S(1)}, f32[16,256]{1,0:T(8,128)S(1)}, u32[]{:S(2)}, u32[]{:S(2)}) collective-permute-start(f32[16,256]{1,0:T(8,128)S(1)} %add.20.two_ref), channel_id=1, source_target_pairs={{0,0},{16,1},{32,2},{48,3},{64,4},{80,5},{96,6},{112,7},{128,8},{1... | collective-permute-start | bytes 49160 | tf_op jit(solution)/shard_map/ppermute | solution.py:196
  215.2 2.3 copy-start.2
  217.5 0.8 copy-start.7
  218.3 68.5 %copy-start.9 = (f32[3,3,16,16]{3,2,1,0:T(8,128)S(1)}, f32[3,3,16,16]{3,2,1,0:T(8,128)}, u32[]{:S(2)}) copy-start(f32[3,3,16,16]{3,2,1,0:T(8,128)} %param.11) | copy-start | bytes 27652
  218.3 76.9 %copy-start.6 = (f32[16,4096]{1,0:T(8,128)S(1)}, f32[16,4096]{1,0:T(8,128)}, u32[]{:S(2)}) copy-start(f32[16,4096]{1,0:T(8,128)} %start_ref.1) | copy-start | bytes 786436
  218.3 76.9 %copy-start.3 = (f32[16,16,256]{2,1,0:T(8,128)S(1)}, f32[16,16,256]{2,1,0:T(8,128)}, u32[]{:S(2)}) copy-start(f32[16,16,256]{2,1,0:T(8,128)} %copy-done.2) | copy-start | bytes 786436
  230.7 23.1 %all-to-all-start.10 = ((f32[32,16,256]{2,1,0:T(8,128)}), f32[32,16,256]{2,1,0:T(8,128)S(1)}, u32[]{:S(2)}, u32[]{:S(2)}) async-start(f32[32,16,256]{2,1,0:T(8,128)} %copy-done.7), calls=%async_computation.10 | async-start | bytes 1048576 | tf_op jit(solution)/shard_map/all_to_all | solution.py:199
  238.6 15.2 %collective-permute-start.5 = (f32[16,256]{1,0:T(8,128)S(1)}, f32[16,256]{1,0:T(8,128)S(1)}, u32[]{:S(2)}, u32[]{:S(2)}) collective-permute-start(f32[16,256]{1,0:T(8,128)S(1)} %reduce_sum.67), channel_id=1, source_target_pairs={{0,0},{1,16},{2,32},{3,48},{4,64},{5,80},{6,96},{7,112},{8,128},{9... | collective-permute-start | bytes 49160 | tf_op jit(solution)/shard_map/ppermute | solution.py:193
  254.9 23.5 %all-to-all-start.11 = ((f32[32,16,128]{2,1,0:T(8,128)}), f32[32,16,128]{2,1,0:T(8,128)S(1)}, u32[]{:S(2)}, u32[]{:S(2)}) async-start(f32[32,16,128]{2,1,0:T(8,128)} %broadcast_in_dim.26), calls=%async_computation.11 | async-start | bytes 524288 | tf_op jit(solution)/shard_map/all_to_all | solution.py:203
  266.0 9.5 %collective-permute-start.6 = (f32[16,256]{1,0:T(8,128)S(1)}, f32[16,256]{1,0:T(8,128)S(1)}, u32[]{:S(2)}, u32[]{:S(2)}) collective-permute-start(f32[16,256]{1,0:T(8,128)S(1)} %add.21.three_ref), channel_id=1, source_target_pairs={{0,0},{16,1},{32,2},{48,3},{64,4},{80,5},{96,6},{112,7},{128,8},{1... | collective-permute-start | bytes 49160 | tf_op jit(solution)/shard_map/ppermute | solution.py:196
  279.2 16.1 %all-to-all-start.12 = ((f32[16,3,16,128]{3,2,1,0:T(8,128)}), f32[16,3,16,128]{3,2,1,0:T(8,128)S(1)}, u32[]{:S(2)}, u32[]{:S(2)}) async-start(f32[16,3,16,128]{3,2,1,0:T(8,128)} %broadcast_in_dim.27), calls=%async_computation.12 | async-start | bytes 786432 | tf_op jit(solution)/shard_map/all_to_all | solution.py:203

commit v9 on v7

--- a/solution.py
+++ b/solution.py
@@ -229,12 +229,13 @@
         moved = lax.all_to_all(x.reshape(rows * cols, 3 * LANE), BOTH, 0, 0)
         return moved.reshape(rows * cols * 3, LANE)
 
+    own_row = lax.axis_index("row")
+    pairs = seg_tiles // 2
+    size = 2 * vecs * 3
+
     def own_block_piece(x):
-        pairs = seg_tiles // 2
-        own_row = lax.axis_index("row")
-        size = 2 * vecs * 3
-        x = lax.dynamic_slice_in_dim(x, (own_row % pairs) * size, size, 0).reshape(2, vecs, 3, LANE)
-        x = jnp.where(own_row < pairs, x[:, :, 1], x[:, :, 2])
+        x = lax.dynamic_slice_in_dim(x, place, size, 0).reshape(2, vecs, 3, LANE)
+        x = jnp.where(low, x[:, :, 1], x[:, :, 2])
         return jnp.concatenate([x[0], x[1]], axis=1)
 
     def to_all(x, axis):
@@ -242,7 +243,9 @@
         return lax.all_to_all(jnp.broadcast_to(x, (count,) + x.shape), axis, 0, 0)
 
     own_start = lax.dynamic_slice_in_dim(start, own_col * pair, pair, 1)
-    index, piece = lax.optimization_barrier((index, lax.ppermute(own_start, BOTH, corner)))
+    piece = lax.ppermute(own_start, BOTH, corner)
+    place = (own_row % pairs * size).astype(jnp.uint32)
+    index, piece, place, low = lax.optimization_barrier((index, piece, place, own_row < pairs))
     block = to_all(piece, "row")
     mirrored = kernel_call(
         first_mirror, "first_mirror", f32(2 * seg_tiles, vecs, LANE), [SMEM] + [VMEM] * 2, work
@@ -265,10 +268,10 @@
     )(index, tiles, images[-1])
 
     direct = jnp.sum(lax.all_to_all(direct, "col", 0, 0), axis=0)
-    direct, mirror = lax.optimization_barrier((direct, mirror))
+    direct, mirror, *kept = lax.optimization_barrier((direct, mirror, *images))
     direct = lax.ppermute(direct, BOTH, corner)
     last = jnp.sum(lax.all_to_all(mirror, "row", 0, 0), axis=0) + direct
-    own = [own_block_piece(image) for image in images]
+    own = [own_block_piece(image) for image in kept]
     grams = kernel_call(gram, "gram", f32(vecs, LANE), [VMEM] * 4)(piece, *own, last)
     last = lax.ppermute(last, BOTH, [(to, at) for at, to in corner])
     grams = jnp.sum(to_all(grams, "row"), axis=0)

time: 288 us -> 288 us (level)
  blocking collectives: 146 us -> 162 us
  waiting for transfers between devices: 42.7 us -> 35.9 us
  starting transfers between devices: 68 us -> 63.8 us
  Pallas kernels: 16.8 us -> 13.1 us
    all_to_all x0 -> x1, blocking collectives: none -> 12.3 us  [body(): direct = jnp.sum(lax.all_to_all(direct, 'col', 0, 0), axis=0)]
    all_to_all x1 -> x0, waiting for transfers between devices: 5.47 us -> none  [body(): direct = jnp.sum(lax.all_to_all(direct, 'col', 0, 0), axis=0)]
    all_to_all x1 -> x0, starting transfers between devices: 3.65 us -> none  [body(): direct = jnp.sum(lax.all_to_all(direct, 'col', 0, 0), axis=0)]
    all_to_all x4, blocking collectives: 146 us -> 149 us  [swap(): moved = lax.all_to_all(x.reshape(rows * cols, 3 * LANE), BOTH, 0, 0)]
  transfers between devices with their start and end apart: 8 -> 7, of which waited for: 7 -> 6; matrix products, arithmetic and copies ran while one was open for 1% -> 1% of each run, Pallas kernels for 1% -> 1%
where the time goes in v9:
time: 288 us; the launch traced here: 287 us
  blocking collectives  162 us (56%)
  starting transfers between devices  63.8 us (22%)
  waiting for transfers between devices  35.9 us (12%)
  Pallas kernels  13.1 us (5%)
  local copies, waits for them, and re-layouts  10.5 us (4%)
    all_to_all x4, blocking collectives, swap(): moved = lax.all_to_all(x.reshape(rows * cols, 3 * LANE), BOTH, 0, 0)  149 us
    all_to_all x3, starting transfers between devices, to_all(): return lax.all_to_all(jnp.broadcast_to(x, (count,) + x.shape), axis, 0, 0)  42.1 us
    all_to_all x3, waiting for transfers between devices, to_all(): return lax.all_to_all(jnp.broadcast_to(x, (count,) + x.shape), axis, 0, 0)  23 us
    all_to_all x1, blocking collectives, body(): direct = jnp.sum(lax.all_to_all(direct, 'col', 0, 0), axis=0)  12.3 us
    all_to_all x1, waiting for transfers between devices, body(): last = jnp.sum(lax.all_to_all(mirror, 'row', 0, 0), axis=0) + direct  8.69 us
    ppermute x1, starting transfers between devices, body(): last = lax.ppermute(last, BOTH, [(to, at) for at, to in corner])  7.16 us
  transfers between devices with their start and end apart: 7, of which 6 were waited for; matrix products, arithmetic and copies ran while one was open for 1% of the time, Pallas kernels for 1%

profile of v9, /device:TPU:1, one launch (start us, length us, event | category | flops | bytes accessed | tf_op | source)
XLA Modules:
  0.0 287.3 jit_solution(9056253850334052884)
XLA Ops:
  0.6 0.7 constant_dynamic-slice_fusion.2
  1.4 5.4 %collective-permute-start = (f32[16,256]{1,0:T(8,128)S(1)}, f32[16,256]{1,0:T(8,128)S(1)}, u32[]{:S(2)}, u32[]{:S(2)}) collective-permute-start(f32[16,256]{1,0:T(8,128)S(1)} %constant_dynamic-slice_fusion.2), channel_id=1, source_target_pairs={{0,0},{1,16},{2,32},{3,48},{4,64},{5,80},{6,96},{7,112},{8,128},{9... | collective-permute-start | bytes 49160 | tf_op jit(solution)/shard_map/ppermute | solution.py:246
  7.4 0.7 pad_add_fusion.index_ref
  8.1 1.8 collective-permute-done.zero_ref
  10.0 0.8 broadcast_in_dim.9
  10.8 23.3 %all-to-all-start = ((f32[32,16,256]{2,1,0:T(8,128)}), f32[32,16,256]{2,1,0:T(8,128)}, u32[]{:S(2)}, u32[]{:S(2)}) async-start(f32[32,16,256]{2,1,0:T(8,128)} %broadcast_in_dim.9), calls=%async_computation | async-start | bytes 1048576 | tf_op jit(solution)/shard_map/all_to_all | solution.py:243
  34.2 0.0 copy-start
  34.2 1.9 copy-done
  36.0 0.0 copy-start.8
  36.0 0.9 copy-done.8
  37.0 0.0 copy-start.1
  37.0 1.4 first_mirror.1.mirrored_ref
  38.5 0.0 copy-start.6
  38.5 0.8 copy-done.6
  39.3 11.9 %all-to-all-done.block_ref = f32[32,16,256]{2,1,0:T(8,128)} async-done(((f32[32,16,256]{2,1,0:T(8,128)}), f32[32,16,256]{2,1,0:T(8,128)}, u32[]{:S(2)}, u32[]{:S(2)}) %all-to-all-start) | async-done | bytes 524320 | tf_op jit(solution)/shard_map/all_to_all | solution.py:243
  51.2 0.0 copy-done.1
  51.2 0.0 copy-start.7
  51.2 1.0 copy-done.7
  52.2 2.5 first_direct.1
  54.8 39.2 %all_to_all.61 = f32[512,1,384]{2,1,0:T(1,128)S(1)} all-to-all(f32[512,1,384]{2,1,0:T(1,128)S(1)} %bitcast.46), channel_id=1, replica_groups=mesh['row'=32,'col'=16] {'row','col'}, dimensions={0} | all-to-all | bytes 1572864 | tf_op jit(solution)/shard_map/all_to_all | solution.py:229
  94.0 0.1 sum_and_deal.2
  94.1 36.3 %all_to_all.62 = f32[512,1,384]{2,1,0:T(1,128)S(1)} all-to-all(f32[512,1,384]{2,1,0:T(1,128)S(1)} %bitcast.43), channel_id=1, replica_groups=mesh['row'=32,'col'=16] {'row','col'}, dimensions={0} | all-to-all | bytes 1572864 | tf_op jit(solution)/shard_map/all_to_all | solution.py:229
  130.5 0.0 copy-start.2
  130.5 2.7 multiply_next.1
  133.2 37.3 %all_to_all.63 = f32[512,1,384]{2,1,0:T(1,128)S(1)} all-to-all(f32[512,1,384]{2,1,0:T(1,128)S(1)} %bitcast.41), channel_id=1, replica_groups=mesh['row'=32,'col'=16] {'row','col'}, dimensions={0} | all-to-all | bytes 1572864 | tf_op jit(solution)/shard_map/all_to_all | solution.py:229
  170.5 0.0 copy-done.2
  170.5 0.1 sum_and_deal.3
  170.6 36.5 %all_to_all.64 = f32[512,1,384]{2,1,0:T(1,128)S(1)} all-to-all(f32[512,1,384]{2,1,0:T(1,128)S(1)} %bitcast.45), channel_id=1, replica_groups=mesh['row'=32,'col'=16] {'row','col'}, dimensions={0} | all-to-all | bytes 1572864 | tf_op jit(solution)/shard_map/all_to_all | solution.py:229
  207.1 0.0 copy-start.4
  207.2 2.7 multiply_last.1
  209.9 0.0 copy-done.4
  209.9 0.0 copy-start.10
  209.9 0.8 copy-done.10
  210.7 0.0 copy-start.11
  210.7 0.0 copy-start.3
  210.7 0.0 copy-start.9
  210.7 0.0 copy-start.5
  210.7 12.3 %all_to_all.65 = f32[16,16,256]{2,1,0:T(8,128)S(1)} all-to-all(f32[16,16,256]{2,1,0:T(8,128)S(1)} %get-tuple-element.14), channel_id=1, replica_groups=mesh['row'=32,'col'=16] {'col'}, dimensions={0} | all-to-all | bytes 524288 | tf_op jit(solution)/shard_map/all_to_all | solution.py:270
  223.0 4.5 %all-to-all-start.6 = ((f32[32,16,256]{2,1,0:T(8,128)}), f32[32,16,256]{2,1,0:T(8,128)S(1)}, u32[]{:S(2)}, u32[]{:S(2)}) async-start(f32[32,16,256]{2,1,0:T(8,128)} %copy-done.10), calls=%async_computation.6 | async-start | bytes 1048576 | tf_op jit(solution)/shard_map/all_to_all | solution.py:273
  227.5 4.6 %collective-permute-start.1 = (f32[16,256]{1,0:T(8,128)S(1)}, f32[16,256]{1,0:T(8,128)S(1)}, u32[]{:S(2)}, u32[]{:S(2)}) collective-permute-start(f32[16,256]{1,0:T(8,128)S(1)} %reduce_sum.27), channel_id=1, source_target_pairs={{0,0},{1,16},{2,32},{3,48},{4,64},{5,80},{6,96},{7,112},{8,128},{9... | collective-permute-start | bytes 49160 | tf_op jit(solution)/shard_map/ppermute | solution.py:272
  232.1 0.8 constant_dynamic-slice_fusion.1
  233.0 0.8 constant_dynamic-slice_fusion
  233.9 8.7 %all-to-all-done.6 = f32[32,16,256]{2,1,0:T(8,128)S(1)} async-done(((f32[32,16,256]{2,1,0:T(8,128)}), f32[32,16,256]{2,1,0:T(8,128)S(1)}, u32[]{:S(2)}, u32[]{:S(2)}) %all-to-all-start.6) | async-done | bytes 524320 | tf_op jit(solution)/shard_map/all_to_all | solution.py:273
  242.7 0.0 collective-permute-done.1
  242.7 0.3 gram.1
  243.0 0.8 broadcast_in_dim.10
  243.7 11.2 %all-to-all-start.7 = ((f32[32,16,128]{2,1,0:T(8,128)}), f32[32,16,128]{2,1,0:T(8,128)S(1)}, u32[]{:S(2)}, u32[]{:S(2)}) async-start(f32[32,16,128]{2,1,0:T(8,128)} %broadcast_in_dim.10), calls=%async_computation.7 | async-start | bytes 524288 | tf_op jit(solution)/shard_map/all_to_all | solution.py:243
  254.9 7.2 %collective-permute-start.2 = (f32[16,256]{1,0:T(8,128)S(1)}, f32[16,256]{1,0:T(8,128)S(1)}, u32[]{:S(2)}, u32[]{:S(2)}) collective-permute-start(f32[16,256]{1,0:T(8,128)S(1)} %add.14.three_ref), channel_id=1, source_target_pairs={{0,0},{16,1},{32,2},{48,3},{64,4},{80,5},{96,6},{112,7},{128,8},{1... | collective-permute-start | bytes 49160 | tf_op jit(solution)/shard_map/ppermute | solution.py:276
  262.1 2.4 collective-permute-done.2
  264.4 2.8 all-to-all-done.7
  267.3 0.8 broadcast_in_dim.11
  268.1 7.6 %all-to-all-start.8 = ((f32[16,3,16,128]{3,2,1,0:T(8,128)}), f32[16,3,16,128]{3,2,1,0:T(8,128)S(1)}, u32[]{:S(2)}, u32[]{:S(2)}) async-start(f32[16,3,16,128]{3,2,1,0:T(8,128)} %broadcast_in_dim.11), calls=%async_computation.8 | async-start | bytes 786432 | tf_op jit(solution)/shard_map/all_to_all | solution.py:243
  275.7 0.0 copy-done.11
  275.7 0.1 copy.31
  275.8 8.3 %all-to-all-done.8.last_ref = f32[16,3,16,128]{3,2,1,0:T(8,128)S(1)} async-done(((f32[16,3,16,128]{3,2,1,0:T(8,128)}), f32[16,3,16,128]{3,2,1,0:T(8,128)S(1)}, u32[]{:S(2)}, u32[]{:S(2)}) %all-to-all-start.8) | async-done | bytes 393248 | tf_op jit(solution)/shard_map/all_to_all | solution.py:243
  284.1 0.0 copy-done.3
  284.1 0.0 copy-done.9
  284.1 0.0 copy-done.5
  284.1 3.2 %finish.1 = (f32[16,4096]{1,0:T(8,128)}, f32[16,16]{1,0:T(8,128)}) custom-call(f32[16,3,16,128]{3,2,1,0:T(8,128)S(1)} %all-to-all-done.8.last_ref, f32[3,3,16,128]{3,2,1,0:T(8,128)S(1)} %pad.4.turn_ref, f32[16,4096]{1,0:T(8,128)S(1)} %copy-done.9, f32[1536,128]{1,0:T(8,128)S(1)} %bitcast.37, f32[1536,128]{1,0:T(8,128)S(1)} %bitcast.40), custom_call_target="tpu_custom_call" | custom-call | tf_op jit(solution)/shard_map/finish/pallas_call | solution.py:280
  (16 shorter events, 0.3 us)
Async XLA Ops:
  1.4 8.6 %collective-permute-start = (f32[16,256]{1,0:T(8,128)S(1)}, f32[16,256]{1,0:T(8,128)S(1)}, u32[]{:S(2)}, u32[]{:S(2)}) collective-permute-start(f32[16,256]{1,0:T(8,128)S(1)} %constant_dynamic-slice_fusion.2), channel_id=1, source_target_pairs={{0,0},{1,16},{2,32},{3,48},{4,64},{5,80},{6,96},{7,112},{8,128},{9... | collective-permute-start | bytes 49160 | tf_op jit(solution)/shard_map/ppermute | solution.py:246
  10.8 40.4 %all-to-all-start = ((f32[32,16,256]{2,1,0:T(8,128)}), f32[32,16,256]{2,1,0:T(8,128)}, u32[]{:S(2)}, u32[]{:S(2)}) async-start(f32[32,16,256]{2,1,0:T(8,128)} %broadcast_in_dim.9), calls=%async_computation | async-start | bytes 1048576 | tf_op jit(solution)/shard_map/all_to_all | solution.py:243
  34.2 1.9 copy-start
  36.0 0.9 copy-start.8
  37.0 14.2 %copy-start.1 = (bf16[1,1,96,128,128]{4,3,2,1,0:T(8,128)(2,1)S(1)}, bf16[1,1,96,128,128]{4,3,2,1,0:T(8,128)(2,1)}, u32[]{:S(2)}) copy-start(bf16[1,1,96,128,128]{4,3,2,1,0:T(8,128)(2,1)} %param.6) | copy-start | bytes 9437188
  38.5 0.8 copy-start.6
  51.2 1.0 copy-start.7
  130.5 40.0 %copy-start.2 = (f32[512,1,384]{2,1,0:T(1,128)}, f32[512,1,384]{2,1,0:T(1,128)S(1)}, u32[]{:S(2)}) copy-start(f32[512,1,384]{2,1,0:T(1,128)S(1)} %all_to_all.62) | copy-start | bytes 2359300
  207.1 2.7 copy-start.4
  209.9 0.8 copy-start.10
  210.7 65.0 %copy-start.11 = (f32[3,3,16,16]{3,2,1,0:T(8,128)S(1)}, f32[3,3,16,16]{3,2,1,0:T(8,128)}, u32[]{:S(2)}) copy-start(f32[3,3,16,16]{3,2,1,0:T(8,128)} %param.11) | copy-start | bytes 27652
  210.7 73.4 %copy-start.3 = (f32[512,1,384]{2,1,0:T(1,128)S(1)}, f32[512,1,384]{2,1,0:T(1,128)}, u32[]{:S(2)}) copy-start(f32[512,1,384]{2,1,0:T(1,128)} %copy-done.2) | copy-start | bytes 2359300
  210.7 73.4 %copy-start.9 = (f32[16,4096]{1,0:T(8,128)S(1)}, f32[16,4096]{1,0:T(8,128)}, u32[]{:S(2)}) copy-start(f32[16,4096]{1,0:T(8,128)} %start_ref.1) | copy-start | bytes 786436
  210.7 73.4 %copy-start.5 = (f32[512,1,384]{2,1,0:T(1,128)S(1)}, f32[512,1,384]{2,1,0:T(1,128)}, u32[]{:S(2)}) copy-start(f32[512,1,384]{2,1,0:T(1,128)} %copy-done.4) | copy-start | bytes 2359300
  223.0 19.6 %all-to-all-start.6 = ((f32[32,16,256]{2,1,0:T(8,128)}), f32[32,16,256]{2,1,0:T(8,128)S(1)}, u32[]{:S(2)}, u32[]{:S(2)}) async-start(f32[32,16,256]{2,1,0:T(8,128)} %copy-done.10), calls=%async_computation.6 | async-start | bytes 1048576 | tf_op jit(solution)/shard_map/all_to_all | solution.py:273
  227.5 15.2 %collective-permute-start.1 = (f32[16,256]{1,0:T(8,128)S(1)}, f32[16,256]{1,0:T(8,128)S(1)}, u32[]{:S(2)}, u32[]{:S(2)}) collective-permute-start(f32[16,256]{1,0:T(8,128)S(1)} %reduce_sum.27), channel_id=1, source_target_pairs={{0,0},{1,16},{2,32},{3,48},{4,64},{5,80},{6,96},{7,112},{8,128},{9... | collective-permute-start | bytes 49160 | tf_op jit(solution)/shard_map/ppermute | solution.py:272
  243.7 23.5 %all-to-all-start.7 = ((f32[32,16,128]{2,1,0:T(8,128)}), f32[32,16,128]{2,1,0:T(8,128)S(1)}, u32[]{:S(2)}, u32[]{:S(2)}) async-start(f32[32,16,128]{2,1,0:T(8,128)} %broadcast_in_dim.10), calls=%async_computation.7 | async-start | bytes 524288 | tf_op jit(solution)/shard_map/all_to_all | solution.py:243
  254.9 9.5 %collective-permute-start.2 = (f32[16,256]{1,0:T(8,128)S(1)}, f32[16,256]{1,0:T(8,128)S(1)}, u32[]{:S(2)}, u32[]{:S(2)}) collective-permute-start(f32[16,256]{1,0:T(8,128)S(1)} %add.14.three_ref), channel_id=1, source_target_pairs={{0,0},{16,1},{32,2},{48,3},{64,4},{80,5},{96,6},{112,7},{128,8},{1... | collective-permute-start | bytes 49160 | tf_op jit(solution)/shard_map/ppermute | solution.py:276
  268.1 16.1 %all-to-all-start.8 = ((f32[16,3,16,128]{3,2,1,0:T(8,128)}), f32[16,3,16,128]{3,2,1,0:T(8,128)S(1)}, u32[]{:S(2)}, u32[]{:S(2)}) async-start(f32[16,3,16,128]{3,2,1,0:T(8,128)} %broadcast_in_dim.11), calls=%async_computation.8 | async-start | bytes 786432 | tf_op jit(solution)/shard_map/all_to_all | solution.py:243

commit v10 on v9

--- a/solution.py
+++ b/solution.py
@@ -244,12 +244,12 @@
 
     own_start = lax.dynamic_slice_in_dim(start, own_col * pair, pair, 1)
     piece = lax.ppermute(own_start, BOTH, corner)
-    place = (own_row % pairs * size).astype(jnp.uint32)
-    index, piece, place, low = lax.optimization_barrier((index, piece, place, own_row < pairs))
-    block = to_all(piece, "row")
     mirrored = kernel_call(
         first_mirror, "first_mirror", f32(2 * seg_tiles, vecs, LANE), [SMEM] + [VMEM] * 2, work
     )(index, tiles, start)
+    place = (own_row % pairs * size).astype(jnp.uint32)
+    mirrored, piece, place, low = lax.optimization_barrier((mirrored, piece, place, own_row < pairs))
+    block = to_all(piece, "row")
     sent = kernel_call(first_direct, "first_direct", dealt, [SMEM] + [VMEM] * 3, work)(
         index, tiles, block, mirrored
     )

time: 288 us -> 284 us (0.986)
  blocking collectives: 162 us -> 201 us
  starting transfers between devices: 63.8 us -> 40.2 us
  waiting for transfers between devices: 35.9 us -> 23.8 us
  local copies, waits for them, and re-layouts: 10.5 us -> 5.39 us
    all_to_all x0 -> x1, blocking collectives: none -> 37.9 us  [to_all(): return lax.all_to_all(jnp.broadcast_to(x, (count,) + x.shape), axis, 0, 0)]
    all_to_all x3 -> x2, starting transfers between devices: 42.1 us -> 18.8 us  [to_all(): return lax.all_to_all(jnp.broadcast_to(x, (count,) + x.shape), axis, 0, 0)]
    all_to_all x3 -> x2, waiting for transfers between devices: 23 us -> 11.1 us  [to_all(): return lax.all_to_all(jnp.broadcast_to(x, (count,) + x.shape), axis, 0, 0)]
  transfers between devices with their start and end apart: 7 -> 6, of which waited for: 6 -> 4; matrix products, arithmetic and copies ran while one was open for 1% -> 0% of each run, Pallas kernels for 1% -> 0%
where the time goes in v10:
time: 284 us; the launch traced here: 283 us
  blocking collectives  201 us (71%)
  starting transfers between devices  40.2 us (14%)
  waiting for transfers between devices  23.8 us (8%)
  Pallas kernels  10.3 us (4%)
  local copies, waits for them, and re-layouts  5.39 us (2%)
    all_to_all x4, blocking collectives, swap(): moved = lax.all_to_all(x.reshape(rows * cols, 3 * LANE), BOTH, 0, 0)  150 us
    all_to_all x1, blocking collectives, to_all(): return lax.all_to_all(jnp.broadcast_to(x, (count,) + x.shape), axis, 0, 0)  37.9 us
    all_to_all x2, starting transfers between devices, to_all(): return lax.all_to_all(jnp.broadcast_to(x, (count,) + x.shape), axis, 0, 0)  18.8 us
    all_to_all x1, blocking collectives, body(): direct = jnp.sum(lax.all_to_all(direct, 'col', 0, 0), axis=0)  12.5 us
    all_to_all x2, waiting for transfers between devices, to_all(): return lax.all_to_all(jnp.broadcast_to(x, (count,) + x.shape), axis, 0, 0)  11.1 us
    all_to_all x1, waiting for transfers between devices, body(): last = jnp.sum(lax.all_to_all(mirror, 'row', 0, 0), axis=0) + direct  10.3 us
    ppermute x1, starting transfers between devices, body(): last = lax.ppermute(last, BOTH, [(to, at) for at, to in corner])  7.16 us
  transfers between devices with their start and end apart: 6, of which 4 were waited for; matrix products, arithmetic and copies ran while one was open for 0% of the time, Pallas kernels for 0%

profile of v10, /device:TPU:1, one launch (start us, length us, event | category | flops | bytes accessed | tf_op | source)
XLA Modules:
  0.0 282.9 jit_solution(15015660923801277896)
XLA Ops:
  0.6 0.7 constant_dynamic-slice_fusion.2
  1.4 5.4 %collective-permute-start = (f32[16,256]{1,0:T(8,128)S(1)}, f32[16,256]{1,0:T(8,128)S(1)}, u32[]{:S(2)}, u32[]{:S(2)}) collective-permute-start(f32[16,256]{1,0:T(8,128)S(1)} %constant_dynamic-slice_fusion.2), channel_id=1, source_target_pairs={{0,0},{1,16},{2,32},{3,48},{4,64},{5,80},{6,96},{7,112},{8,128},{9... | collective-permute-start | bytes 49160 | tf_op jit(solution)/shard_map/ppermute | solution.py:246
  7.4 0.7 pad_add_fusion.index_ref
  8.1 0.0 copy-start
  8.1 1.9 copy-done
  10.0 0.0 copy-start.2
  10.0 0.9 copy-done.2
  11.0 1.1 first_mirror.1.mirrored_ref
  12.0 0.0 collective-permute-done.zero_ref
  12.1 0.1 broadcast_in_dim.9
  12.1 37.9 %all_to_all.61.block_ref = f32[32,16,256]{2,1,0:T(8,128)S(1)} all-to-all(f32[32,16,256]{2,1,0:T(8,128)S(1)} %broadcast_in_dim.9), channel_id=1, replica_groups=mesh['row'=32,'col'=16] {'row'}, dimensions={0} | all-to-all | bytes 1048576 | tf_op jit(solution)/shard_map/all_to_all | solution.py:243
  50.1 1.4 first_direct.1
  51.4 0.0 copy-start.1
  51.4 39.9 %all_to_all.62 = f32[512,1,384]{2,1,0:T(1,128)S(1)} all-to-all(f32[512,1,384]{2,1,0:T(1,128)S(1)} %bitcast.46), channel_id=1, replica_groups=mesh['row'=32,'col'=16] {'row','col'}, dimensions={0} | all-to-all | bytes 1572864 | tf_op jit(solution)/shard_map/all_to_all | solution.py:229
  91.4 0.1 sum_and_deal.2
  91.5 36.3 %all_to_all.63 = f32[512,1,384]{2,1,0:T(1,128)S(1)} all-to-all(f32[512,1,384]{2,1,0:T(1,128)S(1)} %bitcast.43), channel_id=1, replica_groups=mesh['row'=32,'col'=16] {'row','col'}, dimensions={0} | all-to-all | bytes 1572864 | tf_op jit(solution)/shard_map/all_to_all | solution.py:229
  127.8 0.0 copy-done.1
  127.8 1.7 multiply_next.1
  129.6 37.6 %all_to_all.64 = f32[512,1,384]{2,1,0:T(1,128)S(1)} all-to-all(f32[512,1,384]{2,1,0:T(1,128)S(1)} %bitcast.41), channel_id=1, replica_groups=mesh['row'=32,'col'=16] {'row','col'}, dimensions={0} | all-to-all | bytes 1572864 | tf_op jit(solution)/shard_map/all_to_all | solution.py:229
  167.2 0.1 sum_and_deal.3
  167.3 36.5 %all_to_all.65 = f32[512,1,384]{2,1,0:T(1,128)S(1)} all-to-all(f32[512,1,384]{2,1,0:T(1,128)S(1)} %bitcast.45), channel_id=1, replica_groups=mesh['row'=32,'col'=16] {'row','col'}, dimensions={0} | all-to-all | bytes 1572864 | tf_op jit(solution)/shard_map/all_to_all | solution.py:229
  203.8 2.5 multiply_last.1
  206.3 0.0 copy-start.4
  206.3 0.0 copy-start.3
  206.3 12.5 %all_to_all.66 = f32[16,16,256]{2,1,0:T(8,128)S(1)} all-to-all(f32[16,16,256]{2,1,0:T(8,128)S(1)} %get-tuple-element.14), channel_id=1, replica_groups=mesh['row'=32,'col'=16] {'col'}, dimensions={0} | all-to-all | bytes 524288 | tf_op jit(solution)/shard_map/all_to_all | solution.py:270
  218.9 4.3 %all-to-all-start.6 = ((f32[32,16,256]{2,1,0:T(8,128)}), f32[32,16,256]{2,1,0:T(8,128)S(1)}, u32[]{:S(2)}, u32[]{:S(2)}) async-start(f32[32,16,256]{2,1,0:T(8,128)} %get-tuple-element.16), calls=%async_computation.6 | async-start | bytes 1048576 | tf_op jit(solution)/shard_map/all_to_all | solution.py:273
  223.1 4.6 %collective-permute-start.1 = (f32[16,256]{1,0:T(8,128)S(1)}, f32[16,256]{1,0:T(8,128)S(1)}, u32[]{:S(2)}, u32[]{:S(2)}) collective-permute-start(f32[16,256]{1,0:T(8,128)S(1)} %reduce_sum.27), channel_id=1, source_target_pairs={{0,0},{1,16},{2,32},{3,48},{4,64},{5,80},{6,96},{7,112},{8,128},{9... | collective-permute-start | bytes 49160 | tf_op jit(solution)/shard_map/ppermute | solution.py:272
  228.0 10.3 %all-to-all-done.6 = f32[32,16,256]{2,1,0:T(8,128)S(1)} async-done(((f32[32,16,256]{2,1,0:T(8,128)}), f32[32,16,256]{2,1,0:T(8,128)S(1)}, u32[]{:S(2)}, u32[]{:S(2)}) %all-to-all-start.6) | async-done | bytes 524320 | tf_op jit(solution)/shard_map/all_to_all | solution.py:273
  238.3 0.0 collective-permute-done.1
  238.3 0.3 gram.1
  238.6 0.8 broadcast_in_dim.10
  239.3 11.2 %all-to-all-start.7 = ((f32[32,16,128]{2,1,0:T(8,128)}), f32[32,16,128]{2,1,0:T(8,128)S(1)}, u32[]{:S(2)}, u32[]{:S(2)}) async-start(f32[32,16,128]{2,1,0:T(8,128)} %broadcast_in_dim.10), calls=%async_computation.7 | async-start | bytes 524288 | tf_op jit(solution)/shard_map/all_to_all | solution.py:243
  250.5 7.2 %collective-permute-start.2 = (f32[16,256]{1,0:T(8,128)S(1)}, f32[16,256]{1,0:T(8,128)S(1)}, u32[]{:S(2)}, u32[]{:S(2)}) collective-permute-start(f32[16,256]{1,0:T(8,128)S(1)} %add.14.three_ref), channel_id=1, source_target_pairs={{0,0},{16,1},{32,2},{48,3},{64,4},{80,5},{96,6},{112,7},{128,8},{1... | collective-permute-start | bytes 49160 | tf_op jit(solution)/shard_map/ppermute | solution.py:276
  257.7 2.4 collective-permute-done.2
  260.0 2.8 all-to-all-done.7
  262.9 0.8 broadcast_in_dim.11
  263.6 7.6 %all-to-all-start.8 = ((f32[16,3,16,128]{3,2,1,0:T(8,128)}), f32[16,3,16,128]{3,2,1,0:T(8,128)S(1)}, u32[]{:S(2)}, u32[]{:S(2)}) async-start(f32[16,3,16,128]{3,2,1,0:T(8,128)} %broadcast_in_dim.11), calls=%async_computation.8 | async-start | bytes 786432 | tf_op jit(solution)/shard_map/all_to_all | solution.py:243
  271.3 0.0 copy-done.4
  271.3 0.1 copy.31
  271.4 8.3 %all-to-all-done.8.last_ref = f32[16,3,16,128]{3,2,1,0:T(8,128)S(1)} async-done(((f32[16,3,16,128]{3,2,1,0:T(8,128)}), f32[16,3,16,128]{3,2,1,0:T(8,128)S(1)}, u32[]{:S(2)}, u32[]{:S(2)}) %all-to-all-start.8) | async-done | bytes 393248 | tf_op jit(solution)/shard_map/all_to_all | solution.py:243
  279.7 0.0 copy-done.3
  279.7 3.2 %finish.1 = (f32[16,4096]{1,0:T(8,128)}, f32[16,16]{1,0:T(8,128)}) custom-call(f32[16,3,16,128]{3,2,1,0:T(8,128)S(1)} %all-to-all-done.8.last_ref, f32[3,3,16,128]{3,2,1,0:T(8,128)S(1)} %pad.4.turn_ref, f32[16,4096]{1,0:T(8,128)S(1)} %copy-done.3, f32[1536,128]{1,0:T(8,128)S(1)} %bitcast.37, f32[1536,128]{1,0:T(8,128)S(1)} %bitcast.40), custom_call_target="tpu_custom_call" | custom-call | tf_op jit(solution)/shard_map/finish/pallas_call | solution.py:280
  (18 shorter events, 0.3 us)
Async XLA Ops:
  1.4 10.7 %collective-permute-start = (f32[16,256]{1,0:T(8,128)S(1)}, f32[16,256]{1,0:T(8,128)S(1)}, u32[]{:S(2)}, u32[]{:S(2)}) collective-permute-start(f32[16,256]{1,0:T(8,128)S(1)} %constant_dynamic-slice_fusion.2), channel_id=1, source_target_pairs={{0,0},{1,16},{2,32},{3,48},{4,64},{5,80},{6,96},{7,112},{8,128},{9... | collective-permute-start | bytes 49160 | tf_op jit(solution)/shard_map/ppermute | solution.py:246
  8.1 1.9 copy-start
  10.0 0.9 copy-start.2
  51.4 76.4 %copy-start.1 = (bf16[1,1,96,128,128]{4,3,2,1,0:T(8,128)(2,1)S(1)}, bf16[1,1,96,128,128]{4,3,2,1,0:T(8,128)(2,1)}, u32[]{:S(2)}) copy-start(bf16[1,1,96,128,128]{4,3,2,1,0:T(8,128)(2,1)} %param.6) | copy-start | bytes 9437188
  206.3 65.0 %copy-start.4 = (f32[3,3,16,16]{3,2,1,0:T(8,128)S(1)}, f32[3,3,16,16]{3,2,1,0:T(8,128)}, u32[]{:S(2)}) copy-start(f32[3,3,16,16]{3,2,1,0:T(8,128)} %param.11) | copy-start | bytes 27652
  206.3 73.4 %copy-start.3 = (f32[16,4096]{1,0:T(8,128)S(1)}, f32[16,4096]{1,0:T(8,128)}, u32[]{:S(2)}) copy-start(f32[16,4096]{1,0:T(8,128)} %start_ref.1) | copy-start | bytes 786436
  218.9 19.4 %all-to-all-start.6 = ((f32[32,16,256]{2,1,0:T(8,128)}), f32[32,16,256]{2,1,0:T(8,128)S(1)}, u32[]{:S(2)}, u32[]{:S(2)}) async-start(f32[32,16,256]{2,1,0:T(8,128)} %get-tuple-element.16), calls=%async_computation.6 | async-start | bytes 1048576 | tf_op jit(solution)/shard_map/all_to_all | solution.py:273
  223.1 15.2 %collective-permute-start.1 = (f32[16,256]{1,0:T(8,128)S(1)}, f32[16,256]{1,0:T(8,128)S(1)}, u32[]{:S(2)}, u32[]{:S(2)}) collective-permute-start(f32[16,256]{1,0:T(8,128)S(1)} %reduce_sum.27), channel_id=1, source_target_pairs={{0,0},{1,16},{2,32},{3,48},{4,64},{5,80},{6,96},{7,112},{8,128},{9... | collective-permute-start | bytes 49160 | tf_op jit(solution)/shard_map/ppermute | solution.py:272
  239.3 23.5 %all-to-all-start.7 = ((f32[32,16,128]{2,1,0:T(8,128)}), f32[32,16,128]{2,1,0:T(8,128)S(1)}, u32[]{:S(2)}, u32[]{:S(2)}) async-start(f32[32,16,128]{2,1,0:T(8,128)} %broadcast_in_dim.10), calls=%async_computation.7 | async-start | bytes 524288 | tf_op jit(solution)/shard_map/all_to_all | solution.py:243
  250.5 9.5 %collective-permute-start.2 = (f32[16,256]{1,0:T(8,128)S(1)}, f32[16,256]{1,0:T(8,128)S(1)}, u32[]{:S(2)}, u32[]{:S(2)}) collective-permute-start(f32[16,256]{1,0:T(8,128)S(1)} %add.14.three_ref), channel_id=1, source_target_pairs={{0,0},{16,1},{32,2},{48,3},{64,4},{80,5},{96,6},{112,7},{128,8},{1... | collective-permute-start | bytes 49160 | tf_op jit(solution)/shard_map/ppermute | solution.py:276
  263.6 16.1 %all-to-all-start.8 = ((f32[16,3,16,128]{3,2,1,0:T(8,128)}), f32[16,3,16,128]{3,2,1,0:T(8,128)S(1)}, u32[]{:S(2)}, u32[]{:S(2)}) async-start(f32[16,3,16,128]{3,2,1,0:T(8,128)} %broadcast_in_dim.11), calls=%async_computation.8 | async-start | bytes 786432 | tf_op jit(solution)/shard_map/all_to_all | solution.py:243

commit v11 on v10

--- a/solution.py
+++ b/solution.py
@@ -268,15 +268,16 @@
     )(index, tiles, images[-1])
 
     direct = jnp.sum(lax.all_to_all(direct, "col", 0, 0), axis=0)
-    direct, mirror, *kept = lax.optimization_barrier((direct, mirror, *images))
+    direct, mirror, rotation, *kept = lax.optimization_barrier((direct, mirror, rotation, *images))
+    turned = jnp.pad(jnp.swapaxes(rotation, 2, 3), ((0, 0),) * 3 + ((0, LANE - vecs),))
     direct = lax.ppermute(direct, BOTH, corner)
     last = jnp.sum(lax.all_to_all(mirror, "row", 0, 0), axis=0) + direct
     own = [own_block_piece(image) for image in kept]
     grams = kernel_call(gram, "gram", f32(vecs, LANE), [VMEM] * 4)(piece, *own, last)
     last = lax.ppermute(last, BOTH, [(to, at) for at, to in corner])
     grams = jnp.sum(to_all(grams, "row"), axis=0)
-    last = to_all(jnp.stack([last[:, :LANE], last[:, LANE:], grams]), "col")
-    turned = jnp.pad(jnp.swapaxes(rotation, 2, 3), ((0, 0),) * 3 + ((0, LANE - vecs),))
+    last, turned = lax.optimization_barrier((jnp.stack([last[:, :LANE], last[:, LANE:], grams]), turned))
+    last = to_all(last, "col")
     return kernel_call(
         functools.partial(finish, seg_rows * rows), "finish", (f32(vecs, seg_rows), f32(vecs, vecs)), [VMEM] * 5
     )(last, turned, start, *images)

time: 284 us -> 284 us (level)
  blocking collectives: 201 us -> 217 us
  waiting for transfers between devices: 23.8 us -> 15.3 us
  starting transfers between devices: 40.2 us -> 33.5 us
    all_to_all x1 -> x2, blocking collectives: 37.9 us -> 53.8 us  [to_all(): return lax.all_to_all(jnp.broadcast_to(x, (count,) + x.shape), axis, 0, 0)]
    all_to_all x2 -> x1, waiting for transfers between devices: 11.1 us -> 2.78 us  [to_all(): return lax.all_to_all(jnp.broadcast_to(x, (count,) + x.shape), axis, 0, 0)]
    all_to_all x2 -> x1, starting transfers between devices: 18.8 us -> 11.2 us  [to_all(): return lax.all_to_all(jnp.broadcast_to(x, (count,) + x.shape), axis, 0, 0)]
  transfers between devices with their start and end apart: 6 -> 5, of which waited for: 4 -> 3; matrix products, arithmetic and copies ran while one was open for 0% -> 0% of each run, Pallas kernels for 0% -> 0%
where the time goes in v11:
time: 284 us; the launch traced here: 283 us
  blocking collectives  217 us (76%)
  starting transfers between devices  33.5 us (12%)
  waiting for transfers between devices  15.3 us (5%)
  Pallas kernels  10.3 us (4%)
  local copies, waits for them, and re-layouts  4.65 us (2%)
    all_to_all x4, blocking collectives, swap(): moved = lax.all_to_all(x.reshape(rows * cols, 3 * LANE), BOTH, 0, 0)  150 us
    all_to_all x2, blocking collectives, to_all(): return lax.all_to_all(jnp.broadcast_to(x, (count,) + x.shape), axis, 0, 0)  53.8 us
    all_to_all x1, blocking collectives, body(): direct = jnp.sum(lax.all_to_all(direct, 'col', 0, 0), axis=0)  12.6 us
    all_to_all x1, starting transfers between devices, to_all(): return lax.all_to_all(jnp.broadcast_to(x, (count,) + x.shape), axis, 0, 0)  11.2 us
    all_to_all x1, waiting for transfers between devices, body(): last = jnp.sum(lax.all_to_all(mirror, 'row', 0, 0), axis=0) + direct  10.3 us
    ppermute x1, starting transfers between devices, body(): last = lax.ppermute(last, BOTH, [(to, at) for at, to in corner])  7.16 us
  transfers between devices with their start and end apart: 5, of which 3 were waited for; matrix products, arithmetic and copies ran while one was open for 0% of the time, Pallas kernels for 0%

profile of v11, /device:TPU:1, one launch (start us, length us, event | category | flops | bytes accessed | tf_op | source)
XLA Modules:
  0.0 282.8 jit_solution(3404233144069294097)
XLA Ops:
  0.6 0.7 constant_dynamic-slice_fusion.2
  1.4 5.4 %collective-permute-start = (f32[16,256]{1,0:T(8,128)S(1)}, f32[16,256]{1,0:T(8,128)S(1)}, u32[]{:S(2)}, u32[]{:S(2)}) collective-permute-start(f32[16,256]{1,0:T(8,128)S(1)} %constant_dynamic-slice_fusion.2), channel_id=1, source_target_pairs={{0,0},{1,16},{2,32},{3,48},{4,64},{5,80},{6,96},{7,112},{8,128},{9... | collective-permute-start | bytes 49160 | tf_op jit(solution)/shard_map/ppermute | solution.py:246
  7.4 0.7 pad_add_fusion.index_ref
  8.1 0.0 copy-start
  8.1 1.9 copy-done
  10.0 0.0 copy-start.2
  10.0 0.9 copy-done.2
  11.0 1.1 first_mirror.1.mirrored_ref
  12.0 0.0 collective-permute-done.zero_ref
  12.1 0.1 broadcast_in_dim.9
  12.1 38.0 %all_to_all.61.block_ref = f32[32,16,256]{2,1,0:T(8,128)S(1)} all-to-all(f32[32,16,256]{2,1,0:T(8,128)S(1)} %broadcast_in_dim.9), channel_id=1, replica_groups=mesh['row'=32,'col'=16] {'row'}, dimensions={0} | all-to-all | bytes 1048576 | tf_op jit(solution)/shard_map/all_to_all | solution.py:243
  50.1 1.4 first_direct.1
  51.4 0.0 copy-start.1
  51.4 39.6 %all_to_all.62 = f32[512,1,384]{2,1,0:T(1,128)S(1)} all-to-all(f32[512,1,384]{2,1,0:T(1,128)S(1)} %bitcast.46), channel_id=1, replica_groups=mesh['row'=32,'col'=16] {'row','col'}, dimensions={0} | all-to-all | bytes 1572864 | tf_op jit(solution)/shard_map/all_to_all | solution.py:229
  91.1 0.1 sum_and_deal.2
  91.2 36.3 %all_to_all.63 = f32[512,1,384]{2,1,0:T(1,128)S(1)} all-to-all(f32[512,1,384]{2,1,0:T(1,128)S(1)} %bitcast.43), channel_id=1, replica_groups=mesh['row'=32,'col'=16] {'row','col'}, dimensions={0} | all-to-all | bytes 1572864 | tf_op jit(solution)/shard_map/all_to_all | solution.py:229
  127.5 0.0 copy-done.1
  127.5 1.7 multiply_next.1
  129.3 37.8 %all_to_all.64 = f32[512,1,384]{2,1,0:T(1,128)S(1)} all-to-all(f32[512,1,384]{2,1,0:T(1,128)S(1)} %bitcast.41), channel_id=1, replica_groups=mesh['row'=32,'col'=16] {'row','col'}, dimensions={0} | all-to-all | bytes 1572864 | tf_op jit(solution)/shard_map/all_to_all | solution.py:229
  167.0 0.1 sum_and_deal.3
  167.2 36.5 %all_to_all.65 = f32[512,1,384]{2,1,0:T(1,128)S(1)} all-to-all(f32[512,1,384]{2,1,0:T(1,128)S(1)} %bitcast.45), channel_id=1, replica_groups=mesh['row'=32,'col'=16] {'row','col'}, dimensions={0} | all-to-all | bytes 1572864 | tf_op jit(solution)/shard_map/all_to_all | solution.py:229
  203.7 0.0 copy-start.4
  203.7 2.5 multiply_last.1
  206.2 0.0 copy-start.3
  206.2 12.6 %all_to_all.66 = f32[16,16,256]{2,1,0:T(8,128)S(1)} all-to-all(f32[16,16,256]{2,1,0:T(8,128)S(1)} %get-tuple-element.17), channel_id=1, replica_groups=mesh['row'=32,'col'=16] {'col'}, dimensions={0} | all-to-all | bytes 524288 | tf_op jit(solution)/shard_map/all_to_all | solution.py:270
  218.8 5.3 %all-to-all-start.6 = ((f32[32,16,256]{2,1,0:T(8,128)}), f32[32,16,256]{2,1,0:T(8,128)S(1)}, u32[]{:S(2)}, u32[]{:S(2)}) async-start(f32[32,16,256]{2,1,0:T(8,128)} %get-tuple-element.19), calls=%async_computation.6 | async-start | bytes 1048576 | tf_op jit(solution)/shard_map/all_to_all | solution.py:274
  224.1 4.6 %collective-permute-start.1 = (f32[16,256]{1,0:T(8,128)S(1)}, f32[16,256]{1,0:T(8,128)S(1)}, u32[]{:S(2)}, u32[]{:S(2)}) collective-permute-start(f32[16,256]{1,0:T(8,128)S(1)} %reduce_sum.27), channel_id=1, source_target_pairs={{0,0},{1,16},{2,32},{3,48},{4,64},{5,80},{6,96},{7,112},{8,128},{9... | collective-permute-start | bytes 49160 | tf_op jit(solution)/shard_map/ppermute | solution.py:273
  228.9 10.3 %all-to-all-done.6 = f32[32,16,256]{2,1,0:T(8,128)S(1)} async-done(((f32[32,16,256]{2,1,0:T(8,128)}), f32[32,16,256]{2,1,0:T(8,128)S(1)}, u32[]{:S(2)}, u32[]{:S(2)}) %all-to-all-start.6) | async-done | bytes 524320 | tf_op jit(solution)/shard_map/all_to_all | solution.py:274
  239.2 0.0 collective-permute-done.1
  239.2 0.3 gram.1
  239.5 0.8 broadcast_in_dim.10
  240.3 11.2 %all-to-all-start.7 = ((f32[32,16,128]{2,1,0:T(8,128)}), f32[32,16,128]{2,1,0:T(8,128)S(1)}, u32[]{:S(2)}, u32[]{:S(2)}) async-start(f32[32,16,128]{2,1,0:T(8,128)} %broadcast_in_dim.10), calls=%async_computation.7 | async-start | bytes 524288 | tf_op jit(solution)/shard_map/all_to_all | solution.py:243
  251.4 7.2 %collective-permute-start.2 = (f32[16,256]{1,0:T(8,128)S(1)}, f32[16,256]{1,0:T(8,128)S(1)}, u32[]{:S(2)}, u32[]{:S(2)}) collective-permute-start(f32[16,256]{1,0:T(8,128)S(1)} %add.14.three_ref), channel_id=1, source_target_pairs={{0,0},{16,1},{32,2},{48,3},{64,4},{80,5},{96,6},{112,7},{128,8},{1... | collective-permute-start | bytes 49160 | tf_op jit(solution)/shard_map/ppermute | solution.py:277
  258.6 0.0 copy-done.4
  258.6 0.1 copy.31
  258.7 2.2 collective-permute-done.2
  261.0 2.8 all-to-all-done.7
  263.8 15.8 %all_to_all.67.last_ref = f32[16,3,16,128]{3,2,1,0:T(8,128)S(1)} all-to-all(f32[16,3,16,128]{3,2,1,0:T(8,128)S(1)} %broadcast_in_dim.11), channel_id=1, replica_groups=mesh['row'=32,'col'=16] {'col'}, dimensions={0} | all-to-all | bytes 786432 | tf_op jit(solution)/shard_map/all_to_all | solution.py:243
  279.6 0.0 copy-done.3
  279.6 3.2 %finish.1 = (f32[16,4096]{1,0:T(8,128)}, f32[16,16]{1,0:T(8,128)}) custom-call(f32[16,3,16,128]{3,2,1,0:T(8,128)S(1)} %all_to_all.67.last_ref, f32[3,3,16,128]{3,2,1,0:T(8,128)S(1)} %pad.4.turn_ref, f32[16,4096]{1,0:T(8,128)S(1)} %copy-done.3, f32[1536,128]{1,0:T(8,128)S(1)} %bitcast.37, f32[1536,128]{1,0:T(8,128)S(1)} %bitcast.40), custom_call_target="tpu_custom_call" | custom-call | tf_op jit(solution)/shard_map/finish/pallas_call | solution.py:281
  (19 shorter events, 0.3 us)
Async XLA Ops:
  1.4 10.7 %collective-permute-start = (f32[16,256]{1,0:T(8,128)S(1)}, f32[16,256]{1,0:T(8,128)S(1)}, u32[]{:S(2)}, u32[]{:S(2)}) collective-permute-start(f32[16,256]{1,0:T(8,128)S(1)} %constant_dynamic-slice_fusion.2), channel_id=1, source_target_pairs={{0,0},{1,16},{2,32},{3,48},{4,64},{5,80},{6,96},{7,112},{8,128},{9... | collective-permute-start | bytes 49160 | tf_op jit(solution)/shard_map/ppermute | solution.py:246
  8.1 1.9 copy-start
  10.0 0.9 copy-start.2
  51.4 76.1 %copy-start.1 = (bf16[1,1,96,128,128]{4,3,2,1,0:T(8,128)(2,1)S(1)}, bf16[1,1,96,128,128]{4,3,2,1,0:T(8,128)(2,1)}, u32[]{:S(2)}) copy-start(bf16[1,1,96,128,128]{4,3,2,1,0:T(8,128)(2,1)} %param.6) | copy-start | bytes 9437188
  203.7 54.9 %copy-start.4 = (f32[3,3,16,16]{3,2,1,0:T(8,128)S(1)}, f32[3,3,16,16]{3,2,1,0:T(8,128)}, u32[]{:S(2)}) copy-start(f32[3,3,16,16]{3,2,1,0:T(8,128)} %param.11) | copy-start | bytes 27652
  206.2 73.5 %copy-start.3 = (f32[16,4096]{1,0:T(8,128)S(1)}, f32[16,4096]{1,0:T(8,128)}, u32[]{:S(2)}) copy-start(f32[16,4096]{1,0:T(8,128)} %start_ref.1) | copy-start | bytes 786436
  218.8 20.4 %all-to-all-start.6 = ((f32[32,16,256]{2,1,0:T(8,128)}), f32[32,16,256]{2,1,0:T(8,128)S(1)}, u32[]{:S(2)}, u32[]{:S(2)}) async-start(f32[32,16,256]{2,1,0:T(8,128)} %get-tuple-element.19), calls=%async_computation.6 | async-start | bytes 1048576 | tf_op jit(solution)/shard_map/all_to_all | solution.py:274
  224.1 15.2 %collective-permute-start.1 = (f32[16,256]{1,0:T(8,128)S(1)}, f32[16,256]{1,0:T(8,128)S(1)}, u32[]{:S(2)}, u32[]{:S(2)}) collective-permute-start(f32[16,256]{1,0:T(8,128)S(1)} %reduce_sum.27), channel_id=1, source_target_pairs={{0,0},{1,16},{2,32},{3,48},{4,64},{5,80},{6,96},{7,112},{8,128},{9... | collective-permute-start | bytes 49160 | tf_op jit(solution)/shard_map/ppermute | solution.py:273
  240.3 23.5 %all-to-all-start.7 = ((f32[32,16,128]{2,1,0:T(8,128)}), f32[32,16,128]{2,1,0:T(8,128)S(1)}, u32[]{:S(2)}, u32[]{:S(2)}) async-start(f32[32,16,128]{2,1,0:T(8,128)} %broadcast_in_dim.10), calls=%async_computation.7 | async-start | bytes 524288 | tf_op jit(solution)/shard_map/all_to_all | solution.py:243
  251.4 9.5 %collective-permute-start.2 = (f32[16,256]{1,0:T(8,128)S(1)}, f32[16,256]{1,0:T(8,128)S(1)}, u32[]{:S(2)}, u32[]{:S(2)}) collective-permute-start(f32[16,256]{1,0:T(8,128)S(1)} %add.14.three_ref), channel_id=1, source_target_pairs={{0,0},{16,1},{32,2},{48,3},{64,4},{80,5},{96,6},{112,7},{128,8},{1... | collective-permute-start | bytes 49160 | tf_op jit(solution)/shard_map/ppermute | solution.py:277

commit v12 on v11

--- a/solution.py
+++ b/solution.py
@@ -139,9 +139,14 @@
             out_ref[line(r, cols, 1 + half), :] = sums[:, half * LANE : (half + 1) * LANE]
 
 
-def gram(zero_ref, one_ref, two_ref, three_ref, gram_ref):
-    vecs = three_ref.shape[0]
-    basis = [zero_ref[...], one_ref[...], two_ref[...], three_ref[...]]
+def gram(zero_ref, one_ref, two_ref, direct_ref, parts_ref, three_ref, gram_ref):
+    vecs = direct_ref.shape[0]
+    three = parts_ref[0]
+    for r in range(1, parts_ref.shape[0]):
+        three = three + parts_ref[r]
+    three = three + direct_ref[...]
+    three_ref[...] = three
+    basis = [zero_ref[...], one_ref[...], two_ref[...], three]
     parts = []
     for j in range(ITERS + 1):
         others = jnp.concatenate(basis[j : j + 2], axis=0)
@@ -149,7 +154,9 @@
             lax.dot_general(basis[j], others, NT, precision=HIGH, preferred_element_type=jnp.float32)
         )
     parts.append(jnp.zeros((vecs, LANE - (2 * ITERS + 1) * vecs), jnp.float32))
-    gram_ref[...] = jnp.concatenate(parts, axis=1)
+    grams = jnp.concatenate(parts, axis=1)
+    for r in range(gram_ref.shape[0]):
+        gram_ref[r] = grams
 
 
 def finish(states, last_ref, turn_ref, start_ref, one_ref, two_ref, eigen_ref, ritz_ref):
@@ -271,11 +278,13 @@
     direct, mirror, rotation, *kept = lax.optimization_barrier((direct, mirror, rotation, *images))
     turned = jnp.pad(jnp.swapaxes(rotation, 2, 3), ((0, 0),) * 3 + ((0, LANE - vecs),))
     direct = lax.ppermute(direct, BOTH, corner)
-    last = jnp.sum(lax.all_to_all(mirror, "row", 0, 0), axis=0) + direct
+    parts = lax.all_to_all(mirror, "row", 0, 0)
     own = [own_block_piece(image) for image in kept]
-    grams = kernel_call(gram, "gram", f32(vecs, LANE), [VMEM] * 4)(piece, *own, last)
+    last, grams = kernel_call(gram, "gram", (f32(vecs, pair), f32(rows, vecs, LANE)), [VMEM] * 5)(
+        piece, *own, direct, parts
+    )
     last = lax.ppermute(last, BOTH, [(to, at) for at, to in corner])
-    grams = jnp.sum(to_all(grams, "row"), axis=0)
+    grams = jnp.sum(lax.all_to_all(grams, "row", 0, 0), axis=0)
     last, turned = lax.optimization_barrier((jnp.stack([last[:, :LANE], last[:, LANE:], grams]), turned))
     last = to_all(last, "col")
     return kernel_call(

time: 284 us -> 284 us (level)
  Pallas kernels: 10.3 us -> 14.1 us
  blocking collectives: 217 us -> 214 us
  transfers between devices with their start and end apart: 5 -> 5, of which waited for: 3 -> 4; matrix products, arithmetic and copies ran while one was open for 0% -> 0% of each run, Pallas kernels for 0% -> 1%
where the time goes in v12:
time: 284 us
  blocking collectives  214 us (75%)
  starting transfers between devices  34 us (12%)
  waiting for transfers between devices  15.3 us (5%)
  Pallas kernels  14.1 us (5%)
  local copies, waits for them, and re-layouts  3.89 us (1%)
    all_to_all x4, blocking collectives, swap(): moved = lax.all_to_all(x.reshape(rows * cols, 3 * LANE), BOTH, 0, 0)  150 us
    all_to_all x2, blocking collectives, to_all(): return lax.all_to_all(jnp.broadcast_to(x, (count,) + x.shape), axis, 0, 0)  53.4 us
    all_to_all x1, starting transfers between devices, body(): grams = jnp.sum(lax.all_to_all(grams, 'row', 0, 0), axis=0)  11.2 us
    all_to_all x1, blocking collectives, body(): direct = jnp.sum(lax.all_to_all(direct, 'col', 0, 0), axis=0)  11.1 us
    all_to_all x1, waiting for transfers between devices, body(): parts = lax.all_to_all(mirror, 'row', 0, 0)  7.71 us
    ppermute x1, starting transfers between devices, body(): last = lax.ppermute(last, BOTH, [(to, at) for at, to in corner])  7.16 us
    all_to_all x1, starting transfers between devices, body(): parts = lax.all_to_all(mirror, 'row', 0, 0)  5.71 us
  transfers between devices with their start and end apart: 5, of which 4 were waited for; matrix products, arithmetic and copies ran while one was open for 0% of the time, Pallas kernels for 1%

profile of v12, /device:TPU:1, one launch (start us, length us, event | category | flops | bytes accessed | tf_op | source)
XLA Modules:
  0.0 283.7 jit_solution(15250543794190283263)
XLA Ops:
  0.6 0.7 constant_dynamic-slice_fusion.2
  1.4 5.4 %collective-permute-start = (f32[16,256]{1,0:T(8,128)S(1)}, f32[16,256]{1,0:T(8,128)S(1)}, u32[]{:S(2)}, u32[]{:S(2)}) collective-permute-start(f32[16,256]{1,0:T(8,128)S(1)} %constant_dynamic-slice_fusion.2), channel_id=1, source_target_pairs={{0,0},{1,16},{2,32},{3,48},{4,64},{5,80},{6,96},{7,112},{8,128},{9... | collective-permute-start | bytes 49160 | tf_op jit(solution)/shard_map/ppermute | solution.py:253
  7.4 0.7 pad_add_fusion.index_ref
  8.1 0.0 copy-start
  8.1 1.9 copy-done
  10.0 0.0 copy-start.2
  10.0 0.9 copy-done.2
  11.0 1.5 first_mirror.1.mirrored_ref
  12.4 0.0 collective-permute-done.zero_ref
  12.5 0.1 broadcast_in_dim.6
  12.5 37.5 %all_to_all.61.block_ref = f32[32,16,256]{2,1,0:T(8,128)S(1)} all-to-all(f32[32,16,256]{2,1,0:T(8,128)S(1)} %broadcast_in_dim.6), channel_id=1, replica_groups=mesh['row'=32,'col'=16] {'row'}, dimensions={0} | all-to-all | bytes 1048576 | tf_op jit(solution)/shard_map/all_to_all | solution.py:250
  50.1 2.0 first_direct.1
  52.1 0.0 copy-start.1
  52.1 39.4 %all_to_all.62 = f32[512,1,384]{2,1,0:T(1,128)S(1)} all-to-all(f32[512,1,384]{2,1,0:T(1,128)S(1)} %bitcast.46), channel_id=1, replica_groups=mesh['row'=32,'col'=16] {'row','col'}, dimensions={0} | all-to-all | bytes 1572864 | tf_op jit(solution)/shard_map/all_to_all | solution.py:236
  91.5 0.1 sum_and_deal.2
  91.6 36.3 %all_to_all.63 = f32[512,1,384]{2,1,0:T(1,128)S(1)} all-to-all(f32[512,1,384]{2,1,0:T(1,128)S(1)} %bitcast.43), channel_id=1, replica_groups=mesh['row'=32,'col'=16] {'row','col'}, dimensions={0} | all-to-all | bytes 1572864 | tf_op jit(solution)/shard_map/all_to_all | solution.py:236
  127.9 0.0 copy-done.1
  127.9 2.7 multiply_next.1
  130.7 37.3 %all_to_all.64 = f32[512,1,384]{2,1,0:T(1,128)S(1)} all-to-all(f32[512,1,384]{2,1,0:T(1,128)S(1)} %bitcast.41), channel_id=1, replica_groups=mesh['row'=32,'col'=16] {'row','col'}, dimensions={0} | all-to-all | bytes 1572864 | tf_op jit(solution)/shard_map/all_to_all | solution.py:236
  168.0 0.1 sum_and_deal.3
  168.1 36.5 %all_to_all.65 = f32[512,1,384]{2,1,0:T(1,128)S(1)} all-to-all(f32[512,1,384]{2,1,0:T(1,128)S(1)} %bitcast.45), channel_id=1, replica_groups=mesh['row'=32,'col'=16] {'row','col'}, dimensions={0} | all-to-all | bytes 1572864 | tf_op jit(solution)/shard_map/all_to_all | solution.py:236
  204.6 0.0 copy-start.4
  204.6 3.5 %multiply_last.1 = (f32[16,16,256]{2,1,0:T(8,128)S(1)}, f32[32,16,256]{2,1,0:T(8,128)}) custom-call(s32[193]{0:T(256)S(1)} %pad_add_fusion.index_ref, bf16[96,128,128]{2,1,0:T(8,128)(2,1)S(1)} %bitcast.34, f32[1536,128]{1,0:T(8,128)S(1)} %bitcast.38), custom_call_target="tpu_custom_call" | custom-call | tf_op jit(solution)/shard_map/multiply_last/pallas_call | solution.py:273
  208.1 0.0 copy-start.3
  208.1 11.1 %all_to_all.66 = f32[16,16,256]{2,1,0:T(8,128)S(1)} all-to-all(f32[16,16,256]{2,1,0:T(8,128)S(1)} %get-tuple-element.20), channel_id=1, replica_groups=mesh['row'=32,'col'=16] {'col'}, dimensions={0} | all-to-all | bytes 524288 | tf_op jit(solution)/shard_map/all_to_all | solution.py:277
  219.2 5.7 %all-to-all-start.6 = ((f32[32,16,256]{2,1,0:T(8,128)}), f32[32,16,256]{2,1,0:T(8,128)S(1)}, u32[]{:S(2)}, u32[]{:S(2)}) async-start(f32[32,16,256]{2,1,0:T(8,128)} %get-tuple-element.26), calls=%async_computation.6 | async-start | bytes 1048576 | tf_op jit(solution)/shard_map/all_to_all | solution.py:281
  224.9 4.6 %collective-permute-start.1 = (f32[16,256]{1,0:T(8,128)S(1)}, f32[16,256]{1,0:T(8,128)S(1)}, u32[]{:S(2)}, u32[]{:S(2)}) collective-permute-start(f32[16,256]{1,0:T(8,128)S(1)} %reduce_sum.18), channel_id=1, source_target_pairs={{0,0},{1,16},{2,32},{3,48},{4,64},{5,80},{6,96},{7,112},{8,128},{9... | collective-permute-start | bytes 49160 | tf_op jit(solution)/shard_map/ppermute | solution.py:280
  229.7 2.6 collective-permute-done.1.direct_ref
  232.3 7.7 %all-to-all-done.6.parts_ref = f32[32,16,256]{2,1,0:T(8,128)S(1)} async-done(((f32[32,16,256]{2,1,0:T(8,128)}), f32[32,16,256]{2,1,0:T(8,128)S(1)}, u32[]{:S(2)}, u32[]{:S(2)}) %all-to-all-start.6) | async-done | bytes 524320 | tf_op jit(solution)/shard_map/all_to_all | solution.py:281
  240.0 1.0 gram.1
  241.1 11.2 %all-to-all-start.7 = ((f32[32,16,128]{2,1,0:T(8,128)}), f32[32,16,128]{2,1,0:T(8,128)S(1)}, u32[]{:S(2)}, u32[]{:S(2)}) async-start(f32[32,16,128]{2,1,0:T(8,128)} %get-tuple-element.28), calls=%async_computation.7 | async-start | bytes 524288 | tf_op jit(solution)/shard_map/all_to_all | solution.py:287
  252.3 7.2 %collective-permute-start.2 = (f32[16,256]{1,0:T(8,128)S(1)}, f32[16,256]{1,0:T(8,128)S(1)}, u32[]{:S(2)}, u32[]{:S(2)}) collective-permute-start(f32[16,256]{1,0:T(8,128)S(1)} %get-tuple-element.27), channel_id=1, source_target_pairs={{0,0},{16,1},{32,2},{48,3},{64,4},{80,5},{96,6},{112,7},{128,8},{1... | collective-permute-start | bytes 49160 | tf_op jit(solution)/shard_map/ppermute | solution.py:286
  259.5 0.0 copy-done.4
  259.5 0.1 copy.22
  259.6 2.2 collective-permute-done.2
  261.8 2.8 all-to-all-done.7
  264.7 15.8 %all_to_all.67.last_ref = f32[16,3,16,128]{3,2,1,0:T(8,128)S(1)} all-to-all(f32[16,3,16,128]{3,2,1,0:T(8,128)S(1)} %broadcast_in_dim.7), channel_id=1, replica_groups=mesh['row'=32,'col'=16] {'col'}, dimensions={0} | all-to-all | bytes 786432 | tf_op jit(solution)/shard_map/all_to_all | solution.py:250
  280.5 0.0 copy-done.3
  280.5 3.2 %finish.1 = (f32[16,4096]{1,0:T(8,128)}, f32[16,16]{1,0:T(8,128)}) custom-call(f32[16,3,16,128]{3,2,1,0:T(8,128)S(1)} %all_to_all.67.last_ref, f32[3,3,16,128]{3,2,1,0:T(8,128)S(1)} %pad.4.turn_ref, f32[16,4096]{1,0:T(8,128)S(1)} %copy-done.3, f32[1536,128]{1,0:T(8,128)S(1)} %bitcast.37, f32[1536,128]{1,0:T(8,128)S(1)} %bitcast.40), custom_call_target="tpu_custom_call" | custom-call | tf_op jit(solution)/shard_map/finish/pallas_call | solution.py:290
  (17 shorter events, 0.3 us)
Async XLA Ops:
  1.4 11.1 %collective-permute-start = (f32[16,256]{1,0:T(8,128)S(1)}, f32[16,256]{1,0:T(8,128)S(1)}, u32[]{:S(2)}, u32[]{:S(2)}) collective-permute-start(f32[16,256]{1,0:T(8,128)S(1)} %constant_dynamic-slice_fusion.2), channel_id=1, source_target_pairs={{0,0},{1,16},{2,32},{3,48},{4,64},{5,80},{6,96},{7,112},{8,128},{9... | collective-permute-start | bytes 49160 | tf_op jit(solution)/shard_map/ppermute | solution.py:253
  8.1 1.9 copy-start
  10.0 0.9 copy-start.2
  52.1 75.8 %copy-start.1 = (bf16[1,1,96,128,128]{4,3,2,1,0:T(8,128)(2,1)S(1)}, bf16[1,1,96,128,128]{4,3,2,1,0:T(8,128)(2,1)}, u32[]{:S(2)}) copy-start(bf16[1,1,96,128,128]{4,3,2,1,0:T(8,128)(2,1)} %param.6) | copy-start | bytes 9437188
  204.6 54.8 %copy-start.4 = (f32[3,3,16,16]{3,2,1,0:T(8,128)S(1)}, f32[3,3,16,16]{3,2,1,0:T(8,128)}, u32[]{:S(2)}) copy-start(f32[3,3,16,16]{3,2,1,0:T(8,128)} %param.11) | copy-start | bytes 27652
  208.1 72.4 %copy-start.3 = (f32[16,4096]{1,0:T(8,128)S(1)}, f32[16,4096]{1,0:T(8,128)}, u32[]{:S(2)}) copy-start(f32[16,4096]{1,0:T(8,128)} %start_ref.1) | copy-start | bytes 786436
  219.2 20.8 %all-to-all-start.6 = ((f32[32,16,256]{2,1,0:T(8,128)}), f32[32,16,256]{2,1,0:T(8,128)S(1)}, u32[]{:S(2)}, u32[]{:S(2)}) async-start(f32[32,16,256]{2,1,0:T(8,128)} %get-tuple-element.26), calls=%async_computation.6 | async-start | bytes 1048576 | tf_op jit(solution)/shard_map/all_to_all | solution.py:281
  224.9 7.4 %collective-permute-start.1 = (f32[16,256]{1,0:T(8,128)S(1)}, f32[16,256]{1,0:T(8,128)S(1)}, u32[]{:S(2)}, u32[]{:S(2)}) collective-permute-start(f32[16,256]{1,0:T(8,128)S(1)} %reduce_sum.18), channel_id=1, source_target_pairs={{0,0},{1,16},{2,32},{3,48},{4,64},{5,80},{6,96},{7,112},{8,128},{9... | collective-permute-start | bytes 49160 | tf_op jit(solution)/shard_map/ppermute | solution.py:280
  241.1 23.5 %all-to-all-start.7 = ((f32[32,16,128]{2,1,0:T(8,128)}), f32[32,16,128]{2,1,0:T(8,128)S(1)}, u32[]{:S(2)}, u32[]{:S(2)}) async-start(f32[32,16,128]{2,1,0:T(8,128)} %get-tuple-element.28), calls=%async_computation.7 | async-start | bytes 524288 | tf_op jit(solution)/shard_map/all_to_all | solution.py:287
  252.3 9.5 %collective-permute-start.2 = (f32[16,256]{1,0:T(8,128)S(1)}, f32[16,256]{1,0:T(8,128)S(1)}, u32[]{:S(2)}, u32[]{:S(2)}) collective-permute-start(f32[16,256]{1,0:T(8,128)S(1)} %get-tuple-element.27), channel_id=1, source_target_pairs={{0,0},{16,1},{32,2},{48,3},{64,4},{80,5},{96,6},{112,7},{128,8},{1... | collective-permute-start | bytes 49160 | tf_op jit(solution)/shard_map/ppermute | solution.py:286
